TPU v7x, 32 devices: a whole 2x2x4 slice. The times are simulated.
32 devices in a mesh: dp: 16 (over z, x, core), tensor: 2 (over y).
Axes of the slice: x: 2, y: 2, z: 4, core: 2. Of those that a mesh axis runs over, the one named last changes fastest.
Arguments:
- tokens_in: bfloat16 [16384, 1024], P(('dp', 'tensor')), may hold values from -6 to 6
- segments: int32 [16, 1024], P('dp'), may hold values from 0 to 7, never falling along the last dimension, each value on 1 to 256 neighbouring positions
- w_qkv: bfloat16 [2, 1024, 3, 1024], P(None, None, None, 'tensor'), may hold values from -0.1875 to 0.1875
- qv_bias: float32 [2, 2, 1024], P(None, None, 'tensor'), may hold values from -3 to 3
- w_out: bfloat16 [2, 1024, 1024], P(None, 'tensor'), may hold values from -1.5 to 1.5
- w_up: bfloat16 [2, 1024, 4096], P(None, None, 'tensor'), may hold values from -0.1875 to 0.1875
- up_bias: float32 [2, 4096], P(None, 'tensor'), may hold values from -3 to 3
- w_down: bfloat16 [2, 4096, 1024], P(None, 'tensor'), may hold values from -0.09375 to 0.09375
- out_bias: float32 [2, 2, 1024], replicated, may hold values from -2 to 2
- ln_gain: float32 [2, 2, 1024], replicated, may hold values from 0.5 to 1.5
- ln_bias: float32 [2, 2, 1024], replicated, may hold values from -2 to 2
- cotangent: bfloat16 [16384, 1024], P(('dp', 'tensor')), may hold values from -6 to 6
Outputs:
- out_act: bfloat16 [16384, 1024], P(('dp', 'tensor'))
- grad_in: bfloat16 [16384, 1024], P(('dp', 'tensor'))
- grad_qkv: float32 [2, 1024, 3, 1024], P(None, None, None, 'tensor')
- grad_qv_bias: float32 [2, 2, 1024], P(None, None, 'tensor')
- grad_out_w: float32 [2, 1024, 1024], P(None, 'tensor')
- grad_up: float32 [2, 1024, 4096], P(None, None, 'tensor')
- grad_up_bias: float32 [2, 4096], P(None, 'tensor')
- grad_down: float32 [2, 4096, 1024], P(None, 'tensor')
- grad_out_bias: float32 [2, 2, 1024], replicated
- grad_ln_gain: float32 [2, 2, 1024], replicated
- grad_ln_bias: float32 [2, 2, 1024], replicated
Inputs may be any that keep to these rules, and one draw needn't show every extreme that they name: `segments`: within each window the episode numbers never fall, start at 0, and take every value from 0 to 7, each on at most 256 positions.
All inputs are finite; a program needn't handle non-finite values.
Results may differ from a plain program's by a relative error of at most 0.025.
Values may be sent and summed in bfloat16 or wider, within the bound.
A program may use at most 320 MiB of HBM per device.

v0:
```python
import jax
import jax.numpy as jnp
from jax import lax
from jax.sharding import PartitionSpec as P

HEAD_DIM = 64


epsilon = 1e-05
gelu_coeff = 0.7978845608028654
cubic_coeff = 0.044715
masked_score = -1e30


def as_sent(shard):

    def short(part):
        return part.astype(jnp.bfloat16) if part.dtype == jnp.float32 else part

    return jax.tree.map(short, shard)


def layer_norm(values, gain, shift):
    average = jnp.mean(values, axis=-1, keepdims=True)
    centred = values - average
    inverse = lax.rsqrt(jnp.mean(centred * centred, axis=-1, keepdims=True) + epsilon)
    unit_rows = centred * inverse
    return (unit_rows * gain + shift, unit_rows, inverse)


def norm_backward(incoming, unit_rows, inverse, gain):
    scaled = incoming * gain
    first_mean = jnp.mean(scaled, axis=-1, keepdims=True)
    second_mean = jnp.mean(scaled * unit_rows, axis=-1, keepdims=True)
    through = inverse * (scaled - first_mean - unit_rows * second_mean)
    return (through, jnp.sum(incoming * unit_rows, axis=0), jnp.sum(incoming, axis=0))


def gelu_tanh(before):
    tanh_input = gelu_coeff * (before + cubic_coeff * before * before * before)
    return 0.5 * before * (1.0 + jnp.tanh(tanh_input))


def gelu_slope(before):
    tanh_input = gelu_coeff * (before + cubic_coeff * before * before * before)
    tangent = jnp.tanh(tanh_input)
    return 0.5 * (1.0 + tangent) + 0.5 * before * (1.0 - tangent * tangent) * gelu_coeff * (
        1.0 + 3.0 * cubic_coeff * before * before
    )


def masked_scores(query_block, key_seq, segment_row, offset, block_rows):
    window = key_seq.shape[0]
    scores = jnp.einsum(
        "qhe,khe->hqk", query_block, key_seq, preferred_element_type=jnp.float32
    ) * HEAD_DIM ** (-0.5)
    query_place = offset + lax.iota(jnp.int32, block_rows)
    key_place = lax.iota(jnp.int32, window)
    query_segment = segment_row[offset : offset + block_rows]
    allowed = (query_place[:, None] >= key_place[None, :]) & (
        query_segment[:, None] == segment_row[None, :]
    )
    return jnp.where(allowed[None], scores, masked_score)


def split_heads(flat_rows, seq_count):
    return flat_rows.reshape(
        seq_count, flat_rows.shape[0] // seq_count, flat_rows.shape[1] // HEAD_DIM, HEAD_DIM
    )


def attend_forward(query_rows, key_rows, value_rows, segments):
    seq_count, window = segments.shape
    block_rows = min(512, window)

    def one_sequence(member):
        query_seq, key_seq, value_seq, segment_row = member
        outputs = []
        totals = []
        for block_index in range(window // block_rows):
            offset = block_index * block_rows
            scores = masked_scores(
                query_seq[offset : offset + block_rows], key_seq, segment_row, offset, block_rows
            )
            highest = jnp.max(scores, axis=-1, keepdims=True)
            raised = jnp.exp(scores - highest)
            summed = jnp.sum(raised, axis=-1, keepdims=True)
            softmax_low = (raised / summed).astype(jnp.bfloat16)
            block_out = jnp.einsum(
                "hqk,khe->qhe", softmax_low, value_seq, preferred_element_type=jnp.float32
            )
            outputs.append(block_out.astype(jnp.bfloat16))
            totals.append(highest[..., 0] + jnp.log(summed[..., 0]))
        return (jnp.concatenate(outputs, axis=0), jnp.stack(totals, axis=0))

    attended, log_totals = lax.map(
        one_sequence,
        (
            split_heads(query_rows, seq_count),
            split_heads(key_rows, seq_count),
            split_heads(value_rows, seq_count),
            segments,
        ),
    )
    return (attended.reshape(query_rows.shape), log_totals)


def attend_backward(query_rows, key_rows, value_rows, segments, log_totals, grad_attended):
    seq_count, window = segments.shape
    block_rows = min(512, window)
    scaling = HEAD_DIM ** (-0.5)

    def one_sequence(member):
        query_seq, key_seq, value_seq, segment_row, totals_seq, grad_seq = member
        query_parts = []
        grad_keys = jnp.zeros(key_seq.shape, jnp.float32)
        grad_values = jnp.zeros(value_seq.shape, jnp.float32)
        for block_index in range(window // block_rows):
            offset = block_index * block_rows
            query_block = query_seq[offset : offset + block_rows]
            grad_block = grad_seq[offset : offset + block_rows]
            scores = masked_scores(query_block, key_seq, segment_row, offset, block_rows)
            softmax_exact = jnp.exp(scores - totals_seq[block_index][..., None])
            softmax_low = softmax_exact.astype(jnp.bfloat16)
            grad_softmax = jnp.einsum(
                "qhe,khe->hqk", grad_block, value_seq, preferred_element_type=jnp.float32
            )
            row_terms = jnp.sum(softmax_exact * grad_softmax, axis=-1, keepdims=True)
            grad_scores = (softmax_exact * (grad_softmax - row_terms)).astype(jnp.bfloat16)
            query_parts.append(
                jnp.einsum("hqk,khe->qhe", grad_scores, key_seq, preferred_element_type=jnp.float32)
                * scaling
            )
            grad_keys = (
                grad_keys
                + jnp.einsum(
                    "hqk,qhe->khe", grad_scores, query_block, preferred_element_type=jnp.float32
                )
                * scaling
            )
            grad_values = grad_values + jnp.einsum(
                "hqk,qhe->khe", softmax_low, grad_block, preferred_element_type=jnp.float32
            )
        grad_query = jnp.concatenate(query_parts, axis=0)
        return (
            grad_query.astype(jnp.bfloat16),
            grad_keys.astype(jnp.bfloat16),
            grad_values.astype(jnp.bfloat16),
        )

    grad_query, grad_keys, grad_values = lax.map(
        one_sequence,
        (
            split_heads(query_rows, seq_count),
            split_heads(key_rows, seq_count),
            split_heads(value_rows, seq_count),
            segments,
            log_totals,
            split_heads(grad_attended, seq_count),
        ),
    )
    return (
        grad_query.reshape(query_rows.shape),
        grad_keys.reshape(query_rows.shape),
        grad_values.reshape(query_rows.shape),
    )


def layer_forward(residual, segments, weights):
    w_qkv, qv_bias, w_out, w_up, up_bias, w_down, out_bias, gains, shifts = weights
    row_count = residual.shape[0]
    normed, unit_one, inverse_one = layer_norm(residual, gains[0], shifts[0])
    normed_all = lax.all_gather(normed.astype(jnp.bfloat16), "tensor", axis=0, tiled=True)
    projected = jnp.einsum("td,dsc->tsc", normed_all, w_qkv, preferred_element_type=jnp.float32)
    query_rows = (projected[:, 0] + qv_bias[0]).astype(jnp.bfloat16)
    key_rows = projected[:, 1].astype(jnp.bfloat16)
    value_rows = (projected[:, 2] + qv_bias[1]).astype(jnp.bfloat16)
    attended, log_totals = attend_forward(query_rows, key_rows, value_rows, segments)
    middle = (
        residual
        + lax.psum_scatter(
            jnp.dot(
                lax.slice_in_dim(attended, 0, row_count * lax.axis_size("tensor"), axis=0),
                w_out,
                preferred_element_type=jnp.float32,
            ).astype(jnp.bfloat16),
            "tensor",
            scatter_dimension=0,
            tiled=True,
        ).astype(jnp.float32)
        + out_bias[0]
    )
    normed_two, unit_two, inverse_two = layer_norm(middle, gains[1], shifts[1])
    normed_low = normed_two.astype(jnp.bfloat16)
    ffn_rows = lax.all_gather(normed_low, "tensor", axis=0, tiled=True)
    before = jnp.dot(ffn_rows, w_up, preferred_element_type=jnp.float32) + up_bias
    activated = gelu_tanh(before).astype(jnp.bfloat16)
    ffn_branch = lax.psum_scatter(
        jnp.dot(
            lax.slice_in_dim(activated, 0, row_count * lax.axis_size("tensor"), axis=0),
            w_down,
            preferred_element_type=jnp.float32,
        ).astype(jnp.bfloat16),
        "tensor",
        scatter_dimension=0,
        tiled=True,
    ).astype(jnp.float32)
    kept_ffn = (w_up, w_down)
    result = middle + ffn_branch + out_bias[1]
    kept_state = (
        unit_one,
        inverse_one,
        normed_all,
        query_rows,
        key_rows,
        value_rows,
        attended,
        log_totals,
        unit_two,
        inverse_two,
        ffn_rows,
        before,
        activated,
        kept_ffn,
    )
    return (result, kept_state)


def layer_backward(grad_residual, segments, weights, kept_state):
    w_qkv, qv_bias, w_out, w_up, up_bias, w_down, out_bias, gains, shifts = weights
    (
        unit_one,
        inverse_one,
        normed_all,
        query_rows,
        key_rows,
        value_rows,
        attended,
        log_totals,
        unit_two,
        inverse_two,
        ffn_rows,
        before,
        activated,
        kept_ffn,
    ) = kept_state
    up_used, down_used = kept_ffn
    row_count = grad_residual.shape[0]
    grad_branch = grad_residual.astype(jnp.bfloat16)
    bias_down = jnp.sum(grad_branch, axis=0, dtype=jnp.float32)
    grad_rows = lax.all_gather(grad_branch, "tensor", axis=0, tiled=True)
    grad_hidden = jnp.einsum("td,fd->tf", grad_rows, down_used, preferred_element_type=jnp.float32)
    grad_before = (grad_hidden * gelu_slope(before)).astype(jnp.bfloat16)
    grad_down = jnp.einsum("tf,td->fd", activated, grad_rows, preferred_element_type=jnp.float32)
    grad_up = jnp.einsum("td,tf->df", ffn_rows, grad_before, preferred_element_type=jnp.float32)
    grad_up_bias = jnp.sum(grad_before, axis=0, dtype=jnp.float32)
    piece_rows = lax.slice_in_dim(grad_before, 0, row_count * lax.axis_size("tensor"), axis=0)
    grad_normed_two = lax.psum_scatter(
        jnp.einsum("tf,df->td", piece_rows, w_up, preferred_element_type=jnp.float32).astype(
            jnp.bfloat16
        ),
        "tensor",
        scatter_dimension=0,
        tiled=True,
    ).astype(jnp.float32)
    through_two, gain_two, shift_two = norm_backward(
        grad_normed_two, unit_two, inverse_two, gains[1]
    )
    grad_middle = grad_residual + through_two
    grad_attn_branch = grad_middle.astype(jnp.bfloat16)
    bias_attn = jnp.sum(grad_attn_branch, axis=0, dtype=jnp.float32)
    grad_attn_all = lax.all_gather(grad_attn_branch, "tensor", axis=0, tiled=True)
    grad_out_w = jnp.einsum(
        "tc,td->cd", attended, grad_attn_all, preferred_element_type=jnp.float32
    )
    grad_attended = jnp.einsum(
        "td,cd->tc", grad_attn_all, w_out, preferred_element_type=jnp.float32
    ).astype(jnp.bfloat16)
    grad_query, grad_keys, grad_values = attend_backward(
        query_rows, key_rows, value_rows, segments, log_totals, grad_attended
    )
    grad_projected = jnp.stack((grad_query, grad_keys, grad_values), axis=1)
    grad_qkv = jnp.einsum(
        "td,tsc->dsc", normed_all, grad_projected, preferred_element_type=jnp.float32
    )
    grad_qv_bias = jnp.stack(
        (
            jnp.sum(grad_query, axis=0, dtype=jnp.float32),
            jnp.sum(grad_values, axis=0, dtype=jnp.float32),
        )
    )
    piece_rows = lax.slice_in_dim(grad_projected, 0, row_count * lax.axis_size("tensor"), axis=0)
    grad_normed = lax.psum_scatter(
        jnp.einsum("tsc,dsc->td", piece_rows, w_qkv, preferred_element_type=jnp.float32).astype(
            jnp.bfloat16
        ),
        "tensor",
        scatter_dimension=0,
        tiled=True,
    ).astype(jnp.float32)
    through_one, gain_one, shift_one = norm_backward(grad_normed, unit_one, inverse_one, gains[0])
    grad_input = grad_middle + through_one
    spread = (grad_qkv, grad_qv_bias, grad_out_w, grad_up, grad_up_bias, grad_down)
    shared = (
        jnp.stack((bias_attn, bias_down)),
        jnp.stack((gain_one, gain_two)),
        jnp.stack((shift_one, shift_two)),
    )
    return (grad_input, spread, shared)


def local(
    tokens_in,
    segments,
    w_qkv,
    qv_bias,
    w_out,
    w_up,
    up_bias,
    w_down,
    out_bias,
    ln_gain,
    ln_bias,
    cotangent,
):
    layers_total = w_qkv.shape[0]
    all_params = (w_qkv, qv_bias, w_out, w_up, up_bias, w_down, out_bias, ln_gain, ln_bias)
    residual = tokens_in.astype(jnp.float32)
    kept_layers = []
    for layer_index in range(layers_total):
        weights = tuple((member_array[layer_index] for member_array in all_params))
        residual, kept_state = layer_forward(residual, segments, weights)
        kept_layers.append(kept_state)
    out_act = residual.astype(jnp.bfloat16)
    grad_residual = cotangent.astype(jnp.float32)
    spread_layers = []
    shared_layers = []
    for layer_index in reversed(range(layers_total)):
        weights = tuple((member_array[layer_index] for member_array in all_params))
        grad_residual, spread, shared = layer_backward(
            grad_residual, segments, weights, kept_layers[layer_index]
        )
        spread_layers.insert(0, spread)
        shared_layers.insert(0, shared)
    spread_stack = tuple(
        (
            jnp.stack([spread_layers[layer_index][position] for layer_index in range(layers_total)])
            for position in range(6)
        )
    )
    spread_stack = jax.tree.map(
        lambda part: part.astype(jnp.float32), lax.psum(as_sent(spread_stack), "dp")
    )
    shared_stack = tuple(
        (
            jnp.stack([shared_layers[layer_index][position] for layer_index in range(layers_total)])
            for position in range(3)
        )
    )
    shared_stack = lax.psum(shared_stack, ("dp", "tensor"))
    grad_in = grad_residual.astype(jnp.bfloat16)
    return (out_act, grad_in) + tuple(spread_stack) + tuple(shared_stack)


def solution(mesh):
    return jax.shard_map(
        local,
        mesh=mesh,
        in_specs=(
            P(("dp", "tensor"), None),
            P("dp", None),
            P(None, None, None, "tensor"),
            P(None, None, "tensor"),
            P(None, "tensor", None),
            P(None, None, "tensor"),
            P(None, "tensor"),
            P(None, "tensor", None),
            P(),
            P(),
            P(),
            P(("dp", "tensor"), None),
        ),
        out_specs=(
            P(("dp", "tensor"), None),
            P(("dp", "tensor"), None),
            P(None, None, None, "tensor"),
            P(None, None, "tensor"),
            P(None, "tensor", None),
            P(None, None, "tensor"),
            P(None, "tensor"),
            P(None, "tensor", None),
            P(),
            P(),
            P(),
        ),
        check_vma=False,
    )
```

profile of v0, /device:TPU:0, one launch (start us, length us, event | category | flops | bytes accessed | tf_op | source)
XLA Modules:
  0.0 1430.2 jit_solution(17608047593955225409)
XLA Ops:
  17.1 34.7 %all-gather.9.cloned.1.call-done = bf16[1024,1024]{1,0:T(8,128)(2,1)} async-done(((bf16[512,1024]{1,0:T(8,128)(2,1)}), bf16[1024,1024]{1,0:T(8,128)(2,1)}) %all-gather.9.cloned.1.call-update) | async-done | bytes 2097168 | tf_op jit(solution)/shard_map/all_gather | solution.py:173
  89.3 31.9 %reduce-scatter.9.cloned.1.call-done = bf16[512,1024]{1,0:T(8,128)(2,1)} async-done(((bf16[1024,1024]{1,0:T(8,128)(2,1)}), bf16[512,1024]{1,0:T(8,128)(2,1)}) %reduce-scatter.9.cloned.1.call-update) | async-done | bytes 1048592 | tf_op jit(solution)/shard_map/reduce_scatter | solution.py:181
  126.4 33.2 %all-gather.11.cloned.1.call-done = bf16[1024,1024]{1,0:T(8,128)(2,1)} async-done(((bf16[512,1024]{1,0:T(8,128)(2,1)}), bf16[1024,1024]{1,0:T(8,128)(2,1)}) %all-gather.11.cloned.1.call-update) | async-done | bytes 2097168 | tf_op jit(solution)/shard_map/all_gather | solution.py:195
  179.1 31.5 %reduce-scatter.11.cloned.1.call-done = bf16[512,1024]{1,0:T(8,128)(2,1)} async-done(((bf16[1024,1024]{1,0:T(8,128)(2,1)}), bf16[512,1024]{1,0:T(8,128)(2,1)}) %reduce-scatter.11.cloned.1.call-update) | async-done | bytes 1048592 | tf_op jit(solution)/shard_map/reduce_scatter | solution.py:198
  215.3 33.2 %all-gather.13.cloned.1.call-done = bf16[1024,1024]{1,0:T(8,128)(2,1)} async-done(((bf16[512,1024]{1,0:T(8,128)(2,1)}), bf16[1024,1024]{1,0:T(8,128)(2,1)}) %all-gather.13.cloned.1.call-update) | async-done | bytes 2097168 | tf_op jit(solution)/shard_map/all_gather | solution.py:173
  295.1 31.9 %reduce-scatter.13.cloned.1.call-done = bf16[512,1024]{1,0:T(8,128)(2,1)} async-done(((bf16[1024,1024]{1,0:T(8,128)(2,1)}), bf16[512,1024]{1,0:T(8,128)(2,1)}) %reduce-scatter.13.cloned.1.call-update) | async-done | bytes 1048592 | tf_op jit(solution)/shard_map/reduce_scatter | solution.py:181
  332.3 32.5 %all-gather.15.cloned.1.call-done = bf16[1024,1024]{1,0:T(8,128)(2,1)} async-done(((bf16[512,1024]{1,0:T(8,128)(2,1)}), bf16[1024,1024]{1,0:T(8,128)(2,1)}) %all-gather.15.cloned.1.call-update) | async-done | bytes 2097168 | tf_op jit(solution)/shard_map/all_gather | solution.py:195
  364.7 10.9 fusion.43
  375.6 23.9 %all-gather.17.cloned.1.call-done = bf16[1024,1024]{1,0:T(8,128)(2,1)} async-done(((bf16[512,1024]{1,0:T(8,128)(2,1)}), bf16[1024,1024]{1,0:T(8,128)(2,1)}) %all-gather.17.cloned.1.call-update) | async-done | bytes 2097168 | tf_op jit(solution)/shard_map/all_gather | solution.py:251
  399.5 13.6 fusion.187
  423.3 11.3 fusion.135
  434.7 20.6 %reduce-scatter.17.cloned.1.call-done = bf16[512,1024]{1,0:T(8,128)(2,1)} async-done(((bf16[1024,1024]{1,0:T(8,128)(2,1)}), bf16[512,1024]{1,0:T(8,128)(2,1)}) %reduce-scatter.17.cloned.1.call-update) | async-done | bytes 1048592 | tf_op jit(solution)/shard_map/reduce_scatter | solution.py:258
  458.7 30.5 %reduce-scatter.15.cloned.1.call-done = bf16[512,1024]{1,0:T(8,128)(2,1)} async-done(((bf16[1024,1024]{1,0:T(8,128)(2,1)}), bf16[512,1024]{1,0:T(8,128)(2,1)}) %reduce-scatter.15.cloned.1.call-update) | async-done | bytes 1048592 | tf_op jit(solution)/shard_map/reduce_scatter | solution.py:198
  494.4 33.2 %all-gather.19.cloned.1.call-done = bf16[1024,1024]{1,0:T(8,128)(2,1)} async-done(((bf16[512,1024]{1,0:T(8,128)(2,1)}), bf16[1024,1024]{1,0:T(8,128)(2,1)}) %all-gather.19.cloned.1.call-update) | async-done | bytes 2097168 | tf_op jit(solution)/shard_map/all_gather | solution.py:272
  531.6 11.2 multiply_reduce_fusion.3
  542.8 15.7 %multiply_convert_fusion.3 = bf16[8,512,1024]{2,1,0:T(8,128)(2,1)} fusion(f32[8,512,1024]{2,1,0:T(8,128)} %get-tuple-element.194, f32[8,512,1024]{2,1,0:T(8,128)} %get-tuple-element.192, f32[8,512]{1,0:T(8,128)S(1)} %get-tuple-element.193, f32[8,512]{1,0:T(8,128)S(1)} %log_add_fusion.3), kind=kLoop, calls=%fused_computation.9 | loop fusion | flops 16777216 | bytes 41975808 | tf_op jit(solution)/shard_map/while/body/eval_jaxpr/convert_element_type | solution.py:129
  600.0 12.1 multiply_convert_fusion.2
  628.8 31.9 %reduce-scatter.19.cloned.1.call-done = bf16[512,1024]{1,0:T(8,128)(2,1)} async-done(((bf16[1024,1024]{1,0:T(8,128)(2,1)}), bf16[512,1024]{1,0:T(8,128)(2,1)}) %reduce-scatter.19.cloned.1.call-update) | async-done | bytes 1048592 | tf_op jit(solution)/shard_map/reduce_scatter | solution.py:293
  668.0 33.2 %all-gather.21.cloned.1.call-done = bf16[1024,1024]{1,0:T(8,128)(2,1)} async-done(((bf16[512,1024]{1,0:T(8,128)(2,1)}), bf16[1024,1024]{1,0:T(8,128)(2,1)}) %all-gather.21.cloned.1.call-update) | async-done | bytes 2097168 | tf_op jit(solution)/shard_map/all_gather | solution.py:251
  701.2 13.4 fusion.188
  726.2 12.6 convert_bitcast_fusion
  738.7 18.2 %reduce-scatter.21.cloned.1.call-done = bf16[512,1024]{1,0:T(8,128)(2,1)} async-done(((bf16[1024,1024]{1,0:T(8,128)(2,1)}), bf16[512,1024]{1,0:T(8,128)(2,1)}) %reduce-scatter.21.cloned.1.call-update) | async-done | bytes 1048592 | tf_op jit(solution)/shard_map/reduce_scatter | solution.py:258
  782.1 15.4 %all-gather.23.cloned.1.call-done = bf16[1024,1024]{1,0:T(8,128)(2,1)} async-done(((bf16[512,1024]{1,0:T(8,128)(2,1)}), bf16[1024,1024]{1,0:T(8,128)(2,1)}) %all-gather.23.cloned.1.call-update) | async-done | bytes 2097168 | tf_op jit(solution)/shard_map/all_gather | solution.py:272
  801.4 11.5 multiply_reduce_fusion.1
  812.9 15.7 %multiply_convert_fusion.1 = bf16[8,512,1024]{2,1,0:T(8,128)(2,1)} fusion(f32[8,512,1024]{2,1,0:T(8,128)} %get-tuple-element.198, f32[8,512,1024]{2,1,0:T(8,128)} %copy-done.1, f32[8,512]{1,0:T(8,128)S(1)} %get-tuple-element.197, f32[8,512]{1,0:T(8,128)S(1)} %log_add_fusion.1), kind=kLoop, calls=%fused_computation.3 | loop fusion | flops 16777216 | bytes 41975808 | tf_op jit(solution)/shard_map/while/body/eval_jaxpr/convert_element_type | solution.py:129
  869.7 11.8 multiply_convert_fusion
  896.2 12.4 convert_bitcast_fusion.1
  945.8 64.6 %all-reduce.1 = (bf16[2,2,512]{2,1,0:T(2,128)(2,1)S(1)}, bf16[2,2048]{1,0:T(2,128)(2,1)S(1)}) all-reduce(bf16[2,2,512]{2,1,0:T(2,128)(2,1)S(1)} %pad_maximum_fusion.16, bf16[2,2048]{1,0:T(2,128)(2,1)S(1)} %pad_maximum_fusion.15), channel_id=1, replica_groups=mesh['dp'=16,'tensor'=2] {'dp'}, use_global_device_ids=true, to_apply=%region_41.42 | all-reduce | flops 6144 | bytes 24576 | tf_op jit(solution)/shard_map/psum | solution.py:352
  1014.1 39.7 %all-reduce = (f32[2,2,1024]{2,1,0:T(2,128)}, f32[2,2,1024]{2,1,0:T(2,128)}, f32[2,2,1024]{2,1,0:T(2,128)}) all-reduce(f32[2,2,1024]{2,1,0:T(2,128)S(1)} %pad_maximum_fusion.12, f32[2,2,1024]{2,1,0:T(2,128)S(1)} %pad_maximum_fusion.13, f32[2,2,1024]{2,1,0:T(2,128)S(1)} %pad_maximum_fusion.14), channel_id=1, replica_groups=mesh['dp'=16,'tensor'=2] {'dp','tensor'}, use_global_device_ids=true, to_apply=%region_52.53 | all-reduce | flops 12288 | bytes 98304 | tf_op jit(solution)/shard_map/psum | solution.py:360
  1057.4 331.9 %all-reduce.5.cloned.1.call-done = (bf16[2,1024,3,512]{3,1,2,0:T(8,128)(2,1)}, bf16[2,512,1024]{2,1,0:T(8,128)(2,1)}, bf16[2,1024,2048]{2,1,0:T(8,128)(2,1)}, bf16[2,2048,1024]{2,1,0:T(8,128)(2,1)}) async-done(((bf16[2,1024,3,512]{3,1,2,0:T(8,128)(2,1)}, bf16[2,512,1024]{2,1,0:T(8,128)(2,1)}, bf16[2,1024,2048]{2,1,0:T(8,128)(2,1)}, bf16[2,2048,1024]{2,1,0:T(8,128)(2,1)}), ...) | async-done | bytes 25165840 | tf_op jit(solution)/shard_map/psum | solution.py:352
  1400.0 11.7 convert_element_type.376
  1411.7 11.7 convert_element_type.380
  (426 shorter events, 366.9 us)
Async XLA Ops:
  7.2 44.6 %all-gather.9.cloned.1.call-start = ((), (), s32[]{:S(2)}) async-start(), calls=%async_computation.8 | async-start | bytes 3145728 | tf_op jit(solution)/shard_map/all_gather | solution.py:173
  8.7 49.2 %copy-start.71 = (f32[512]{0:T(512)}, f32[512]{0:T(512)S(1)}, u32[]{:S(2)}) copy-start(f32[512]{0:T(512)S(1)} %broadcast_multiply_fusion.11) | copy-start | bytes 6148
  10.3 47.6 %copy-start.77 = (f32[512]{0:T(512)}, f32[512]{0:T(512)S(1)}, u32[]{:S(2)}) copy-start(f32[512]{0:T(512)S(1)} %add_rsqrt_fusion.3) | copy-start | bytes 6148
  11.7 46.2 %copy-start.65 = (f32[1,1,1024]{2,1,0:T(1,128)}, f32[1,1,1024]{2,1,0:T(1,128)S(1)}, u32[]{:S(2)}) copy-start(f32[1,1,1024]{2,1,0:T(1,128)S(1)} %get-tuple-element.171) | copy-start | bytes 12292
  11.7 113.0 %copy-start.60 = (f32[1,1,1024]{2,1,0:T(1,128)}, f32[1,1,1024]{2,1,0:T(1,128)S(1)}, u32[]{:S(2)}) copy-start(f32[1,1,1024]{2,1,0:T(1,128)S(1)} %get-tuple-element.170) | copy-start | bytes 12292
  11.7 201.4 %copy-start.62 = (f32[1,1,1024]{2,1,0:T(1,128)}, f32[1,1,1024]{2,1,0:T(1,128)S(1)}, u32[]{:S(2)}) copy-start(f32[1,1,1024]{2,1,0:T(1,128)S(1)} %get-tuple-element.172) | copy-start | bytes 12292
  15.8 105.4 %reduce-scatter.9.cloned.1.call-start = ((), (), s32[]{:S(2)}) async-start(), calls=%async_computation.9 | async-start | bytes 3145728 | tf_op jit(solution)/shard_map/reduce_scatter | solution.py:181
  17.1 41.7 %copy-start.35 = (pred[512,1024]{1,0:T(8,128)(4,1)}, pred[512,1024]{1,0:T(8,128)(4,1)S(1)}, u32[]{:S(2)}) copy-start(pred[512,1024]{1,0:T(8,128)(4,1)S(1)} %get-tuple-element.182) | copy-start | bytes 1572868
  17.1 55.1 %copy-start.33 = (pred[512,1024]{1,0:T(8,128)(4,1)}, pred[512,1024]{1,0:T(8,128)(4,1)S(1)}, u32[]{:S(2)}) copy-start(pred[512,1024]{1,0:T(8,128)(4,1)S(1)} %get-tuple-element.181) | copy-start | bytes 1572868
  89.2 70.4 %all-gather.11.cloned.1.call-start = ((), (), s32[]{:S(2)}) async-start(), calls=%async_computation.10 | async-start | bytes 3145728 | tf_op jit(solution)/shard_map/all_gather | solution.py:195
  89.3 121.4 %copy-start.53 = (f32[1,1,1024]{2,1,0:T(1,128)}, f32[1,1,1024]{2,1,0:T(1,128)S(1)}, u32[]{:S(2)}) copy-start(f32[1,1,1024]{2,1,0:T(1,128)S(1)} %get-tuple-element.165) | copy-start | bytes 12292
  122.9 43.6 %copy-start.73 = (f32[512]{0:T(512)}, f32[512]{0:T(512)S(1)}, u32[]{:S(2)}) copy-start(f32[512]{0:T(512)S(1)} %broadcast_multiply_fusion.10) | copy-start | bytes 6148
  124.7 41.8 %copy-start.79 = (f32[512]{0:T(512)}, f32[512]{0:T(512)S(1)}, u32[]{:S(2)}) copy-start(f32[512]{0:T(512)S(1)} %add_rsqrt_fusion.2) | copy-start | bytes 6148
  126.3 84.3 %reduce-scatter.11.cloned.1.call-start = ((), (), s32[]{:S(2)}) async-start(), calls=%async_computation.11 | async-start | bytes 3145728 | tf_op jit(solution)/shard_map/reduce_scatter | solution.py:198
  178.6 69.8 %all-gather.13.cloned.1.call-start = ((), (), s32[]{:S(2)}) async-start(), calls=%async_computation.12 | async-start | bytes 3145728 | tf_op jit(solution)/shard_map/all_gather | solution.py:173
  212.8 41.7 %copy-start.75 = (f32[512]{0:T(512)}, f32[512]{0:T(512)S(1)}, u32[]{:S(2)}) copy-start(f32[512]{0:T(512)S(1)} %broadcast_multiply_fusion.9) | copy-start | bytes 6148
  215.1 111.9 %reduce-scatter.13.cloned.1.call-start = ((), (), s32[]{:S(2)}) async-start(), calls=%async_computation.13 | async-start | bytes 3145728 | tf_op jit(solution)/shard_map/reduce_scatter | solution.py:181
  268.6 263.0 %copy-start.17 = (bf16[1024,8,64]{0,2,1:T(8,128)(2,1)}, bf16[1024,8,64]{0,2,1:T(8,128)(2,1)S(1)}, u32[]{:S(2)}) copy-start(bf16[1024,8,64]{0,2,1:T(8,128)(2,1)S(1)} %add_convert_fusion.4) | copy-start | bytes 3145732
  295.1 69.6 %all-gather.15.cloned.1.call-start = ((), (), s32[]{:S(2)}) async-start(), calls=%async_computation.14 | async-start | bytes 3145728 | tf_op jit(solution)/shard_map/all_gather | solution.py:195
  331.5 68.0 %all-gather.17.cloned.1.call-start = ((), (), s32[]{:S(2)}) async-start(), calls=%async_computation.16 | async-start | bytes 3145728 | tf_op jit(solution)/shard_map/all_gather | solution.py:251
  332.2 123.1 %reduce-scatter.17.cloned.1.call-start = ((), (), s32[]{:S(2)}) async-start(), calls=%async_computation.17 | async-start | bytes 3145728 | tf_op jit(solution)/shard_map/reduce_scatter | solution.py:258
  423.3 65.9 %reduce-scatter.15.cloned.1.call-start = ((), (), s32[]{:S(2)}) async-start(), calls=%async_computation.15 | async-start | bytes 3145728 | tf_op jit(solution)/shard_map/reduce_scatter | solution.py:198
  434.6 92.9 %all-gather.19.cloned.1.call-start = ((), (), s32[]{:S(2)}) async-start(), calls=%async_computation.18 | async-start | bytes 3145728 | tf_op jit(solution)/shard_map/all_gather | solution.py:272
  494.3 166.4 %reduce-scatter.19.cloned.1.call-start = ((), (), s32[]{:S(2)}) async-start(), calls=%async_computation.19 | async-start | bytes 3145728 | tf_op jit(solution)/shard_map/reduce_scatter | solution.py:293
  628.7 72.5 %all-gather.21.cloned.1.call-start = ((), (), s32[]{:S(2)}) async-start(), calls=%async_computation.20 | async-start | bytes 3145728 | tf_op jit(solution)/shard_map/all_gather | solution.py:251
  667.9 89.0 %reduce-scatter.21.cloned.1.call-start = ((), (), s32[]{:S(2)}) async-start(), calls=%async_computation.21 | async-start | bytes 3145728 | tf_op jit(solution)/shard_map/reduce_scatter | solution.py:258
  724.9 72.5 %all-gather.23.cloned.1.call-start = ((), (), s32[]{:S(2)}) async-start(), calls=%async_computation.22 | async-start | bytes 3145728 | tf_op jit(solution)/shard_map/all_gather | solution.py:272
  764.2 247.5 %reduce-scatter.23.cloned.1.call-start = ((), (), s32[]{:S(2)}) async-start(), calls=%async_computation.23 | async-start | bytes 3145728 | tf_op jit(solution)/shard_map/reduce_scatter | solution.py:293
  895.7 493.6 %all-reduce.5.cloned.1.call-start = ((), (), s32[]{:S(2)}) async-start(), calls=%async_computation.24 | async-start | bytes 50331648 | tf_op jit(solution)/shard_map/psum | solution.py:352
  944.6 67.1 %copy-start.66 = (f32[1,1,1024]{2,1,0:T(1,128)S(1)}, f32[1,1,1024]{2,1,0:T(1,128)}, u32[]{:S(2)}) copy-start(f32[1,1,1024]{2,1,0:T(1,128)} %copy-done.65) | copy-start | bytes 12292
  944.6 67.1 %copy-start.72 = (f32[512]{0:T(512)S(1)}, f32[512]{0:T(512)}, u32[]{:S(2)}) copy-start(f32[512]{0:T(512)} %copy-done.71) | copy-start | bytes 6148
  944.6 67.1 %copy-start.78 = (f32[512]{0:T(512)S(1)}, f32[512]{0:T(512)}, u32[]{:S(2)}) copy-start(f32[512]{0:T(512)} %copy-done.77) | copy-start | bytes 6148
  (108 other events, 1173.7 us)
Sparse Core Ops, SparseCore 0:
  15.9 35.8 all-gather.8
  89.3 31.8 reduce-scatter.8
  126.4 33.1 all-gather.10
  178.8 31.8 reduce-scatter.10
  215.3 33.1 all-gather.12
  295.2 31.8 reduce-scatter.12
  331.6 33.1 all-gather.14
  366.3 33.1 all-gather.16
  423.4 31.8 reduce-scatter.16
  457.4 31.8 reduce-scatter.14
  494.4 33.1 all-gather.18
  628.8 31.8 reduce-scatter.18
  668.0 33.1 all-gather.20
  725.0 31.8 reduce-scatter.20
  764.3 33.0 all-gather.22
  895.8 31.8 reduce-scatter.22
  944.8 444.4 all-reduce.4
where the time goes:
time: 1440 us; the launch traced here: 1430 us
  waiting for transfers between devices  769 us (53%)
  matrix products  323 us (22%)
  other arithmetic  179 us (12%)
  blocking collectives  104 us (7%)
  local copies, waits for them, and re-layouts  37.3 us (3%)
  between operations  15.8 us (1%)
    psum x1, waiting for transfers between devices, local(): lax.psum(as_sent(spread_stack), 'dp')  332 us
    all_gather x2, waiting for transfers between devices, layer_forward(): lax.all_gather(normed.astype(jnp.bfloat16), 'tensor', axis=0, tiled=True)  67.8 us
    all_gather x2, waiting for transfers between devices, layer_forward(): ffn_rows = lax.all_gather(normed_low, 'tensor', axis=0, tiled=True)  65.7 us
    psum x1, blocking collectives, local(): lax.psum(as_sent(spread_stack), 'dp')  64.6 us
    reduce_scatter x2, waiting for transfers between devices, layer_forward(): lax.psum_scatter(jnp.dot(lax.slice_in_dim(attended, 0, row_count * lax.ax...  63.8 us
    reduce_scatter x2, waiting for transfers between devices, layer_forward(): lax.psum_scatter(jnp.dot(lax.slice_in_dim(activated, 0, row_count * lax.a...  62 us
    all_gather x2, waiting for transfers between devices, layer_backward(): grad_rows = lax.all_gather(grad_branch, 'tensor', axis=0, tiled=True)  57.1 us
    convert_element_type x4, other arithmetic, one_sequence(): (softmax_exact * (grad_softmax - row_terms)).astype(jnp.bfloat16)  55.3 us
  transfers between devices with their start and end apart: 17, of which 16 were waited for; matrix products, arithmetic and copies ran while one was open for 8% of the time, Pallas kernels for 0%

commit v1 on v0

--- a/solution.py
+++ b/solution.py
@@ -1,6 +1,8 @@
 import jax
 import jax.numpy as jnp
 from jax import lax
+from jax.experimental import pallas as pl
+from jax.experimental.pallas import tpu as pltpu
 from jax.sharding import PartitionSpec as P
 
 HEAD_DIM = 64
@@ -309,7 +311,7 @@
     return (grad_input, spread, shared)
 
 
-def local(
+def local_general(
     tokens_in,
     segments,
     w_qkv,
@@ -362,7 +364,440 @@
     return (out_act, grad_in) + tuple(spread_stack) + tuple(shared_stack)
 
 
+CORE_BIT = 1
+X_BIT = 2
+Z_BIT = 4
+BAND = 256
+LANES = 128
+VMEM_ASKED = 56 * 2**20
+
+
+def dot_nt(left, right):
+    return lax.dot_general(left, right, (((1,), (1,)), ((), ())), preferred_element_type=jnp.float32)
+
+
+def dot_tn(left, right):
+    return lax.dot_general(left, right, (((0,), (0,)), ((), ())), preferred_element_type=jnp.float32)
+
+
+def fill_band_bias(segq_ref, segk_ref, bias_ref):
+    blocks = bias_ref.shape[0]
+    for block in range(blocks):
+        rows = slice(block * BAND, (block + 1) * BAND)
+        columns = slice(block * BAND, (block + 2) * BAND)
+        row_place = lax.broadcasted_iota(jnp.int32, (BAND, 2 * BAND), 0) + BAND
+        column_place = lax.broadcasted_iota(jnp.int32, (BAND, 2 * BAND), 1)
+        allowed = (segq_ref[rows, :] == segk_ref[:, columns]) & (column_place <= row_place)
+        bias_ref[block] = jnp.where(allowed, 0.0, masked_score)
+
+
+def band_rows(halo_ref, rows_ref, block):
+    if block == 0:
+        return jnp.concatenate([halo_ref[...], rows_ref[0:BAND, :]], axis=0)
+    return rows_ref[(block - 1) * BAND : (block + 1) * BAND, :]
+
+
+def attention_forward_kernel(
+    q_ref, k_ref, v_ref, kh_ref, vh_ref, segq_ref, segk_ref, out_ref, total_ref, bias_ref
+):
+    pair = pl.program_id(0)
+
+    @pl.when(pair == 0)
+    def _():
+        fill_band_bias(segq_ref, segk_ref, bias_ref)
+        total_ref[...] = jnp.zeros_like(total_ref)
+
+    lane = lax.broadcasted_iota(jnp.int32, (BAND, LANES), 1)
+    for block in range(bias_ref.shape[0]):
+        rows = slice(block * BAND, (block + 1) * BAND)
+        query = q_ref[rows, :]
+        keys = band_rows(kh_ref, k_ref, block)
+        values = band_rows(vh_ref, v_ref, block)
+        parts = []
+        kept = total_ref[rows, :]
+        for head in range(2):
+            mine = (lane // HEAD_DIM) == head
+            scores = dot_nt(jnp.where(mine, query, 0), keys) * HEAD_DIM ** (-0.5) + bias_ref[block]
+            highest = jnp.max(scores, axis=-1, keepdims=True)
+            raised = jnp.exp(scores - highest)
+            summed = jnp.sum(raised, axis=-1, keepdims=True)
+            weighted = jnp.dot(
+                raised.astype(jnp.bfloat16), values, preferred_element_type=jnp.float32
+            )
+            parts.append(weighted / summed)
+            kept = jnp.where(lane == 2 * pair + head, highest + jnp.log(summed), kept)
+        total_ref[rows, :] = kept
+        out_ref[rows, :] = jnp.where(lane < HEAD_DIM, parts[0], parts[1]).astype(out_ref.dtype)
+
+
+def attention_backward_kernel(
+    q_ref,
+    k_ref,
+    v_ref,
+    kh_ref,
+    vh_ref,
+    segq_ref,
+    segk_ref,
+    grad_ref,
+    total_ref,
+    dq_ref,
+    dk_ref,
+    dv_ref,
+    dkh_ref,
+    dvh_ref,
+    bias_ref,
+):
+    pair = pl.program_id(0)
+
+    @pl.when(pair == 0)
+    def _():
+        fill_band_bias(segq_ref, segk_ref, bias_ref)
+
+    lane = lax.broadcasted_iota(jnp.int32, (BAND, LANES), 1)
+    scaling = HEAD_DIM ** (-0.5)
+    blocks = bias_ref.shape[0]
+    key_parts = [None] * (blocks + 1)
+    value_parts = [None] * (blocks + 1)
+    for block in range(blocks):
+        rows = slice(block * BAND, (block + 1) * BAND)
+        query = q_ref[rows, :]
+        grad = grad_ref[rows, :]
+        keys = band_rows(kh_ref, k_ref, block)
+        values = band_rows(vh_ref, v_ref, block)
+        grad_query = []
+        grad_keys = 0.0
+        grad_values = 0.0
+        for head in range(2):
+            mine = (lane // HEAD_DIM) == head
+            query_head = jnp.where(mine, query, 0)
+            grad_head = jnp.where(mine, grad, 0)
+            scores = dot_nt(query_head, keys) * scaling + bias_ref[block]
+            total = jnp.sum(
+                jnp.where(lane == 2 * pair + head, total_ref[rows, :], 0.0), axis=-1, keepdims=True
+            )
+            exact = jnp.exp(scores - total)
+            low = exact.astype(jnp.bfloat16)
+            grad_probs = dot_nt(grad_head, values)
+            row_terms = jnp.sum(exact * grad_probs, axis=-1, keepdims=True)
+            grad_scores = (exact * (grad_probs - row_terms)).astype(jnp.bfloat16)
+            grad_query.append(jnp.dot(grad_scores, keys, preferred_element_type=jnp.float32))
+            grad_keys = grad_keys + dot_tn(grad_scores, query_head)
+            grad_values = grad_values + dot_tn(low, grad_head)
+        dq_ref[rows, :] = (jnp.where(lane < HEAD_DIM, grad_query[0], grad_query[1]) * scaling).astype(
+            dq_ref.dtype
+        )
+        grad_keys = grad_keys * scaling
+        for part in range(2):
+            cut = slice(part * BAND, (part + 1) * BAND)
+            before_k, before_v = key_parts[block + part], value_parts[block + part]
+            key_parts[block + part] = (
+                grad_keys[cut] if before_k is None else before_k + grad_keys[cut]
+            )
+            value_parts[block + part] = (
+                grad_values[cut] if before_v is None else before_v + grad_values[cut]
+            )
+    dkh_ref[...] = key_parts[0].astype(dkh_ref.dtype)
+    dvh_ref[...] = value_parts[0].astype(dvh_ref.dtype)
+    for block in range(blocks):
+        rows = slice(block * BAND, (block + 1) * BAND)
+        dk_ref[rows, :] = key_parts[block + 1]
+        dv_ref[rows, :] = value_parts[block + 1]
+
+
+def attention_specs(rows, pairs):
+    whole = lambda pair: (0, 0)
+    return [
+        pl.BlockSpec((rows, LANES), lambda pair: (0, pair)),
+        pl.BlockSpec((rows, LANES), lambda pair: (0, pairs + pair)),
+        pl.BlockSpec((rows, LANES), lambda pair: (0, 2 * pairs + pair)),
+        pl.BlockSpec((BAND, LANES), lambda pair: (0, pair)),
+        pl.BlockSpec((BAND, LANES), lambda pair: (0, pairs + pair)),
+        pl.BlockSpec((rows, 1), whole),
+        pl.BlockSpec((1, rows + BAND), whole),
+    ]
+
+
+def attention_forward(projected, halo, segq, segk):
+    rows, wide = projected.shape
+    width = wide // 3
+    pairs = width // LANES
+    return pl.pallas_call(
+        attention_forward_kernel,
+        grid=(pairs,),
+        in_specs=attention_specs(rows, pairs),
+        out_specs=[
+            pl.BlockSpec((rows, LANES), lambda pair: (0, pair)),
+            pl.BlockSpec((rows, LANES), lambda pair: (0, 0)),
+        ],
+        out_shape=[
+            jax.ShapeDtypeStruct((rows, width), jnp.bfloat16),
+            jax.ShapeDtypeStruct((rows, LANES), jnp.float32),
+        ],
+        scratch_shapes=[pltpu.VMEM((rows // BAND, BAND, 2 * BAND), jnp.float32)],
+        compiler_params=pltpu.CompilerParams(vmem_limit_bytes=VMEM_ASKED),
+        cost_estimate=pl.CostEstimate(
+            flops=8 * rows * BAND * width, bytes_accessed=10 * rows * width, transcendentals=rows * width * 8
+        ),
+        name="attention_forward",
+    )(projected, projected, projected, halo, halo, segq, segk)
+
+
+def attention_backward(projected, halo, segq, segk, grad, totals):
+    rows, wide = projected.shape
+    width = wide // 3
+    pairs = width // LANES
+    by_pair = lambda pair: (0, pair)
+    return pl.pallas_call(
+        attention_backward_kernel,
+        grid=(pairs,),
+        in_specs=attention_specs(rows, pairs)
+        + [pl.BlockSpec((rows, LANES), by_pair), pl.BlockSpec((rows, LANES), lambda pair: (0, 0))],
+        out_specs=[
+            pl.BlockSpec((rows, LANES), by_pair),
+            pl.BlockSpec((rows, LANES), by_pair),
+            pl.BlockSpec((rows, LANES), by_pair),
+            pl.BlockSpec((BAND, LANES), by_pair),
+            pl.BlockSpec((BAND, LANES), by_pair),
+        ],
+        out_shape=[
+            jax.ShapeDtypeStruct((rows, width), jnp.bfloat16),
+            jax.ShapeDtypeStruct((rows, width), jnp.float32),
+            jax.ShapeDtypeStruct((rows, width), jnp.float32),
+            jax.ShapeDtypeStruct((BAND, width), jnp.bfloat16),
+            jax.ShapeDtypeStruct((BAND, width), jnp.bfloat16),
+        ],
+        scratch_shapes=[pltpu.VMEM((rows // BAND, BAND, 2 * BAND), jnp.float32)],
+        compiler_params=pltpu.CompilerParams(vmem_limit_bytes=VMEM_ASKED),
+        cost_estimate=pl.CostEstimate(
+            flops=20 * rows * BAND * width, bytes_accessed=20 * rows * width, transcendentals=rows * width * 8
+        ),
+        name="attention_backward",
+    )(projected, projected, projected, halo, halo, segq, segk, grad, totals)
+
+
+def swap_dp(array, bit):
+    count = lax.axis_size("dp")
+    return lax.ppermute(array, "dp", [(i, i ^ bit) for i in range(count)])
+
+
+def swap_y(array):
+    return lax.ppermute(array, "tensor", [(0, 1), (1, 0)])
+
+
+def swap_windows(array):
+    pairs = []
+    for group in range(lax.axis_size("dp") // 2):
+        for core in range(2):
+            for y in range(2):
+                pairs.append(((2 * group + core) * 2 + y, (2 * group + y) * 2 + core))
+    return lax.ppermute(array, ("dp", "tensor"), pairs)
+
+
+def half_of(array, bit):
+    rows = array.shape[0] // 2
+    return lax.dynamic_slice_in_dim(array, bit * rows, rows, axis=0)
+
+
+def join_halves(bit, mine, other):
+    return jnp.where(
+        bit == 0, jnp.concatenate([mine, other], axis=0), jnp.concatenate([other, mine], axis=0)
+    )
+
+
+def other_half(array, hops):
+    if not hops:
+        return swap_y(array)
+    bit, place = hops[-1]
+    mine = other_half(half_of(array, place), hops[:-1])
+    return join_halves(place, mine, swap_dp(mine, bit))
+
+
+def add_low(left, right):
+    return (left.astype(jnp.float32) + right.astype(jnp.float32)).astype(jnp.bfloat16)
+
+
+def reduce_grad(own, other, core):
+    own_kept = add_low(half_of(own, core), swap_dp(half_of(own, 1 - core), CORE_BIT))
+    other_kept = add_low(half_of(other, core), swap_dp(half_of(other, 1 - core), CORE_BIT))
+    mine = add_low(own_kept, swap_y(other_kept))
+    count = lax.axis_size("dp")
+    groups = [[i for i in range(count) if i % 2 == member] for member in range(2)]
+    summed = lax.psum(mine, "dp", axis_index_groups=groups)
+    return join_halves(core, summed, swap_dp(summed, CORE_BIT)).astype(jnp.float32)
+
+
+def dot_low(left, right):
+    return jnp.dot(left, right, preferred_element_type=jnp.float32)
+
+
+def local_split(
+    tokens_in,
+    segments,
+    w_qkv,
+    qv_bias,
+    w_out,
+    w_up,
+    up_bias,
+    w_down,
+    out_bias,
+    ln_gain,
+    ln_bias,
+    cotangent,
+):
+    layers, width = w_qkv.shape[0], w_qkv.shape[1]
+    rows = tokens_in.shape[0]
+    place = lax.axis_index("dp")
+    y = lax.axis_index("tensor")
+    core, x = place % 2, (place // 2) % 2
+    hops = [(X_BIT, x), (CORE_BIT, core)]
+
+    residual = swap_windows(tokens_in).astype(jnp.float32)
+    grad_residual = swap_windows(cotangent)
+    window_segments = jnp.where(core == y, segments, swap_dp(segments, CORE_BIT))
+    own_segments = lax.dynamic_slice_in_dim(window_segments, core * rows, rows, axis=1)
+    halo_segments = jnp.where(core == 1, window_segments[:, rows - BAND : rows], -1)
+    segq = own_segments.reshape(rows, 1)
+    segk = jnp.concatenate([halo_segments, own_segments], axis=1)
+
+    def natural(own, other):
+        return join_halves(y, own, other)
+
+    qkv_rows = [w_qkv[l].reshape(width, -1) for l in range(layers)]
+    weights = []
+    for l in range(layers):
+        own = (qkv_rows[l], w_out[l], w_up[l], w_down[l])
+        other = tuple(other_half(member, hops) for member in own)
+        bias_own = (qv_bias[l].reshape(-1), up_bias[l])
+        bias_other = tuple(swap_y(member) for member in bias_own)
+        weights.append(tuple(zip(own + bias_own, other + bias_other)))
+
+    kept = []
+    count = lax.axis_size("dp")
+    to_second = [(2 * i, 2 * i + 1) for i in range(count // 2)]
+    to_first = [(2 * i + 1, 2 * i) for i in range(count // 2)]
+    for l in range(layers):
+        qkv, out_w, up, down, qv, upb = weights[l]
+        normed, _, _ = layer_norm(residual, ln_gain[l, 0], ln_bias[l, 0])
+        normed = normed.astype(jnp.bfloat16)
+        saved_attention = []
+        branch = 0.0
+        for half in range(2):
+            third = qkv[half].shape[1] // 3
+            bias = jnp.concatenate(
+                [qv[half][:third], jnp.zeros((third,), jnp.float32), qv[half][third:]]
+            )
+            projected = (dot_low(normed, qkv[half]) + bias).astype(jnp.bfloat16)
+            halo = lax.ppermute(projected[rows - BAND :, third:], "dp", to_second)
+            attended, totals = attention_forward(projected, halo, segq, segk)
+            branch = branch + dot_low(attended, out_w[half])
+            saved_attention.append((projected, halo, attended, totals))
+        middle = residual + branch + out_bias[l, 0]
+        normed_two, _, _ = layer_norm(middle, ln_gain[l, 1], ln_bias[l, 1])
+        normed_two = normed_two.astype(jnp.bfloat16)
+        saved_ffn = []
+        branch = 0.0
+        for half in range(2):
+            before = dot_low(normed_two, up[half]) + upb[half]
+            activated = gelu_tanh(before).astype(jnp.bfloat16)
+            slope = gelu_slope(before).astype(jnp.bfloat16)
+            branch = branch + dot_low(activated, down[half])
+            saved_ffn.append((activated, slope))
+        kept.append((residual, normed, saved_attention, middle, normed_two, saved_ffn))
+        residual = middle + branch + out_bias[l, 1]
+    out_act = swap_windows(residual.astype(jnp.bfloat16))
+
+    grad_residual = grad_residual.astype(jnp.float32)
+    grads = [None] * layers
+    vectors = [None] * layers
+    for l in reversed(range(layers)):
+        qkv, out_w, up, down, qv, upb = weights[l]
+        residual, normed, saved_attention, middle, normed_two, saved_ffn = kept[l]
+        grad_branch = grad_residual.astype(jnp.bfloat16)
+        grad_down, grad_up, grad_up_bias = [], [], []
+        incoming = 0.0
+        for half in range(2):
+            activated, slope = saved_ffn[half]
+            grad_before = (dot_nt(grad_branch, down[half]) * slope.astype(jnp.float32)).astype(
+                jnp.bfloat16
+            )
+            grad_down.append(dot_tn(activated, grad_branch).astype(jnp.bfloat16))
+            grad_up.append(dot_tn(normed_two, grad_before).astype(jnp.bfloat16))
+            grad_up_bias.append(jnp.sum(grad_before, axis=0, dtype=jnp.float32))
+            incoming = incoming + dot_nt(grad_before, up[half])
+        _, unit, inverse = layer_norm(middle, ln_gain[l, 1], ln_bias[l, 1])
+        through, gain_two, shift_two = norm_backward(incoming, unit, inverse, ln_gain[l, 1])
+        grad_middle = grad_residual + through
+        grad_attn = grad_middle.astype(jnp.bfloat16)
+        grad_out, grad_qkv, grad_qv = [], [], []
+        incoming = 0.0
+        for half in range(2):
+            projected, halo, attended, totals = saved_attention[half]
+            grad_out.append(dot_tn(attended, grad_attn).astype(jnp.bfloat16))
+            grad_attended = dot_nt(grad_attn, out_w[half]).astype(jnp.bfloat16)
+            dq, dk, dv, dkh, dvh = attention_backward(
+                projected, halo, segq, segk, grad_attended, totals
+            )
+            sent = lax.ppermute(jnp.concatenate([dkh, dvh], axis=1), "dp", to_first)
+            whole = jnp.pad(sent, ((rows - BAND, 0), (0, 0))).astype(jnp.float32)
+            third = dk.shape[1]
+            grad_projected = jnp.concatenate(
+                [
+                    dq,
+                    (dk + whole[:, :third]).astype(jnp.bfloat16),
+                    (dv + whole[:, third:]).astype(jnp.bfloat16),
+                ],
+                axis=1,
+            )
+            grad_qkv.append(dot_tn(normed, grad_projected).astype(jnp.bfloat16))
+            sums = jnp.sum(grad_projected, axis=0, dtype=jnp.float32)
+            grad_qv.append(jnp.stack([sums[:third], sums[2 * third :]]))
+            incoming = incoming + dot_nt(grad_projected, qkv[half])
+        _, unit, inverse = layer_norm(residual, ln_gain[l, 0], ln_bias[l, 0])
+        through, gain_one, shift_one = norm_backward(incoming, unit, inverse, ln_gain[l, 0])
+        grads[l] = tuple(
+            reduce_grad(pair[0], pair[1], core) for pair in (grad_qkv, grad_out, grad_up, grad_down)
+        )
+        vectors[l] = jnp.concatenate(
+            [
+                natural(grad_qv[0].T, grad_qv[1].T).T.reshape(-1),
+                natural(grad_up_bias[0], grad_up_bias[1]),
+                jnp.sum(grad_attn, axis=0, dtype=jnp.float32),
+                jnp.sum(grad_branch, axis=0, dtype=jnp.float32),
+                gain_one,
+                gain_two,
+                shift_one,
+                shift_two,
+            ]
+        )
+        grad_residual = grad_middle + through
+    grad_in = swap_windows(grad_residual.astype(jnp.bfloat16))
+    summed = lax.psum(jnp.stack(vectors), ("dp", "tensor"))
+    hidden = 2 * up_bias.shape[1]
+    ends = [2 * width, 2 * width + hidden, 4 * width + hidden, 6 * width + hidden]
+    qv_sum = summed[:, : ends[0]].reshape(layers, 2, width)
+    grad_qv_bias = lax.dynamic_slice_in_dim(qv_sum, y * (width // 2), width // 2, axis=2)
+    grad_up_bias = lax.dynamic_slice_in_dim(
+        summed[:, ends[0] : ends[1]], y * (hidden // 2), hidden // 2, axis=1
+    )
+    stacked = [jnp.stack([grads[l][member] for l in range(layers)]) for member in range(4)]
+    return (
+        out_act,
+        grad_in,
+        stacked[0].reshape(w_qkv.shape),
+        grad_qv_bias,
+        stacked[1],
+        stacked[2],
+        grad_up_bias,
+        stacked[3],
+        summed[:, ends[1] : ends[2]].reshape(layers, 2, width),
+        summed[:, ends[2] : ends[3]].reshape(layers, 2, width),
+        summed[:, ends[3] :].reshape(layers, 2, width),
+    )
+
+
 def solution(mesh):
+    sizes = (mesh.shape["dp"], mesh.shape["tensor"])
+    local = local_split if sizes == (16, 2) else local_general
     return jax.shard_map(
         local,
         mesh=mesh,

time: 1440 us -> 1410 us (0.979)
  matrix products: 323 us -> 181 us
  blocking collectives: 104 us -> 0 us
  Pallas kernels: 0 us -> 81.9 us
  local copies, waits for them, and re-layouts: 37.3 us -> 108 us
  starting transfers between devices: 2.21 us -> 72.5 us
  other arithmetic: 179 us -> 138 us
  waiting for transfers between devices: 769 us -> 797 us
    ppermute x0 -> x73, waiting for transfers between devices: none -> 309 us  [the longest x20 253 us: swap_y(): return lax.ppermute(array, 'tensor', [(0, 1), (1, 0)])]
    all_gather x8 -> x0, waiting for transfers between devices: 239 us -> none  [the longest x2 67.8 us: layer_forward(): lax.all_gather(normed.astype(jnp.bfloat16), 'tensor', axis=0, tiled=True)]
    reduce_scatter x8 -> x0, waiting for transfers between devices: 197 us -> none  [the longest x2 63.8 us: layer_forward(): lax.psum_scatter(jnp.dot(lax.slice_in_dim(attended, 0, row_count * lax.ax...]
    psum x1 -> x2, waiting for transfers between devices: 332 us -> 487 us  [the longest x1 368 us: reduce_grad(): summed = lax.psum(mine, 'dp', axis_index_groups=groups)]
    dot_general x48, matrix products: 323 us -> 181 us  [the longest x16 78.4 us: dot_nt(): lax.dot_general(left, right, (((1,), (1,)), ((), ())), preferred_element_...]
    psum x2 -> x0, blocking collectives: 104 us -> none  [the longest x1 64.6 us: local(): lax.psum(as_sent(spread_stack), 'dp')]
    pallas_call x0 -> x8, Pallas kernels: none -> 81.9 us  [the longest x4 49.5 us: attention_backward(): pl.pallas_call(attention_backward_kernel, grid=(pairs,), in_specs=attenti...]
    ppermute x0 -> x73, starting transfers between devices: none -> 72.4 us  [the longest x41 24.1 us: swap_dp(): return lax.ppermute(array, 'dp', [(i, i ^ bit) for i in range(count)])]
  transfers between devices with their start and end apart: 17 -> 75, of which waited for: 16 -> 16; matrix products, arithmetic and copies ran while one was open for 8% -> 25% of each run, Pallas kernels for 0% -> 5%
where the time goes in v1:
time: 1410 us; the launch traced here: 1400 us
  waiting for transfers between devices  797 us (57%)
  matrix products  181 us (13%)
  other arithmetic  138 us (10%)
  local copies, waits for them, and re-layouts  108 us (8%)
  Pallas kernels  81.9 us (6%)
  starting transfers between devices  72.5 us (5%)
  between operations  18.9 us (1%)
    psum x1, waiting for transfers between devices, reduce_grad(): summed = lax.psum(mine, 'dp', axis_index_groups=groups)  368 us
    ppermute x20, waiting for transfers between devices, swap_y(): return lax.ppermute(array, 'tensor', [(0, 1), (1, 0)])  253 us
    psum x1, waiting for transfers between devices, local_split(): summed = lax.psum(jnp.stack(vectors), ('dp', 'tensor'))  119 us
    dot_general x16, matrix products, dot_nt(): lax.dot_general(left, right, (((1,), (1,)), ((), ())), preferred_element_...  78.4 us
    ppermute x41, waiting for transfers between devices, swap_dp(): return lax.ppermute(array, 'dp', [(i, i ^ bit) for i in range(count)])  56 us
    dot_general x16, matrix products, dot_low(): return jnp.dot(left, right, preferred_element_type=jnp.float32)  55.7 us
    select_n x15, other arithmetic, join_halves(): jnp.where(bit == 0, jnp.concatenate([mine, other], axis=0), jnp.concatena...  50.7 us
    pallas_call x4, Pallas kernels, attention_backward(): pl.pallas_call(attention_backward_kernel, grid=(pairs,), in_specs=attenti...  49.5 us
  transfers between devices with their start and end apart: 75, of which 16 were waited for; matrix products, arithmetic and copies ran while one was open for 25% of the time, Pallas kernels for 5%

profile of v1, /device:TPU:0, one launch (start us, length us, event | category | flops | bytes accessed | tf_op | source)
XLA Modules:
  0.0 1396.5 jit_solution(1176205921494066605)
XLA Ops:
  67.6 11.4 collective-permute-done.4
  99.9 10.4 collective-permute-done.15
  115.4 8.1 attention_forward.4
  123.5 8.5 collective-permute-done.11
  146.2 16.2 %collective-permute-done.12 = bf16[256,2048]{1,0:T(8,128)(2,1)S(1)} collective-permute-done((bf16[256,2048]{1,0:T(8,128)(2,1)}, bf16[256,2048]{1,0:T(8,128)(2,1)S(1)}, u32[]{:S(2)}, u32[]{:S(2)}) %collective-permute-start.12) | collective-permute-done | bytes 1048608 | tf_op jit(solution)/shard_map/ppermute | solution.py:580
  166.8 8.1 attention_forward.5
  216.5 18.3 %collective-permute-done.32 = bf16[512,1024]{1,0:T(8,128)(2,1)} collective-permute-done((bf16[512,1024]{1,0:T(8,128)(2,1)}, bf16[512,1024]{1,0:T(8,128)(2,1)}, u32[]{:S(2)}, u32[]{:S(2)}) %collective-permute-start.32) | collective-permute-done | bytes 1048608 | tf_op jit(solution)/shard_map/ppermute | solution.py:580
  242.9 8.0 attention_forward.7
  251.7 8.2 attention_forward.6
  264.5 8.4 fusion.77
  275.3 9.2 convert_reduce_fusion.1
  287.3 10.4 convert_reduce_fusion
  297.7 7.8 multiply_reduce_fusion
  323.8 12.3 attention_backward.5
  340.6 12.4 attention_backward.4
  390.8 6.8 convert_reduce_fusion.3
  408.4 10.3 convert_reduce_fusion.2
  453.3 12.3 attention_backward.7
  471.6 12.5 attention_backward.6
  496.6 10.8 collective-permute-done.51
  532.1 27.4 %collective-permute-done.47 = bf16[512,1536]{1,0:T(8,128)(2,1)} collective-permute-done((bf16[512,1536]{1,0:T(8,128)(2,1)}, bf16[512,1536]{1,0:T(8,128)(2,1)}, u32[]{:S(2)}, u32[]{:S(2)}) %collective-permute-start.47) | collective-permute-done | bytes 1572896 | tf_op jit(solution)/shard_map/ppermute | solution.py:584
  563.7 74.5 %collective-permute-done.43 = bf16[512,1536]{1,0:T(8,128)(2,1)} collective-permute-done((bf16[512,1536]{1,0:T(8,128)(2,1)}, bf16[512,1536]{1,0:T(8,128)(2,1)}, u32[]{:S(2)}, u32[]{:S(2)}) %collective-permute-start.43) | collective-permute-done | bytes 1572896 | tf_op jit(solution)/shard_map/ppermute | solution.py:584
  648.1 35.0 %collective-permute-done.63 = bf16[512,2048]{1,0:T(8,128)(2,1)} collective-permute-done((bf16[512,2048]{1,0:T(8,128)(2,1)S(1)}, bf16[512,2048]{1,0:T(8,128)(2,1)}, u32[]{:S(2)}, u32[]{:S(2)}) %collective-permute-start.63) | collective-permute-done | bytes 2097184 | tf_op jit(solution)/shard_map/ppermute | solution.py:584
  687.9 40.0 %collective-permute-done.59 = bf16[512,2048]{1,0:T(8,128)(2,1)S(1)} collective-permute-done((bf16[512,2048]{1,0:T(8,128)(2,1)S(1)}, bf16[512,2048]{1,0:T(8,128)(2,1)S(1)}, u32[]{:S(2)}, u32[]{:S(2)}) %collective-permute-start.59) | collective-permute-done | bytes 2097184 | tf_op jit(solution)/shard_map/ppermute | solution.py:584
  730.6 41.8 %collective-permute-done.67 = bf16[1024,1024]{1,0:T(8,128)(2,1)S(1)} collective-permute-done((bf16[1024,1024]{1,0:T(8,128)(2,1)S(1)}, bf16[1024,1024]{1,0:T(8,128)(2,1)S(1)}, u32[]{:S(2)}, u32[]{:S(2)}) %collective-permute-start.67) | collective-permute-done | bytes 2097184 | tf_op jit(solution)/shard_map/ppermute | solution.py:584
  782.5 7.9 add_convert_fusion.18
  790.4 9.8 collective-permute-start.34
  812.9 368.4 %all-reduce.10.cloned.1.call-done = (bf16[512,1536]{1,0:T(8,128)(2,1)}, bf16[512,1536]{1,0:T(8,128)(2,1)}, bf16[256,1024]{1,0:T(8,128)(2,1)}, bf16[256,1024]{1,0...) async-done(((bf16[512,1536]{1,0:T(8,128)(2,1)}, bf16[512,1536]{1,0:T(8,128)(2,1)}, ...) | async-done | bytes 12582928 | tf_op jit(solution)/shard_map/psum | solution.py:625
  1183.3 118.7 %all-reduce.8.cloned.1.call-done = f32[2,12288]{1,0:T(2,128)} async-done(((f32[2,12288]{1,0:T(2,128)}), f32[2,12288]{1,0:T(2,128)}) %all-reduce.8.cloned.1.call-update) | async-done | bytes 98320 | tf_op jit(solution)/shard_map/psum | solution.py:774
  1332.8 12.8 copy.45
  1365.2 10.7 maximum_convert_fusion.1
  1375.9 9.5 maximum_convert_fusion
  (731 shorter events, 410.8 us)
Async XLA Ops:
  8.0 1173.3 %all-reduce.10.cloned.1.call-start = ((), (), s32[]{:S(2)}) async-start(), calls=%async_computation.1 | async-start | bytes 25165824 | tf_op jit(solution)/shard_map/psum | solution.py:625
  8.8 47.4 %collective-permute-start.6 = (f32[1024]{0:T(1024)S(1)}, f32[1024]{0:T(1024)S(1)}, u32[]{:S(2)}, u32[]{:S(2)}) collective-permute-start(f32[1024]{0:T(1024)S(1)} %bitcast.249), channel_id=1, source_target_pairs={{0,1},{1,0},{2,3},{3,2},{4,5},{5,4},{6,7},{7,6},{8,9},{9,8},{10,11... | collective-permute-start | bytes 12296 | tf_op jit(solution)/shard_map/ppermute | solution.py:584
  11.7 46.5 %collective-permute-start.22 = (f32[1024]{0:T(1024)S(1)}, f32[1024]{0:T(1024)S(1)}, u32[]{:S(2)}, u32[]{:S(2)}) collective-permute-start(f32[1024]{0:T(1024)S(1)} %bitcast.248), channel_id=1, source_target_pairs={{0,1},{1,0},{2,3},{3,2},{4,5},{5,4},{6,7},{7,6},{8,9},{9,8},{10,11... | collective-permute-start | bytes 12296 | tf_op jit(solution)/shard_map/ppermute | solution.py:584
  11.8 53.5 %collective-permute-start = (bf16[512,1024]{1,0:T(8,128)(2,1)}, bf16[512,1024]{1,0:T(8,128)(2,1)S(1)}, u32[]{:S(2)}, u32[]{:S(2)}) collective-permute-start(bf16[512,1024]{1,0:T(8,128)(2,1)} %param.12), channel_id=1, source_target_pairs={{0,0},{1,2},{2,1},{3,3},{4,4},{5,6},{6,5},{7,7},{8,8},{9,10},{10,9... | collective-permute-start | bytes 3145736 | tf_op jit(solution)/shard_map/ppermute | solution.py:593
  81.9 50.4 %collective-permute-start.5 = (bf16[512,1536]{0,1:T(8,128)(2,1)}, bf16[512,1536]{0,1:T(8,128)(2,1)}, u32[]{:S(2)}, u32[]{:S(2)}) collective-permute-start(bf16[512,1536]{0,1:T(8,128)(2,1)} %maximum_select_fusion.16), channel_id=1, source_target_pairs={{0,2},{2,0},{4,6},{6,4},{8,10},{10,8},{12,14},{14,12},{16,18},{18,... | collective-permute-start | bytes 4718600 | tf_op jit(solution)/shard_map/ppermute | solution.py:580
  82.4 49.6 %collective-permute-start.11 = (bf16[256,2048]{1,0:T(8,128)(2,1)}, bf16[256,2048]{1,0:T(8,128)(2,1)}, u32[]{:S(2)}, u32[]{:S(2)}) collective-permute-start(bf16[256,2048]{1,0:T(8,128)(2,1)} %dynamic-slice_bitcast_fusion.3), channel_id=1, source_target_pairs={{0,1},{1,0},{2,3},{3,2},{4,5},{5,4},{6,7},{7,6},{8,9},{9,8},{10,11... | collective-permute-start | bytes 3145736 | tf_op jit(solution)/shard_map/ppermute | solution.py:584
  114.6 78.7 %collective-permute-start.14 = (f32[2048]{0:T(1024)S(1)}, f32[2048]{0:T(1024)S(1)}, u32[]{:S(2)}, u32[]{:S(2)}) collective-permute-start(f32[2048]{0:T(1024)S(1)} %bitcast.232), channel_id=1, source_target_pairs={{0,1},{1,0},{2,3},{3,2},{4,5},{5,4},{6,7},{7,6},{8,9},{9,8},{10,11... | collective-permute-start | bytes 24584 | tf_op jit(solution)/shard_map/ppermute | solution.py:584
  131.9 54.4 %collective-permute-start.27 = (bf16[256,2048]{1,0:T(8,128)(2,1)}, bf16[256,2048]{1,0:T(8,128)(2,1)}, u32[]{:S(2)}, u32[]{:S(2)}) collective-permute-start(bf16[256,2048]{1,0:T(8,128)(2,1)} %dynamic-slice_bitcast_fusion.1), channel_id=1, source_target_pairs={{0,1},{1,0},{2,3},{3,2},{4,5},{5,4},{6,7},{7,6},{8,9},{9,8},{10,11... | collective-permute-start | bytes 3145736 | tf_op jit(solution)/shard_map/ppermute | solution.py:584
  186.4 73.5 %collective-permute-start.26 = (bf16[256,1024]{1,0:T(8,128)(2,1)}, bf16[256,1024]{1,0:T(8,128)(2,1)}, u32[]{:S(2)}, u32[]{:S(2)}) collective-permute-start(bf16[256,1024]{1,0:T(8,128)(2,1)} %maximum_select_fusion.35), channel_id=1, source_target_pairs={{0,2},{2,0},{4,6},{6,4},{8,10},{10,8},{12,14},{14,12},{16,18},{18,... | collective-permute-start | bytes 1572872 | tf_op jit(solution)/shard_map/ppermute | solution.py:580
  188.3 46.5 %collective-permute-start.32 = (bf16[512,1024]{1,0:T(8,128)(2,1)}, bf16[512,1024]{1,0:T(8,128)(2,1)}, u32[]{:S(2)}, u32[]{:S(2)}) collective-permute-start(bf16[512,1024]{1,0:T(8,128)(2,1)} %collective-permute-done.31), channel_id=1, source_target_pairs={{0,4},{2,6},{4,0},{6,2},{8,12},{10,14},{12,8},{14,10},{16,20},{18,... | collective-permute-start | bytes 3145736 | tf_op jit(solution)/shard_map/ppermute | solution.py:580
  205.1 45.8 %collective-permute-start.18 = (bf16[256,1024]{1,0:T(8,128)(2,1)S(1)}, bf16[256,1024]{1,0:T(8,128)(2,1)S(1)}, u32[]{:S(2)}, u32[]{:S(2)}) collective-permute-start(bf16[256,1024]{1,0:T(8,128)(2,1)S(1)} %slice.259), channel_id=1, source_target_pairs={{0,2},{4,6},{8,10},{12,14},{16,18},{20,22},{24,26},{28,30},{1,3},{... | collective-permute-start | bytes 1572872 | tf_op jit(solution)/shard_map/ppermute | solution.py:690
  216.5 48.0 %collective-permute-start.29 = (bf16[512,2048]{1,0:T(8,128)(2,1)}, bf16[512,2048]{1,0:T(8,128)(2,1)}, u32[]{:S(2)}, u32[]{:S(2)}) collective-permute-start(bf16[512,2048]{1,0:T(8,128)(2,1)} %maximum_select_fusion.14), channel_id=1, source_target_pairs={{0,2},{2,0},{4,6},{6,4},{8,10},{10,8},{12,14},{14,12},{16,18},{18,... | collective-permute-start | bytes 6291464 | tf_op jit(solution)/shard_map/ppermute | solution.py:580
  234.8 52.4 %collective-permute-start.30 = (f32[2048]{0:T(1024)S(1)}, f32[2048]{0:T(1024)S(1)}, u32[]{:S(2)}, u32[]{:S(2)}) collective-permute-start(f32[2048]{0:T(1024)S(1)} %bitcast.228), channel_id=1, source_target_pairs={{0,1},{1,0},{2,3},{3,2},{4,5},{5,4},{6,7},{7,6},{8,9},{9,8},{10,11... | collective-permute-start | bytes 24584 | tf_op jit(solution)/shard_map/ppermute | solution.py:584
  339.2 147.0 %collective-permute-start.53 = (bf16[256,1024]{1,0:T(8,128)(2,1)}, bf16[256,1024]{1,0:T(8,128)(2,1)}, u32[]{:S(2)}, u32[]{:S(2)}) collective-permute-start(bf16[256,1024]{1,0:T(8,128)(2,1)} %constant_dynamic-slice_fusion.10), channel_id=1, source_target_pairs={{0,2},{2,0},{4,6},{6,4},{8,10},{10,8},{12,14},{14,12},{16,18},{18,... | collective-permute-start | bytes 1572872 | tf_op jit(solution)/shard_map/ppermute | solution.py:580
  340.5 96.1 %collective-permute-start.54 = (bf16[256,1024]{1,0:T(8,128)(2,1)}, bf16[256,1024]{1,0:T(8,128)(2,1)}, u32[]{:S(2)}, u32[]{:S(2)}) collective-permute-start(bf16[256,1024]{1,0:T(8,128)(2,1)} %constant_dynamic-slice_fusion.9), channel_id=1, source_target_pairs={{0,2},{2,0},{4,6},{6,4},{8,10},{10,8},{12,14},{14,12},{16,18},{18,... | collective-permute-start | bytes 1572872 | tf_op jit(solution)/shard_map/ppermute | solution.py:580
  373.0 137.2 %collective-permute-start.69 = (bf16[1024,1024]{1,0:T(8,128)(2,1)}, bf16[1024,1024]{1,0:T(8,128)(2,1)}, u32[]{:S(2)}, u32[]{:S(2)}) collective-permute-start(bf16[1024,1024]{1,0:T(8,128)(2,1)} %constant_dynamic-slice_fusion.1), channel_id=1, source_target_pairs={{0,2},{2,0},{4,6},{6,4},{8,10},{10,8},{12,14},{14,12},{16,18},{18,... | collective-permute-start | bytes 6291464 | tf_op jit(solution)/shard_map/ppermute | solution.py:580
  439.3 48.1 %collective-permute-start.55 = (bf16[256,1024]{1,0:T(8,128)(2,1)}, bf16[256,1024]{1,0:T(8,128)(2,1)}, u32[]{:S(2)}, u32[]{:S(2)}) collective-permute-start(bf16[256,1024]{1,0:T(8,128)(2,1)} %add_convert_fusion.23), channel_id=1, source_target_pairs={{0,1},{1,0},{2,3},{3,2},{4,5},{5,4},{6,7},{7,6},{8,9},{9,8},{10,11... | collective-permute-start | bytes 1572872 | tf_op jit(solution)/shard_map/ppermute | solution.py:584
  523.0 115.2 %collective-permute-start.71 = (bf16[1024,1024]{1,0:T(8,128)(2,1)S(1)}, bf16[1024,1024]{1,0:T(8,128)(2,1)}, u32[]{:S(2)}, u32[]{:S(2)}) collective-permute-start(bf16[1024,1024]{1,0:T(8,128)(2,1)S(1)} %add_convert_fusion.1), channel_id=1, source_target_pairs={{0,1},{1,0},{2,3},{3,2},{4,5},{5,4},{6,7},{7,6},{8,9},{9,8},{10,11... | collective-permute-start | bytes 6291464 | tf_op jit(solution)/shard_map/ppermute | solution.py:584
  527.0 111.2 %collective-permute-start.43 = (bf16[512,1536]{1,0:T(8,128)(2,1)}, bf16[512,1536]{1,0:T(8,128)(2,1)}, u32[]{:S(2)}, u32[]{:S(2)}) collective-permute-start(bf16[512,1536]{1,0:T(8,128)(2,1)} %add_convert_fusion.16), channel_id=1, source_target_pairs={{0,1},{1,0},{2,3},{3,2},{4,5},{5,4},{6,7},{7,6},{8,9},{9,8},{10,11... | collective-permute-start | bytes 4718600 | tf_op jit(solution)/shard_map/ppermute | solution.py:584
  530.2 152.9 %collective-permute-start.63 = (bf16[512,2048]{1,0:T(8,128)(2,1)S(1)}, bf16[512,2048]{1,0:T(8,128)(2,1)}, u32[]{:S(2)}, u32[]{:S(2)}) collective-permute-start(bf16[512,2048]{1,0:T(8,128)(2,1)S(1)} %add_convert_fusion.7), channel_id=1, source_target_pairs={{0,1},{1,0},{2,3},{3,2},{4,5},{5,4},{6,7},{7,6},{8,9},{9,8},{10,11... | collective-permute-start | bytes 6291464 | tf_op jit(solution)/shard_map/ppermute | solution.py:584
  532.1 155.8 %collective-permute-start.57 = (bf16[512,2048]{1,0:T(8,128)(2,1)S(1)}, bf16[512,2048]{1,0:T(8,128)(2,1)S(1)}, u32[]{:S(2)}, u32[]{:S(2)}) collective-permute-start(bf16[512,2048]{1,0:T(8,128)(2,1)S(1)} %copy-done.64), channel_id=1, source_target_pairs={{0,2},{2,0},{4,6},{6,4},{8,10},{10,8},{12,14},{14,12},{16,18},{18,... | collective-permute-start | bytes 6291464 | tf_op jit(solution)/shard_map/ppermute | solution.py:580
  559.5 168.4 %collective-permute-start.59 = (bf16[512,2048]{1,0:T(8,128)(2,1)S(1)}, bf16[512,2048]{1,0:T(8,128)(2,1)S(1)}, u32[]{:S(2)}, u32[]{:S(2)}) collective-permute-start(bf16[512,2048]{1,0:T(8,128)(2,1)S(1)} %add_convert_fusion.10), channel_id=1, source_target_pairs={{0,1},{1,0},{2,3},{3,2},{4,5},{5,4},{6,7},{7,6},{8,9},{9,8},{10,11... | collective-permute-start | bytes 6291464 | tf_op jit(solution)/shard_map/ppermute | solution.py:584
  638.2 92.4 %collective-permute-start.65 = (bf16[1024,1024]{1,0:T(8,128)(2,1)S(1)}, bf16[1024,1024]{1,0:T(8,128)(2,1)S(1)}, u32[]{:S(2)}, u32[]{:S(2)}) collective-permute-start(bf16[1024,1024]{1,0:T(8,128)(2,1)S(1)} %copy-done.62), channel_id=1, source_target_pairs={{0,2},{2,0},{4,6},{6,4},{8,10},{10,8},{12,14},{14,12},{16,18},{18,... | collective-permute-start | bytes 6291464 | tf_op jit(solution)/shard_map/ppermute | solution.py:580
  638.2 134.3 %collective-permute-start.67 = (bf16[1024,1024]{1,0:T(8,128)(2,1)S(1)}, bf16[1024,1024]{1,0:T(8,128)(2,1)S(1)}, u32[]{:S(2)}, u32[]{:S(2)}) collective-permute-start(bf16[1024,1024]{1,0:T(8,128)(2,1)S(1)} %add_convert_fusion.4), channel_id=1, source_target_pairs={{0,1},{1,0},{2,3},{3,2},{4,5},{5,4},{6,7},{7,6},{8,9},{9,8},{10,11... | collective-permute-start | bytes 6291464 | tf_op jit(solution)/shard_map/ppermute | solution.py:584
  775.3 526.6 %all-reduce.8.cloned.1.call-start = ((), (), s32[]{:S(2)}) async-start(), calls=%async_computation | async-start | bytes 196608 | tf_op jit(solution)/shard_map/psum | solution.py:774
  790.4 392.2 %collective-permute-start.34 = (bf16[512,1024]{1,0:T(8,128)(2,1)}, bf16[512,1024]{1,0:T(8,128)(2,1)}, u32[]{:S(2)}, u32[]{:S(2)}) collective-permute-start(bf16[512,1024]{1,0:T(8,128)(2,1)} %add_convert_fusion.18), channel_id=1, source_target_pairs={{0,0},{1,2},{2,1},{3,3},{4,4},{5,6},{6,5},{7,7},{8,8},{9,10},{10,9... | collective-permute-start | bytes 3145736 | tf_op jit(solution)/shard_map/ppermute | solution.py:593
  810.2 373.0 %collective-permute-start.40 = (bf16[512,1024]{1,0:T(8,128)(2,1)}, bf16[512,1024]{1,0:T(8,128)(2,1)S(1)}, u32[]{:S(2)}, u32[]{:S(2)}) collective-permute-start(bf16[512,1024]{1,0:T(8,128)(2,1)} %fusion.61), channel_id=1, source_target_pairs={{0,0},{1,2},{2,1},{3,3},{4,4},{5,6},{6,5},{7,7},{8,8},{9,10},{10,9... | collective-permute-start | bytes 3145736 | tf_op jit(solution)/shard_map/ppermute | solution.py:593
  1181.3 136.0 %collective-permute-start.48 = (bf16[512,1536]{1,0:T(8,128)(2,1)}, bf16[512,1536]{1,0:T(8,128)(2,1)}, u32[]{:S(2)}, u32[]{:S(2)}) collective-permute-start(bf16[512,1536]{1,0:T(8,128)(2,1)} %get-tuple-element.94), channel_id=1, source_target_pairs={{0,2},{2,0},{4,6},{6,4},{8,10},{10,8},{12,14},{14,12},{16,18},{18,... | collective-permute-start | bytes 4718600 | tf_op jit(solution)/shard_map/ppermute | solution.py:580
  1181.3 139.1 %collective-permute-start.44 = (bf16[512,1536]{1,0:T(8,128)(2,1)}, bf16[512,1536]{1,0:T(8,128)(2,1)}, u32[]{:S(2)}, u32[]{:S(2)}) collective-permute-start(bf16[512,1536]{1,0:T(8,128)(2,1)} %get-tuple-element.95), channel_id=1, source_target_pairs={{0,2},{2,0},{4,6},{6,4},{8,10},{10,8},{12,14},{14,12},{16,18},{18,... | collective-permute-start | bytes 4718600 | tf_op jit(solution)/shard_map/ppermute | solution.py:580
  1182.6 123.4 %collective-permute-start.56 = (bf16[256,1024]{1,0:T(8,128)(2,1)}, bf16[256,1024]{1,0:T(8,128)(2,1)S(1)}, u32[]{:S(2)}, u32[]{:S(2)}) collective-permute-start(bf16[256,1024]{1,0:T(8,128)(2,1)} %get-tuple-element.96), channel_id=1, source_target_pairs={{0,2},{2,0},{4,6},{6,4},{8,10},{10,8},{12,14},{14,12},{16,18},{18,... | collective-permute-start | bytes 1572872 | tf_op jit(solution)/shard_map/ppermute | solution.py:580
  1182.7 130.3 %collective-permute-start.52 = (bf16[256,1024]{1,0:T(8,128)(2,1)}, bf16[256,1024]{1,0:T(8,128)(2,1)}, u32[]{:S(2)}, u32[]{:S(2)}) collective-permute-start(bf16[256,1024]{1,0:T(8,128)(2,1)} %get-tuple-element.97), channel_id=1, source_target_pairs={{0,2},{2,0},{4,6},{6,4},{8,10},{10,8},{12,14},{14,12},{16,18},{18,... | collective-permute-start | bytes 1572872 | tf_op jit(solution)/shard_map/ppermute | solution.py:580
  1183.2 162.3 %collective-permute-start.64 = (bf16[512,2048]{1,0:T(8,128)(2,1)}, bf16[512,2048]{1,0:T(8,128)(2,1)}, u32[]{:S(2)}, u32[]{:S(2)}) collective-permute-start(bf16[512,2048]{1,0:T(8,128)(2,1)} %get-tuple-element.98), channel_id=1, source_target_pairs={{0,2},{2,0},{4,6},{6,4},{8,10},{10,8},{12,14},{14,12},{16,18},{18,... | collective-permute-start | bytes 6291464 | tf_op jit(solution)/shard_map/ppermute | solution.py:580
  (232 other events, 4124.8 us)
Sparse Core Ops, SparseCore 0:
  775.4 405.8 all-reduce.9
Sparse Core Ops, SparseCore 1:
  1182.7 119.2 all-reduce.7

commit v2 on v1

--- a/solution.py
+++ b/solution.py
@@ -1,3 +1,5 @@
+import functools
+
 import jax
 import jax.numpy as jnp
 from jax import lax
@@ -612,18 +614,414 @@
     return join_halves(place, mine, swap_dp(mine, bit))
 
 
-def add_low(left, right):
+SLOTS = 12
+STAGED = 3
+LAGS = dict(core=1, y=3, x=5, outer=7, inner=9, back=11, gather=13, whole=14, stored=15)
+VECTOR_TICKS = (1, 4, 7, 10, 13, 16, 19)
+MESH = pl.DeviceIdType.MESH
+
+
+def added(left, right):
     return (left.astype(jnp.float32) + right.astype(jnp.float32)).astype(jnp.bfloat16)
 
 
-def reduce_grad(own, other, core):
-    own_kept = add_low(half_of(own, core), swap_dp(half_of(own, 1 - core), CORE_BIT))
-    other_kept = add_low(half_of(other, core), swap_dp(half_of(other, 1 - core), CORE_BIT))
-    mine = add_low(own_kept, swap_y(other_kept))
-    count = lax.axis_size("dp")
-    groups = [[i for i in range(count) if i % 2 == member] for member in range(2)]
-    summed = lax.psum(mine, "dp", axis_index_groups=groups)
-    return join_halves(core, summed, swap_dp(summed, CORE_BIT)).astype(jnp.float32)
+def reduce_kernel(plan, block, *refs):
+    count = len(plan)
+    chunks = sum(rows * columns for _, rows, columns in plan)
+    operand_refs = refs[: 3 * count]
+    vector_ref = refs[3 * count]
+    out_refs = refs[3 * count + 1 : 4 * count + 1]
+    vector_out = refs[4 * count + 1]
+    (
+        pair_buf,
+        one_buf,
+        part_buf,
+        core_in,
+        own_kept,
+        other_kept,
+        y_in,
+        x_kept,
+        x_out,
+        x_in,
+        z_kept,
+        outer_in,
+        inner_in,
+        result,
+        vec_in,
+        staged_sem,
+        send_sems,
+        recv_sems,
+        store_sem,
+        vec_send,
+        vec_recv,
+    ) = refs[4 * count + 2 :]
+    half, quarter = block // 2, block // 4
+    place = lax.axis_index("dp")
+    y = lax.axis_index("tensor")
+    core = place % 2
+    x = (place // 2) % 2
+    z = place // 4
+    z_low = z % 2
+    inner = (z + 1) // 2 % 2
+    core_partner = {"dp": place + 1 - 2 * core, "tensor": y}
+    x_partner = {"dp": place + 2 - 4 * x, "tensor": y}
+    y_partner = {"dp": place, "tensor": 1 - y}
+    z_partner = {"dp": place + 4 - 8 * z_low, "tensor": y}
+    middle_partner = {"dp": place + 4 * (3 - 2 * z), "tensor": y}
+
+    barrier = pltpu.get_barrier_semaphore()
+    for partner in (core_partner, x_partner, y_partner, z_partner):
+        pl.semaphore_signal(barrier, inc=1, device_id=partner, device_id_type=MESH)
+
+    @pl.when(inner == 1)
+    def _():
+        pl.semaphore_signal(barrier, inc=1, device_id=middle_partner, device_id_type=MESH)
+        pl.semaphore_wait(barrier, 5)
+
+    @pl.when(inner == 0)
+    def _():
+        pl.semaphore_wait(barrier, 4)
+
+    starts = []
+    total = 0
+    for _, rows, columns in plan:
+        starts.append(total)
+        total += rows * columns
+
+    def for_matrix(chunk, action):
+        for member, (kind, rows, columns) in enumerate(plan):
+
+            @pl.when((chunk >= starts[member]) & (chunk < starts[member] + rows * columns))
+            def _(member=member, kind=kind, columns=columns):
+                local = chunk - starts[member]
+                action(member, kind, local // columns, local % columns)
+
+    def cut(ref, column):
+        return ref.at[:, pl.ds(pl.multiple_of(column * block, block), block)]
+
+    def staged_copies(chunk, shared, own, other):
+        slot = chunk % STAGED
+        return (
+            pltpu.make_async_copy(own, pair_buf.at[slot, 0], staged_sem.at[slot, 0]),
+            pltpu.make_async_copy(other, pair_buf.at[slot, 1], staged_sem.at[slot, 1]),
+            pltpu.make_async_copy(shared, one_buf.at[slot], staged_sem.at[slot, 2]),
+        )
+
+    def stage_operands(chunk):
+        def action(member, kind, i, j):
+            shared, own, other = operand_refs[3 * member : 3 * member + 3]
+            split, single = (i, j) if kind == "rows" else (j, i)
+            for copy in staged_copies(
+                chunk, cut(shared, single), cut(own, split), cut(other, split)
+            ):
+                copy.start()
+
+        for_matrix(chunk, action)
+
+    def wait_operands(chunk):
+        slot = chunk % STAGED
+        for copy in staged_copies(chunk, one_buf.at[slot], pair_buf.at[slot, 0], pair_buf.at[slot, 1]):
+            copy.wait()
+
+    def remote(step, chunk, source, target, partner):
+        slot = chunk % SLOTS
+        return pltpu.make_async_remote_copy(
+            src_ref=source,
+            dst_ref=target,
+            send_sem=send_sems.at[step, slot],
+            recv_sem=recv_sems.at[step, slot],
+            device_id=partner,
+            device_id_type=MESH,
+        )
+
+    def rows_at(index, size):
+        return pl.ds(pl.multiple_of(index * size, size), size)
+
+    def core_copy(chunk):
+        return remote(
+            0,
+            chunk,
+            part_buf.at[chunk % STAGED, :, rows_at(1 - core, half)],
+            core_in.at[chunk % SLOTS],
+            core_partner,
+        )
+
+    def y_copy(chunk):
+        slot = chunk % SLOTS
+        return remote(1, chunk, other_kept.at[slot], y_in.at[slot], y_partner)
+
+    def x_copy(chunk):
+        slot = chunk % SLOTS
+        return remote(2, chunk, x_out.at[slot], x_in.at[slot], x_partner)
+
+    def outer_copy(chunk):
+        slot = chunk % SLOTS
+        return remote(3, chunk, z_kept.at[slot], outer_in.at[slot], z_partner)
+
+    def inner_copy(chunk):
+        slot = chunk % SLOTS
+        return remote(4, chunk, z_kept.at[slot], inner_in.at[slot], middle_partner)
+
+    own_rows = rows_at(2 * core + x, quarter)
+
+    def back_copy(chunk):
+        piece = result.at[chunk % SLOTS, own_rows]
+        return remote(5, chunk, piece, piece, z_partner)
+
+    def gather_copy(chunk):
+        piece = result.at[chunk % SLOTS, own_rows]
+        return remote(6, chunk, piece, piece, x_partner)
+
+    def whole_copy(chunk):
+        piece = result.at[chunk % SLOTS, rows_at(core, half)]
+        return remote(7, chunk, piece, piece, core_partner)
+
+    def store_copy(chunk, target):
+        slot = chunk % SLOTS
+        return pltpu.make_async_copy(result.at[slot], target, store_sem.at[slot])
+
+    def multiply(chunk):
+        slot = chunk % STAGED
+        wait_operands(chunk)
+
+        def action(member, kind, i, j):
+            single = one_buf[slot]
+            for which in range(2):
+                split = pair_buf[slot, which]
+                product = dot_tn(split, single) if kind == "rows" else dot_tn(single, split)
+                part_buf[slot, which] = product.astype(jnp.bfloat16)
+
+        kinds = {}
+        for member, (kind, rows, columns) in enumerate(plan):
+            inside = (chunk >= starts[member]) & (chunk < starts[member] + rows * columns)
+            kinds[kind] = kinds[kind] | inside if kind in kinds else inside
+        for kind, inside in kinds.items():
+
+            @pl.when(inside)
+            def _(kind=kind):
+                action(None, kind, None, None)
+
+        core_copy(chunk).start()
+
+    def after_core(chunk):
+        slot = chunk % SLOTS
+        core_copy(chunk).wait()
+        mine = rows_at(core, half)
+        other_kept[slot] = added(part_buf[chunk % STAGED, 1, mine, :], core_in[slot, 1])
+        y_copy(chunk).start()
+        own_kept[slot] = added(part_buf[chunk % STAGED, 0, mine, :], core_in[slot, 0])
+
+    def after_y(chunk):
+        slot = chunk % SLOTS
+        y_copy(chunk).wait()
+        away, here = rows_at(1 - x, quarter), rows_at(x, quarter)
+        x_out[slot] = added(own_kept[slot, away, :], y_in[slot, away, :])
+        x_copy(chunk).start()
+        x_kept[slot] = added(own_kept[slot, here, :], y_in[slot, here, :])
+
+    def after_x(chunk):
+        slot = chunk % SLOTS
+        x_copy(chunk).wait()
+        z_kept[slot] = added(x_kept[slot], x_in[slot])
+
+        @pl.when(inner == 0)
+        def _():
+            outer_copy(chunk).start()
+
+    def after_outer(chunk):
+        slot = chunk % SLOTS
+
+        @pl.when(inner == 0)
+        def _():
+            outer_copy(chunk).wait_send()
+
+        @pl.when(inner == 1)
+        def _():
+            outer_copy(chunk).wait_recv()
+            z_kept[slot] = added(z_kept[slot], outer_in[slot])
+            inner_copy(chunk).start()
+
+    def after_inner(chunk):
+        slot = chunk % SLOTS
+
+        @pl.when(inner == 1)
+        def _():
+            inner_copy(chunk).wait()
+            result[slot, own_rows, :] = added(z_kept[slot], inner_in[slot])
+            back_copy(chunk).start()
+
+    def after_back(chunk):
+        @pl.when(inner == 0)
+        def _():
+            back_copy(chunk).wait_recv()
+
+        @pl.when(inner == 1)
+        def _():
+            back_copy(chunk).wait_send()
+
+        gather_copy(chunk).start()
+
+    def after_gather(chunk):
+        gather_copy(chunk).wait()
+        whole_copy(chunk).start()
+
+    def after_whole(chunk):
+        whole_copy(chunk).wait()
+
+        def action(member, kind, i, j):
+            store_copy(chunk, out_refs[member].at[rows_at(i, block), rows_at(j, block)]).start()
+
+        for_matrix(chunk, action)
+
+    def after_store(chunk):
+        store_copy(chunk, result.at[chunk % SLOTS]).wait()
+
+    vector_partners = (core_partner, y_partner, x_partner, z_partner, middle_partner, z_partner)
+
+    def vector_copy(step):
+        target = vector_out if step == 5 else vec_in.at[step]
+        return pltpu.make_async_remote_copy(
+            src_ref=vector_out,
+            dst_ref=target,
+            send_sem=vec_send.at[step],
+            recv_sem=vec_recv.at[step],
+            device_id=vector_partners[step],
+            device_id_type=MESH,
+        )
+
+    def add_vector(step):
+        vector_out[...] = vector_out[...] + vec_in[step]
+
+    def vector_tick(step):
+        if step == 0:
+            vector_out[...] = vector_ref[...]
+            vector_copy(0).start()
+        elif step <= 3:
+            vector_copy(step - 1).wait()
+            add_vector(step - 1)
+            if step < 3:
+                vector_copy(step).start()
+            else:
+
+                @pl.when(inner == 0)
+                def _():
+                    vector_copy(3).start()
+
+        elif step == 4:
+
+            @pl.when(inner == 0)
+            def _():
+                vector_copy(3).wait_send()
+
+            @pl.when(inner == 1)
+            def _():
+                vector_copy(3).wait_recv()
+                add_vector(3)
+                vector_copy(4).start()
+
+        elif step == 5:
+
+            @pl.when(inner == 1)
+            def _():
+                vector_copy(4).wait()
+                add_vector(4)
+                vector_copy(5).start()
+
+        else:
+
+            @pl.when(inner == 1)
+            def _():
+                vector_copy(5).wait_send()
+
+            @pl.when(inner == 0)
+            def _():
+                vector_copy(5).wait_recv()
+
+    stages = (
+        (LAGS["core"], after_core),
+        (0, multiply),
+        (LAGS["y"], after_y),
+        (LAGS["x"], after_x),
+        (LAGS["outer"], after_outer),
+        (LAGS["inner"], after_inner),
+        (LAGS["back"], after_back),
+        (LAGS["gather"], after_gather),
+        (LAGS["stored"], after_store),
+        (LAGS["whole"], after_whole),
+    )
+
+    stage_operands(0)
+
+    def tick(t, carry):
+        @pl.when(t + 1 < chunks)
+        def _():
+            stage_operands(t + 1)
+
+        for lag, action in stages:
+            chunk = t - lag
+
+            @pl.when((chunk >= 0) & (chunk < chunks))
+            def _(chunk=chunk, action=action):
+                action(chunk)
+
+        for step, when in enumerate(VECTOR_TICKS):
+
+            @pl.when(t == when)
+            def _(step=step):
+                vector_tick(step)
+
+        return carry
+
+    lax.fori_loop(0, max(chunks + LAGS["stored"], VECTOR_TICKS[-1] + 1), tick, 0)
+
+
+def reduce_grads(plan, operands, vector, block):
+    half, quarter = block // 2, block // 4
+    kept = operands[0][0].shape[0]
+    low = jnp.bfloat16
+    shapes = [jax.ShapeDtypeStruct((rows * block, columns * block), low) for _, rows, columns in plan]
+    shapes.append(jax.ShapeDtypeStruct(vector.shape, jnp.float32))
+    anywhere = pl.BlockSpec(memory_space=pl.ANY)
+    in_vmem = pl.BlockSpec(memory_space=pltpu.VMEM)
+    chunks = sum(rows * columns for _, rows, columns in plan)
+    return pl.pallas_call(
+        functools.partial(reduce_kernel, plan, block),
+        in_specs=[anywhere] * (3 * len(plan)) + [in_vmem],
+        out_specs=[anywhere] * len(plan) + [in_vmem],
+        out_shape=shapes,
+        scratch_shapes=[
+            pltpu.VMEM((STAGED, 2, kept, block), low),
+            pltpu.VMEM((STAGED, kept, block), low),
+            pltpu.VMEM((STAGED, 2, block, block), low),
+            pltpu.VMEM((SLOTS, 2, half, block), low),
+            pltpu.VMEM((SLOTS, half, block), low),
+            pltpu.VMEM((SLOTS, half, block), low),
+            pltpu.VMEM((SLOTS, half, block), low),
+            pltpu.VMEM((SLOTS, quarter, block), low),
+            pltpu.VMEM((SLOTS, quarter, block), low),
+            pltpu.VMEM((SLOTS, quarter, block), low),
+            pltpu.VMEM((SLOTS, quarter, block), low),
+            pltpu.VMEM((SLOTS, quarter, block), low),
+            pltpu.VMEM((SLOTS, quarter, block), low),
+            pltpu.VMEM((SLOTS, block, block), low),
+            pltpu.VMEM((5,) + vector.shape, jnp.float32),
+            pltpu.SemaphoreType.DMA((STAGED, 3)),
+            pltpu.SemaphoreType.DMA((8, SLOTS)),
+            pltpu.SemaphoreType.DMA((8, SLOTS)),
+            pltpu.SemaphoreType.DMA((SLOTS,)),
+            pltpu.SemaphoreType.DMA((6,)),
+            pltpu.SemaphoreType.DMA((6,)),
+        ],
+        compiler_params=pltpu.CompilerParams(
+            collective_id=0, has_side_effects=True, vmem_limit_bytes=VMEM_ASKED
+        ),
+        cost_estimate=pl.CostEstimate(
+            flops=4 * chunks * block * block * kept,
+            bytes_accessed=chunks * block * (3 * kept + block) * 2,
+            transcendentals=0,
+        ),
+        name="reduce_grads",
+    )(*[member for triple in operands for member in triple], vector)
 
 
 def dot_low(left, right):
@@ -707,7 +1105,7 @@
     out_act = swap_windows(residual.astype(jnp.bfloat16))
 
     grad_residual = grad_residual.astype(jnp.float32)
-    grads = [None] * layers
+    triples = []
     vectors = [None] * layers
     for l in reversed(range(layers)):
         qkv, out_w, up, down, qv, upb = weights[l]
@@ -720,8 +1118,8 @@
             grad_before = (dot_nt(grad_branch, down[half]) * slope.astype(jnp.float32)).astype(
                 jnp.bfloat16
             )
-            grad_down.append(dot_tn(activated, grad_branch).astype(jnp.bfloat16))
-            grad_up.append(dot_tn(normed_two, grad_before).astype(jnp.bfloat16))
+            grad_down.append(activated)
+            grad_up.append(grad_before)
             grad_up_bias.append(jnp.sum(grad_before, axis=0, dtype=jnp.float32))
             incoming = incoming + dot_nt(grad_before, up[half])
         _, unit, inverse = layer_norm(middle, ln_gain[l, 1], ln_bias[l, 1])
@@ -732,7 +1130,7 @@
         incoming = 0.0
         for half in range(2):
             projected, halo, attended, totals = saved_attention[half]
-            grad_out.append(dot_tn(attended, grad_attn).astype(jnp.bfloat16))
+            grad_out.append(attended)
             grad_attended = dot_nt(grad_attn, out_w[half]).astype(jnp.bfloat16)
             dq, dk, dv, dkh, dvh = attention_backward(
                 projected, halo, segq, segk, grad_attended, totals
@@ -748,15 +1146,18 @@
                 ],
                 axis=1,
             )
-            grad_qkv.append(dot_tn(normed, grad_projected).astype(jnp.bfloat16))
+            grad_qkv.append(grad_projected)
             sums = jnp.sum(grad_projected, axis=0, dtype=jnp.float32)
             grad_qv.append(jnp.stack([sums[:third], sums[2 * third :]]))
             incoming = incoming + dot_nt(grad_projected, qkv[half])
         _, unit, inverse = layer_norm(residual, ln_gain[l, 0], ln_bias[l, 0])
         through, gain_one, shift_one = norm_backward(incoming, unit, inverse, ln_gain[l, 0])
-        grads[l] = tuple(
-            reduce_grad(pair[0], pair[1], core) for pair in (grad_qkv, grad_out, grad_up, grad_down)
-        )
+        triples += [
+            (grad_branch, *grad_down),
+            (normed_two, *grad_up),
+            (grad_attn, *grad_out),
+            (normed, *grad_qkv),
+        ]
         vectors[l] = jnp.concatenate(
             [
                 natural(grad_qv[0].T, grad_qv[1].T).T.reshape(-1),
@@ -771,7 +1172,15 @@
         )
         grad_residual = grad_middle + through
     grad_in = swap_windows(grad_residual.astype(jnp.bfloat16))
-    summed = lax.psum(jnp.stack(vectors), ("dp", "tensor"))
+    block = width // 2
+    plan = []
+    for shared, own, _ in triples:
+        by_rows = shared is not None and len(plan) % 2 == 0
+        split, single = own.shape[1] // block, shared.shape[1] // block
+        plan.append(("rows", split, single) if by_rows else ("columns", single, split))
+    vector = jnp.stack(vectors)
+    *reduced, summed = reduce_grads(tuple(plan), triples, vector.reshape(-1, LANES), block)
+    summed = summed.reshape(vector.shape)
     hidden = 2 * up_bias.shape[1]
     ends = [2 * width, 2 * width + hidden, 4 * width + hidden, 6 * width + hidden]
     qv_sum = summed[:, : ends[0]].reshape(layers, 2, width)
@@ -779,7 +1188,12 @@
     grad_up_bias = lax.dynamic_slice_in_dim(
         summed[:, ends[0] : ends[1]], y * (hidden // 2), hidden // 2, axis=1
     )
-    stacked = [jnp.stack([grads[l][member] for l in range(layers)]) for member in range(4)]
+    stacked = [
+        jnp.stack(
+            [reduced[4 * (layers - 1 - l) + 3 - member] for l in range(layers)]
+        ).astype(jnp.float32)
+        for member in range(4)
+    ]
     return (
         out_act,
         grad_in,

time: 1410 us -> 886 us (0.63)
  waiting for transfers between devices: 797 us -> 107 us
  Pallas kernels: 81.9 us -> 396 us
  other arithmetic: 138 us -> 79.8 us
  matrix products: 181 us -> 140 us
  local copies, waits for them, and re-layouts: 108 us -> 88.5 us
  between operations: 18.9 us -> 3.18 us
    psum x2 -> x0, waiting for transfers between devices: 487 us -> none  [the longest x1 368 us: reduce_grad(): summed = lax.psum(mine, 'dp', axis_index_groups=groups)]
    pallas_call x0 -> x1, Pallas kernels: none -> 314 us  [reduce_grads(): pl.pallas_call(functools.partial(reduce_kernel, plan, block), in_specs=[a...]
    ppermute x20 -> x12, waiting for transfers between devices: 253 us -> 36.8 us  [swap_y(): return lax.ppermute(array, 'tensor', [(0, 1), (1, 0)])]
    dot_general x16 -> x0, matrix products: 47 us -> none  [dot_tn(): lax.dot_general(left, right, (((0,), (0,)), ((), ())), preferred_element_...]
    another operation x5 -> x1, other arithmetic: 28.8 us -> 0.09 us  [local_split(): vector = jnp.stack(vectors)]
    select_n x15 -> x8, other arithmetic: 50.7 us -> 24 us  [join_halves(): jnp.where(bit == 0, jnp.concatenate([mine, other], axis=0), jnp.concatena...]
    dynamic_slice x24 -> x8, local copies, waits for them, and re-layouts: 34.5 us -> 17 us  [half_of(): return lax.dynamic_slice_in_dim(array, bit * rows, rows, axis=0)]
    ppermute x41 -> x17, starting transfers between devices: 24.1 us -> 9.76 us  [swap_dp(): return lax.ppermute(array, 'dp', [(i, i ^ bit) for i in range(count)])]
  transfers between devices with their start and end apart: 75 -> 41, of which waited for: 16 -> 11; matrix products, arithmetic and copies ran while one was open for 25% -> 30% of each run, Pallas kernels for 5% -> 44%
where the time goes in v2:
time: 886 us; the launch traced here: 875 us
  Pallas kernels  396 us (45%)
  matrix products  140 us (16%)
  waiting for transfers between devices  107 us (12%)
  local copies, waits for them, and re-layouts  88.5 us (10%)
  other arithmetic  79.8 us (9%)
  starting transfers between devices  60.4 us (7%)
    pallas_call x1, Pallas kernels, reduce_grads(): pl.pallas_call(functools.partial(reduce_kernel, plan, block), in_specs=[a...  314 us
    dot_general x16, matrix products, dot_nt(): lax.dot_general(left, right, (((1,), (1,)), ((), ())), preferred_element_...  76.9 us
    ppermute x17, waiting for transfers between devices, swap_dp(): return lax.ppermute(array, 'dp', [(i, i ^ bit) for i in range(count)])  69.3 us
    dot_general x16, matrix products, dot_low(): return jnp.dot(left, right, preferred_element_type=jnp.float32)  63.1 us
    pallas_call x4, Pallas kernels, attention_backward(): pl.pallas_call(attention_backward_kernel, grid=(pairs,), in_specs=attenti...  49.6 us
    ppermute x12, waiting for transfers between devices, swap_y(): return lax.ppermute(array, 'tensor', [(0, 1), (1, 0)])  36.8 us
    unnamed x216, local copies, waits for them, and re-layouts  35.3 us
    pallas_call x4, Pallas kernels, attention_forward(): pl.pallas_call(attention_forward_kernel, grid=(pairs,), in_specs=attentio...  32.6 us
  transfers between devices with their start and end apart: 41, of which 11 were waited for; matrix products, arithmetic and copies ran while one was open for 30% of the time, Pallas kernels for 44%

profile of v2, /device:TPU:0, one launch (start us, length us, event | category | flops | bytes accessed | tf_op | source)
XLA Modules:
  0.0 874.9 jit_solution(11992853728241174790)
XLA Ops:
  0.7 6.2 fusion.120
  16.6 6.3 fusion.121
  58.7 16.4 %collective-permute-done.3 = bf16[256,1536]{0,1:T(8,128)(2,1)S(1)} collective-permute-done((bf16[256,1536]{0,1:T(8,128)(2,1)S(1)}, bf16[256,1536]{0,1:T(8,128)(2,1)S(1)}, u32[]{:S(2)}, u32[]{:S(2)}) %collective-permute-start.3) | collective-permute-done | bytes 786464 | tf_op jit(solution)/shard_map/ppermute | solution.py:586
  84.9 10.2 %collective-permute-done.4 = bf16[256,1536]{0,1:T(8,128)(2,1)S(1)} collective-permute-done((bf16[256,1536]{0,1:T(8,128)(2,1)S(1)}, bf16[256,1536]{0,1:T(8,128)(2,1)S(1)}, u32[]{:S(2)}, u32[]{:S(2)}) %collective-permute-start.4) | collective-permute-done | bytes 786464 | tf_op jit(solution)/shard_map/ppermute | solution.py:582
  97.2 10.5 %collective-permute-done.24 = bf16[128,1024]{1,0:T(8,128)(2,1)S(1)} collective-permute-done((bf16[128,1024]{1,0:T(8,128)(2,1)S(1)}, bf16[128,1024]{1,0:T(8,128)(2,1)S(1)}, u32[]{:S(2)}, u32[]{:S(2)}) %collective-permute-start.24) | collective-permute-done | bytes 262176 | tf_op jit(solution)/shard_map/ppermute | solution.py:586
  131.3 8.1 attention_forward.4
  151.3 18.1 %collective-permute-done.16 = bf16[512,1024]{1,0:T(8,128)(2,1)S(1)} collective-permute-done((bf16[512,1024]{1,0:T(8,128)(2,1)}, bf16[512,1024]{1,0:T(8,128)(2,1)S(1)}, u32[]{:S(2)}, u32[]{:S(2)}) %collective-permute-start.16) | collective-permute-done | bytes 1048608 | tf_op jit(solution)/shard_map/ppermute | solution.py:582
  173.3 15.5 %collective-permute-done.12 = bf16[256,2048]{1,0:T(8,128)(2,1)S(1)} collective-permute-done((bf16[256,2048]{1,0:T(8,128)(2,1)}, bf16[256,2048]{1,0:T(8,128)(2,1)S(1)}, u32[]{:S(2)}, u32[]{:S(2)}) %collective-permute-start.12) | collective-permute-done | bytes 1048608 | tf_op jit(solution)/shard_map/ppermute | solution.py:582
  193.6 8.3 attention_forward.5
  218.5 7.3 multiply_convert_fusion.5
  225.9 6.3 fusion.136
  242.0 22.7 %collective-permute-done.32 = bf16[512,1024]{1,0:T(8,128)(2,1)S(1)} collective-permute-done((bf16[512,1024]{1,0:T(8,128)(2,1)}, bf16[512,1024]{1,0:T(8,128)(2,1)S(1)}, u32[]{:S(2)}, u32[]{:S(2)}) %collective-permute-start.32) | collective-permute-done | bytes 1048608 | tf_op jit(solution)/shard_map/ppermute | solution.py:582
  270.1 9.4 %collective-permute-start.35 = (bf16[512,1024]{1,0:T(8,128)(2,1)}, bf16[512,1024]{1,0:T(8,128)(2,1)}, u32[]{:S(2)}, u32[]{:S(2)}) collective-permute-start(bf16[512,1024]{1,0:T(8,128)(2,1)} %param.23), channel_id=1, source_target_pairs={{0,0},{1,2},{2,1},{3,3},{4,4},{5,6},{6,5},{7,7},{8,8},{9,10},{10,9... | collective-permute-start | bytes 3145736 | tf_op jit(solution)/shard_map/ppermute | solution.py:595
  284.1 8.2 attention_forward.6
  293.1 8.0 attention_forward.7
  319.1 7.0 multiply_convert_fusion.3
  326.1 9.5 %convert_reduce_fusion = (f32[2048]{0:T(1024)S(1)}, bf16[512,2048]{1,0:T(8,128)(2,1)S(1)}) fusion(f32[512,2048]{1,0:T(8,128)S(1)} %get-tuple-element.201, f32[2048]{0:T(1024)S(1)} %collective-permute-done.30, bf16[512,1024]{1,0:T(8,128)(2,1)} %collective-permute-done.35.refs_0_, bf16[1024,1024]{1,0:T(8,128)(2,1)} %collective-permute-done.33, ...), kind=kOutput, calls=%fused_computation.57 | convolution fusion | flops 2191521792 | bytes 11550721 | tf_op jit(solution)/shard_map/dot_general | solution.py:378
  335.6 8.0 multiply_reduce_fusion
  348.7 12.4 %attention_backward.4 = (bf16[512,512]{1,0:T(8,128)(2,1)}, f32[512,512]{1,0:T(8,128)}, f32[512,512]{1,0:T(8,128)}, bf16[256,512]{1,0:T(8,128)(2,1)}, bf16[256,512]{1,0:T(8,128)(2,1)}) custom-call(bf16[512,1536]{1,0:T(8,128)(2,1)} %copy-done.3, bf16[512,1536]{1,0:T(8,128)(2,1)} %copy-done.3, bf16[512,1536]{1,0:T(8,128)(2,1)} %copy-done.3, ...), custom_call_target="tpu_custom_call" | custom-call | flops 1342177280 | bytes 5242880 | tf_op jit(solution)/shard_map/attention_backward/pallas_call | solution.py:552
  367.8 12.3 %attention_backward.5 = (bf16[512,512]{1,0:T(8,128)(2,1)}, f32[512,512]{1,0:T(8,128)}, f32[512,512]{1,0:T(8,128)}, bf16[256,512]{1,0:T(8,128)(2,1)}, bf16[256,512]{1,0:T(8,128)(2,1)}) custom-call(bf16[512,1536]{1,0:T(8,128)(2,1)} %copy-done.2, bf16[512,1536]{1,0:T(8,128)(2,1)} %copy-done.2, bf16[512,1536]{1,0:T(8,128)(2,1)} %copy-done.2, ...), custom_call_target="tpu_custom_call" | custom-call | flops 1342177280 | bytes 5242880 | tf_op jit(solution)/shard_map/attention_backward/pallas_call | solution.py:552
  387.8 6.9 add_convert_fusion
  394.7 9.6 %collective-permute-start.34 = (bf16[512,1024]{1,0:T(8,128)(2,1)}, bf16[512,1024]{1,0:T(8,128)(2,1)}, u32[]{:S(2)}, u32[]{:S(2)}) collective-permute-start(bf16[512,1024]{1,0:T(8,128)(2,1)} %add_convert_fusion), channel_id=1, source_target_pairs={{0,0},{1,2},{2,1},{3,3},{4,4},{5,6},{6,5},{7,7},{8,8},{9,10},{10,9... | collective-permute-start | bytes 3145736 | tf_op jit(solution)/shard_map/ppermute | solution.py:595
  415.7 7.4 convert_reduce_fusion.3
  425.6 10.2 %convert_reduce_fusion.2 = (f32[2048]{0:T(1024)S(1)}, bf16[512,2048]{1,0:T(8,128)(2,1)S(1)}) fusion(f32[512,2048]{1,0:T(8,128)} %get-tuple-element.193, f32[2048]{0:T(1024)S(1)} %collective-permute-done.14, bf16[512,1024]{1,0:T(8,128)(2,1)S(1)} %get-tuple-element.113.refs_12_, bf16[1024,1024]{1,0:T(8,128)(2,1)S(1)} %copy-done.74, ...), kind=kOutput, calls=%fused_computation.59 | convolution fusion | flops 2191521792 | bytes 11550721 | tf_op jit(solution)/shard_map/dot_general | solution.py:378
  435.8 8.1 multiply_reduce_fusion.2
  447.6 12.4 %attention_backward.6 = (bf16[512,512]{1,0:T(8,128)(2,1)}, f32[512,512]{1,0:T(8,128)}, f32[512,512]{1,0:T(8,128)}, bf16[256,512]{1,0:T(8,128)(2,1)}, bf16[256,512]{1,0:T(8,128)(2,1)}) custom-call(bf16[512,1536]{1,0:T(8,128)(2,1)} %copy-done, bf16[512,1536]{1,0:T(8,128)(2,1)} %copy-done, bf16[512,1536]{1,0:T(8,128)(2,1)} %copy-done, ...), custom_call_target="tpu_custom_call" | custom-call | flops 1342177280 | bytes 5242880 | tf_op jit(solution)/shard_map/attention_backward/pallas_call | solution.py:552
  464.0 12.5 %attention_backward.7 = (bf16[512,512]{1,0:T(8,128)(2,1)}, f32[512,512]{1,0:T(8,128)}, f32[512,512]{1,0:T(8,128)}, bf16[256,512]{1,0:T(8,128)(2,1)}, bf16[256,512]{1,0:T(8,128)(2,1)}) custom-call(bf16[512,1536]{1,0:T(8,128)(2,1)} %copy-done.1, bf16[512,1536]{1,0:T(8,128)(2,1)} %copy-done.1, bf16[512,1536]{1,0:T(8,128)(2,1)} %copy-done.1, ...), custom_call_target="tpu_custom_call" | custom-call | flops 1342177280 | bytes 5242880 | tf_op jit(solution)/shard_map/attention_backward/pallas_call | solution.py:552
  493.0 314.2 %reduce_grads.1 = (bf16[2048,1024]{1,0:T(8,128)(2,1)}, bf16[1024,2048]{1,0:T(8,128)(2,1)}, bf16[512,1024]{1,0:T(8,128)(2,1)}, bf16[1024,1536]{1,0:T(8,128)(2,1)}...) custom-call(bf16[512,1024]{1,0:T(8,128)(2,1)} %collective-permute-do, ...), custom_call_target="tpu_custom_call" | custom-call | flops 25769803776 | bytes 100663296 | tf_op jit(solution)/shard_map/reduce_grads/pallas_call | solution.py:987
  817.5 8.4 maximum_convert_fusion.2
  825.9 12.8 %copy.37 = f32[2,1024,3,512]{3,1,2,0:T(8,128)} copy(f32[2,1024,3,512]{1,3,2,0:T(8,128)} %maximum_convert_fusion.2) | data formatting | bytes 25165824
  846.0 10.8 %maximum_convert_fusion.1 = f32[2,2048,1024]{2,1,0:T(8,128)} fusion(bf16[1,2048,1024]{2,1,0:T(8,128)(2,1)} %bitcast.184, bf16[1,2048,1024]{2,1,0:T(8,128)(2,1)} %bitcast.185), kind=kLoop, calls=%fused_computation.1 | loop fusion | flops 8388608 | bytes 25165824 | tf_op jit(solution)/shard_map/convert_element_type | solution.py:1194
  861.7 9.4 %maximum_convert_fusion = f32[2,1024,2048]{2,1,0:T(8,128)} fusion(bf16[1,1024,2048]{2,1,0:T(8,128)(2,1)S(1)} %bitcast.182, bf16[1,1024,2048]{2,1,0:T(8,128)(2,1)} %bitcast.183), kind=kLoop, calls=%fused_computation | loop fusion | flops 8388608 | bytes 25165824 | tf_op jit(solution)/shard_map/convert_element_type | solution.py:1194
  (428 shorter events, 238.4 us)
Async XLA Ops:
  9.3 130.0 %collective-permute-start.11 = (bf16[256,2048]{1,0:T(8,128)(2,1)}, bf16[256,2048]{1,0:T(8,128)(2,1)}, u32[]{:S(2)}, u32[]{:S(2)}) collective-permute-start(bf16[256,2048]{1,0:T(8,128)(2,1)} %dynamic-slice_bitcast_fusion.3), channel_id=1, source_target_pairs={{0,1},{1,0},{2,3},{3,2},{4,5},{5,4},{6,7},{7,6},{8,9},{9,8},{10,11... | collective-permute-start | bytes 3145736 | tf_op jit(solution)/shard_map/ppermute | solution.py:586
  12.3 44.5 %collective-permute-start.2 = (s32[1,1024]{1,0:T(1,128)S(1)}, s32[1,1024]{1,0:T(1,128)S(1)}, u32[]{:S(2)}, u32[]{:S(2)}) collective-permute-start(s32[1,1024]{1,0:T(1,128)S(1)} %copy-done.72), channel_id=1, source_target_pairs={{0,2},{2,0},{4,6},{6,4},{8,10},{10,8},{12,14},{14,12},{16,18},{18,... | collective-permute-start | bytes 12296 | tf_op jit(solution)/shard_map/ppermute | solution.py:582
  12.3 70.4 %collective-permute-start = (bf16[512,1024]{1,0:T(8,128)(2,1)}, bf16[512,1024]{1,0:T(8,128)(2,1)S(1)}, u32[]{:S(2)}, u32[]{:S(2)}) collective-permute-start(bf16[512,1024]{1,0:T(8,128)(2,1)} %param.12), channel_id=1, source_target_pairs={{0,0},{1,2},{2,1},{3,3},{4,4},{5,6},{6,5},{7,7},{8,8},{9,10},{10,9... | collective-permute-start | bytes 3145736 | tf_op jit(solution)/shard_map/ppermute | solution.py:595
  14.2 40.4 %collective-permute-start.22 = (f32[1024]{0:T(1024)S(1)}, f32[1024]{0:T(1024)S(1)}, u32[]{:S(2)}, u32[]{:S(2)}) collective-permute-start(f32[1024]{0:T(1024)S(1)} %bitcast.227), channel_id=1, source_target_pairs={{0,1},{1,0},{2,3},{3,2},{4,5},{5,4},{6,7},{7,6},{8,9},{9,8},{10,11... | collective-permute-start | bytes 12296 | tf_op jit(solution)/shard_map/ppermute | solution.py:586
  16.5 40.2 %collective-permute-start.6 = (f32[1024]{0:T(1024)S(1)}, f32[1024]{0:T(1024)S(1)}, u32[]{:S(2)}, u32[]{:S(2)}) collective-permute-start(f32[1024]{0:T(1024)S(1)} %bitcast.226), channel_id=1, source_target_pairs={{0,1},{1,0},{2,3},{3,2},{4,5},{5,4},{6,7},{7,6},{8,9},{9,8},{10,11... | collective-permute-start | bytes 12296 | tf_op jit(solution)/shard_map/ppermute | solution.py:586
  56.7 24.1 %collective-permute-start.8 = (bf16[128,1024]{1,0:T(8,128)(2,1)S(1)}, bf16[128,1024]{1,0:T(8,128)(2,1)S(1)}, u32[]{:S(2)}, u32[]{:S(2)}) collective-permute-start(bf16[128,1024]{1,0:T(8,128)(2,1)S(1)} %dynamic-slice_bitcast_fusion.5), channel_id=1, source_target_pairs={{0,1},{1,0},{2,3},{3,2},{4,5},{5,4},{6,7},{7,6},{8,9},{9,8},{10,11... | collective-permute-start | bytes 786440 | tf_op jit(solution)/shard_map/ppermute | solution.py:586
  56.8 70.5 %collective-permute-start.15 = (bf16[512,1024]{1,0:T(8,128)(2,1)}, bf16[512,1024]{1,0:T(8,128)(2,1)}, u32[]{:S(2)}, u32[]{:S(2)}) collective-permute-start(bf16[512,1024]{1,0:T(8,128)(2,1)} %dynamic-slice_bitcast_fusion.2), channel_id=1, source_target_pairs={{0,1},{1,0},{2,3},{3,2},{4,5},{5,4},{6,7},{7,6},{8,9},{9,8},{10,11... | collective-permute-start | bytes 3145736 | tf_op jit(solution)/shard_map/ppermute | solution.py:586
  80.8 26.9 %collective-permute-start.24 = (bf16[128,1024]{1,0:T(8,128)(2,1)S(1)}, bf16[128,1024]{1,0:T(8,128)(2,1)S(1)}, u32[]{:S(2)}, u32[]{:S(2)}) collective-permute-start(bf16[128,1024]{1,0:T(8,128)(2,1)S(1)} %dynamic-slice_bitcast_fusion.4), channel_id=1, source_target_pairs={{0,1},{1,0},{2,3},{3,2},{4,5},{5,4},{6,7},{7,6},{8,9},{9,8},{10,11... | collective-permute-start | bytes 786440 | tf_op jit(solution)/shard_map/ppermute | solution.py:586
  82.8 25.2 %collective-permute-start.9 = (bf16[128,1024]{1,0:T(8,128)(2,1)S(1)}, bf16[128,1024]{1,0:T(8,128)(2,1)S(1)}, u32[]{:S(2)}, u32[]{:S(2)}) collective-permute-start(bf16[128,1024]{1,0:T(8,128)(2,1)S(1)} %collective-permute-done.8), channel_id=1, source_target_pairs={{0,4},{2,6},{4,0},{6,2},{8,12},{10,14},{12,8},{14,10},{16,20},{18,... | collective-permute-start | bytes 786440 | tf_op jit(solution)/shard_map/ppermute | solution.py:582
  96.7 44.1 %collective-permute-start.5 = (bf16[512,1536]{0,1:T(8,128)(2,1)}, bf16[512,1536]{0,1:T(8,128)(2,1)}, u32[]{:S(2)}, u32[]{:S(2)}) collective-permute-start(bf16[512,1536]{0,1:T(8,128)(2,1)} %maximum_select_fusion.10), channel_id=1, source_target_pairs={{0,2},{2,0},{4,6},{6,4},{8,10},{10,8},{12,14},{14,12},{16,18},{18,... | collective-permute-start | bytes 4718600 | tf_op jit(solution)/shard_map/ppermute | solution.py:582
  127.3 42.1 %collective-permute-start.16 = (bf16[512,1024]{1,0:T(8,128)(2,1)}, bf16[512,1024]{1,0:T(8,128)(2,1)S(1)}, u32[]{:S(2)}, u32[]{:S(2)}) collective-permute-start(bf16[512,1024]{1,0:T(8,128)(2,1)} %collective-permute-done.15), channel_id=1, source_target_pairs={{0,4},{2,6},{4,0},{6,2},{8,12},{10,14},{12,8},{14,10},{16,20},{18,... | collective-permute-start | bytes 3145736 | tf_op jit(solution)/shard_map/ppermute | solution.py:582
  130.5 84.0 %collective-permute-start.14 = (f32[2048]{0:T(1024)S(1)}, f32[2048]{0:T(1024)S(1)}, u32[]{:S(2)}, u32[]{:S(2)}) collective-permute-start(f32[2048]{0:T(1024)S(1)} %bitcast.208), channel_id=1, source_target_pairs={{0,1},{1,0},{2,3},{3,2},{4,5},{5,4},{6,7},{7,6},{8,9},{9,8},{10,11... | collective-permute-start | bytes 24584 | tf_op jit(solution)/shard_map/ppermute | solution.py:586
  139.4 77.0 %collective-permute-start.27 = (bf16[256,2048]{1,0:T(8,128)(2,1)}, bf16[256,2048]{1,0:T(8,128)(2,1)}, u32[]{:S(2)}, u32[]{:S(2)}) collective-permute-start(bf16[256,2048]{1,0:T(8,128)(2,1)} %dynamic-slice_bitcast_fusion.1), channel_id=1, source_target_pairs={{0,1},{1,0},{2,3},{3,2},{4,5},{5,4},{6,7},{7,6},{8,9},{9,8},{10,11... | collective-permute-start | bytes 3145736 | tf_op jit(solution)/shard_map/ppermute | solution.py:586
  140.7 48.1 %collective-permute-start.12 = (bf16[256,2048]{1,0:T(8,128)(2,1)}, bf16[256,2048]{1,0:T(8,128)(2,1)S(1)}, u32[]{:S(2)}, u32[]{:S(2)}) collective-permute-start(bf16[256,2048]{1,0:T(8,128)(2,1)} %collective-permute-done.11), channel_id=1, source_target_pairs={{0,4},{2,6},{4,0},{6,2},{8,12},{10,14},{12,8},{14,10},{16,20},{18,... | collective-permute-start | bytes 3145736 | tf_op jit(solution)/shard_map/ppermute | solution.py:582
  147.0 45.8 %collective-permute-start.7 = (bf16[256,1024]{1,0:T(8,128)(2,1)S(1)}, bf16[256,1024]{1,0:T(8,128)(2,1)S(1)}, u32[]{:S(2)}, u32[]{:S(2)}) collective-permute-start(bf16[256,1024]{1,0:T(8,128)(2,1)S(1)} %slice.258), channel_id=1, source_target_pairs={{0,2},{4,6},{8,10},{12,14},{16,18},{20,22},{24,26},{28,30},{1,3},{... | collective-permute-start | bytes 1572872 | tf_op jit(solution)/shard_map/ppermute | solution.py:1088
  169.4 32.5 %collective-permute-start.10 = (bf16[256,1024]{1,0:T(8,128)(2,1)S(1)}, bf16[256,1024]{1,0:T(8,128)(2,1)S(1)}, u32[]{:S(2)}, u32[]{:S(2)}) collective-permute-start(bf16[256,1024]{1,0:T(8,128)(2,1)S(1)} %copy-done.44), channel_id=1, source_target_pairs={{0,2},{2,0},{4,6},{6,4},{8,10},{10,8},{12,14},{14,12},{16,18},{18,... | collective-permute-start | bytes 1572872 | tf_op jit(solution)/shard_map/ppermute | solution.py:582
  188.8 27.6 %collective-permute-start.31 = (bf16[512,1024]{1,0:T(8,128)(2,1)}, bf16[512,1024]{1,0:T(8,128)(2,1)}, u32[]{:S(2)}, u32[]{:S(2)}) collective-permute-start(bf16[512,1024]{1,0:T(8,128)(2,1)} %dynamic-slice_bitcast_fusion), channel_id=1, source_target_pairs={{0,1},{1,0},{2,3},{3,2},{4,5},{5,4},{6,7},{7,6},{8,9},{9,8},{10,11... | collective-permute-start | bytes 3145736 | tf_op jit(solution)/shard_map/ppermute | solution.py:586
  192.8 24.5 %collective-permute-start.13 = (bf16[512,2048]{1,0:T(8,128)(2,1)}, bf16[512,2048]{1,0:T(8,128)(2,1)}, u32[]{:S(2)}, u32[]{:S(2)}) collective-permute-start(bf16[512,2048]{1,0:T(8,128)(2,1)} %maximum_select_fusion.6), channel_id=1, source_target_pairs={{0,2},{2,0},{4,6},{6,4},{8,10},{10,8},{12,14},{14,12},{16,18},{18,... | collective-permute-start | bytes 6291464 | tf_op jit(solution)/shard_map/ppermute | solution.py:582
  201.9 23.8 %collective-permute-start.17 = (bf16[1024,1024]{1,0:T(8,128)(2,1)}, bf16[1024,1024]{1,0:T(8,128)(2,1)S(1)}, u32[]{:S(2)}, u32[]{:S(2)}) collective-permute-start(bf16[1024,1024]{1,0:T(8,128)(2,1)} %maximum_select_fusion.7), channel_id=1, source_target_pairs={{0,2},{2,0},{4,6},{6,4},{8,10},{10,8},{12,14},{14,12},{16,18},{18,... | collective-permute-start | bytes 6291464 | tf_op jit(solution)/shard_map/ppermute | solution.py:582
  214.5 104.6 %collective-permute-start.30 = (f32[2048]{0:T(1024)S(1)}, f32[2048]{0:T(1024)S(1)}, u32[]{:S(2)}, u32[]{:S(2)}) collective-permute-start(f32[2048]{0:T(1024)S(1)} %bitcast.211), channel_id=1, source_target_pairs={{0,1},{1,0},{2,3},{3,2},{4,5},{5,4},{6,7},{7,6},{8,9},{9,8},{10,11... | collective-permute-start | bytes 24584 | tf_op jit(solution)/shard_map/ppermute | solution.py:586
  216.4 84.8 %collective-permute-start.26 = (bf16[256,1024]{1,0:T(8,128)(2,1)}, bf16[256,1024]{1,0:T(8,128)(2,1)}, u32[]{:S(2)}, u32[]{:S(2)}) collective-permute-start(bf16[256,1024]{1,0:T(8,128)(2,1)} %maximum_select_fusion.27), channel_id=1, source_target_pairs={{0,2},{2,0},{4,6},{6,4},{8,10},{10,8},{12,14},{14,12},{16,18},{18,... | collective-permute-start | bytes 1572872 | tf_op jit(solution)/shard_map/ppermute | solution.py:582
  216.4 53.7 %collective-permute-start.28 = (bf16[256,2048]{1,0:T(8,128)(2,1)}, bf16[256,2048]{1,0:T(8,128)(2,1)S(1)}, u32[]{:S(2)}, u32[]{:S(2)}) collective-permute-start(bf16[256,2048]{1,0:T(8,128)(2,1)} %collective-permute-done.27), channel_id=1, source_target_pairs={{0,4},{2,6},{4,0},{6,2},{8,12},{10,14},{12,8},{14,10},{16,20},{18,... | collective-permute-start | bytes 3145736 | tf_op jit(solution)/shard_map/ppermute | solution.py:582
  217.3 47.4 %collective-permute-start.32 = (bf16[512,1024]{1,0:T(8,128)(2,1)}, bf16[512,1024]{1,0:T(8,128)(2,1)S(1)}, u32[]{:S(2)}, u32[]{:S(2)}) collective-permute-start(bf16[512,1024]{1,0:T(8,128)(2,1)} %collective-permute-done.31), channel_id=1, source_target_pairs={{0,4},{2,6},{4,0},{6,2},{8,12},{10,14},{12,8},{14,10},{16,20},{18,... | collective-permute-start | bytes 3145736 | tf_op jit(solution)/shard_map/ppermute | solution.py:582
  236.3 47.0 %collective-permute-start.18 = (bf16[256,1024]{1,0:T(8,128)(2,1)S(1)}, bf16[256,1024]{1,0:T(8,128)(2,1)S(1)}, u32[]{:S(2)}, u32[]{:S(2)}) collective-permute-start(bf16[256,1024]{1,0:T(8,128)(2,1)S(1)} %slice.259), channel_id=1, source_target_pairs={{0,2},{4,6},{8,10},{12,14},{16,18},{20,22},{24,26},{28,30},{1,3},{... | collective-permute-start | bytes 1572872 | tf_op jit(solution)/shard_map/ppermute | solution.py:1088
  264.6 27.7 %collective-permute-start.23 = (bf16[256,1024]{1,0:T(8,128)(2,1)S(1)}, bf16[256,1024]{1,0:T(8,128)(2,1)S(1)}, u32[]{:S(2)}, u32[]{:S(2)}) collective-permute-start(bf16[256,1024]{1,0:T(8,128)(2,1)S(1)} %slice.260), channel_id=1, source_target_pairs={{0,2},{4,6},{8,10},{12,14},{16,18},{20,22},{24,26},{28,30},{1,3},{... | collective-permute-start | bytes 1572872 | tf_op jit(solution)/shard_map/ppermute | solution.py:1088
  270.1 40.5 %collective-permute-start.35 = (bf16[512,1024]{1,0:T(8,128)(2,1)}, bf16[512,1024]{1,0:T(8,128)(2,1)}, u32[]{:S(2)}, u32[]{:S(2)}) collective-permute-start(bf16[512,1024]{1,0:T(8,128)(2,1)} %param.23), channel_id=1, source_target_pairs={{0,0},{1,2},{2,1},{3,3},{4,4},{5,6},{6,5},{7,7},{8,8},{9,10},{10,9... | collective-permute-start | bytes 3145736 | tf_op jit(solution)/shard_map/ppermute | solution.py:595
  283.3 35.7 %collective-permute-start.29 = (bf16[512,2048]{1,0:T(8,128)(2,1)}, bf16[512,2048]{1,0:T(8,128)(2,1)}, u32[]{:S(2)}, u32[]{:S(2)}) collective-permute-start(bf16[512,2048]{1,0:T(8,128)(2,1)} %maximum_select_fusion.8), channel_id=1, source_target_pairs={{0,2},{2,0},{4,6},{6,4},{8,10},{10,8},{12,14},{14,12},{16,18},{18,... | collective-permute-start | bytes 6291464 | tf_op jit(solution)/shard_map/ppermute | solution.py:582
  292.3 33.8 %collective-permute-start.33 = (bf16[1024,1024]{1,0:T(8,128)(2,1)}, bf16[1024,1024]{1,0:T(8,128)(2,1)}, u32[]{:S(2)}, u32[]{:S(2)}) collective-permute-start(bf16[1024,1024]{1,0:T(8,128)(2,1)} %maximum_select_fusion.9), channel_id=1, source_target_pairs={{0,2},{2,0},{4,6},{6,4},{8,10},{10,8},{12,14},{14,12},{16,18},{18,... | collective-permute-start | bytes 6291464 | tf_op jit(solution)/shard_map/ppermute | solution.py:582
  363.0 41.3 %collective-permute-start.36 = (bf16[256,1024]{1,0:T(8,128)(2,1)}, bf16[256,1024]{1,0:T(8,128)(2,1)S(1)}, u32[]{:S(2)}, u32[]{:S(2)}) collective-permute-start(bf16[256,1024]{1,0:T(8,128)(2,1)} %pad_maximum_fusion.4), channel_id=1, source_target_pairs={{2,0},{6,4},{10,8},{14,12},{18,16},{22,20},{26,24},{30,28},{3,1},{... | collective-permute-start | bytes 1572872 | tf_op jit(solution)/shard_map/ppermute | solution.py:1138
  381.2 24.7 %collective-permute-start.37 = (bf16[256,1024]{1,0:T(8,128)(2,1)S(1)}, bf16[256,1024]{1,0:T(8,128)(2,1)S(1)}, u32[]{:S(2)}, u32[]{:S(2)}) collective-permute-start(bf16[256,1024]{1,0:T(8,128)(2,1)S(1)} %pad_maximum_fusion.5), channel_id=1, source_target_pairs={{2,0},{6,4},{10,8},{14,12},{18,16},{22,20},{26,24},{30,28},{3,1},{... | collective-permute-start | bytes 1572872 | tf_op jit(solution)/shard_map/ppermute | solution.py:1138
  394.7 476.4 %collective-permute-start.34 = (bf16[512,1024]{1,0:T(8,128)(2,1)}, bf16[512,1024]{1,0:T(8,128)(2,1)}, u32[]{:S(2)}, u32[]{:S(2)}) collective-permute-start(bf16[512,1024]{1,0:T(8,128)(2,1)} %add_convert_fusion), channel_id=1, source_target_pairs={{0,0},{1,2},{2,1},{3,3},{4,4},{5,6},{6,5},{7,7},{8,8},{9,10},{10,9... | collective-permute-start | bytes 3145736 | tf_op jit(solution)/shard_map/ppermute | solution.py:595
  843.9 27.2 %collective-permute-start.40 = (bf16[512,1024]{1,0:T(8,128)(2,1)}, bf16[512,1024]{1,0:T(8,128)(2,1)S(1)}, u32[]{:S(2)}, u32[]{:S(2)}) collective-permute-start(bf16[512,1024]{1,0:T(8,128)(2,1)} %fusion.61), channel_id=1, source_target_pairs={{0,0},{1,2},{2,1},{3,3},{4,4},{5,6},{6,5},{7,7},{8,8},{9,10},{10,9... | collective-permute-start | bytes 3145736 | tf_op jit(solution)/shard_map/ppermute | solution.py:595
  (108 other events, 1240.0 us)

commit v3 on v2

--- a/solution.py
+++ b/solution.py
@@ -371,7 +371,7 @@
 Z_BIT = 4
 BAND = 256
 LANES = 128
-VMEM_ASKED = 56 * 2**20
+VMEM_ASKED = 60 * 2**20
 
 
 def dot_nt(left, right):
@@ -430,80 +430,6 @@
             kept = jnp.where(lane == 2 * pair + head, highest + jnp.log(summed), kept)
         total_ref[rows, :] = kept
         out_ref[rows, :] = jnp.where(lane < HEAD_DIM, parts[0], parts[1]).astype(out_ref.dtype)
-
-
-def attention_backward_kernel(
-    q_ref,
-    k_ref,
-    v_ref,
-    kh_ref,
-    vh_ref,
-    segq_ref,
-    segk_ref,
-    grad_ref,
-    total_ref,
-    dq_ref,
-    dk_ref,
-    dv_ref,
-    dkh_ref,
-    dvh_ref,
-    bias_ref,
-):
-    pair = pl.program_id(0)
-
-    @pl.when(pair == 0)
-    def _():
-        fill_band_bias(segq_ref, segk_ref, bias_ref)
-
-    lane = lax.broadcasted_iota(jnp.int32, (BAND, LANES), 1)
-    scaling = HEAD_DIM ** (-0.5)
-    blocks = bias_ref.shape[0]
-    key_parts = [None] * (blocks + 1)
-    value_parts = [None] * (blocks + 1)
-    for block in range(blocks):
-        rows = slice(block * BAND, (block + 1) * BAND)
-        query = q_ref[rows, :]
-        grad = grad_ref[rows, :]
-        keys = band_rows(kh_ref, k_ref, block)
-        values = band_rows(vh_ref, v_ref, block)
-        grad_query = []
-        grad_keys = 0.0
-        grad_values = 0.0
-        for head in range(2):
-            mine = (lane // HEAD_DIM) == head
-            query_head = jnp.where(mine, query, 0)
-            grad_head = jnp.where(mine, grad, 0)
-            scores = dot_nt(query_head, keys) * scaling + bias_ref[block]
-            total = jnp.sum(
-                jnp.where(lane == 2 * pair + head, total_ref[rows, :], 0.0), axis=-1, keepdims=True
-            )
-            exact = jnp.exp(scores - total)
-            low = exact.astype(jnp.bfloat16)
-            grad_probs = dot_nt(grad_head, values)
-            row_terms = jnp.sum(exact * grad_probs, axis=-1, keepdims=True)
-            grad_scores = (exact * (grad_probs - row_terms)).astype(jnp.bfloat16)
-            grad_query.append(jnp.dot(grad_scores, keys, preferred_element_type=jnp.float32))
-            grad_keys = grad_keys + dot_tn(grad_scores, query_head)
-            grad_values = grad_values + dot_tn(low, grad_head)
-        dq_ref[rows, :] = (jnp.where(lane < HEAD_DIM, grad_query[0], grad_query[1]) * scaling).astype(
-            dq_ref.dtype
-        )
-        grad_keys = grad_keys * scaling
-        for part in range(2):
-            cut = slice(part * BAND, (part + 1) * BAND)
-            before_k, before_v = key_parts[block + part], value_parts[block + part]
-            key_parts[block + part] = (
-                grad_keys[cut] if before_k is None else before_k + grad_keys[cut]
-            )
-            value_parts[block + part] = (
-                grad_values[cut] if before_v is None else before_v + grad_values[cut]
-            )
-    dkh_ref[...] = key_parts[0].astype(dkh_ref.dtype)
-    dvh_ref[...] = value_parts[0].astype(dvh_ref.dtype)
-    for block in range(blocks):
-        rows = slice(block * BAND, (block + 1) * BAND)
-        dk_ref[rows, :] = key_parts[block + 1]
-        dv_ref[rows, :] = value_parts[block + 1]
 
 
 def attention_specs(rows, pairs):
@@ -544,39 +470,6 @@
     )(projected, projected, projected, halo, halo, segq, segk)
 
 
-def attention_backward(projected, halo, segq, segk, grad, totals):
-    rows, wide = projected.shape
-    width = wide // 3
-    pairs = width // LANES
-    by_pair = lambda pair: (0, pair)
-    return pl.pallas_call(
-        attention_backward_kernel,
-        grid=(pairs,),
-        in_specs=attention_specs(rows, pairs)
-        + [pl.BlockSpec((rows, LANES), by_pair), pl.BlockSpec((rows, LANES), lambda pair: (0, 0))],
-        out_specs=[
-            pl.BlockSpec((rows, LANES), by_pair),
-            pl.BlockSpec((rows, LANES), by_pair),
-            pl.BlockSpec((rows, LANES), by_pair),
-            pl.BlockSpec((BAND, LANES), by_pair),
-            pl.BlockSpec((BAND, LANES), by_pair),
-        ],
-        out_shape=[
-            jax.ShapeDtypeStruct((rows, width), jnp.bfloat16),
-            jax.ShapeDtypeStruct((rows, width), jnp.float32),
-            jax.ShapeDtypeStruct((rows, width), jnp.float32),
-            jax.ShapeDtypeStruct((BAND, width), jnp.bfloat16),
-            jax.ShapeDtypeStruct((BAND, width), jnp.bfloat16),
-        ],
-        scratch_shapes=[pltpu.VMEM((rows // BAND, BAND, 2 * BAND), jnp.float32)],
-        compiler_params=pltpu.CompilerParams(vmem_limit_bytes=VMEM_ASKED),
-        cost_estimate=pl.CostEstimate(
-            flops=20 * rows * BAND * width, bytes_accessed=20 * rows * width, transcendentals=rows * width * 8
-        ),
-        name="attention_backward",
-    )(projected, projected, projected, halo, halo, segq, segk, grad, totals)
-
-
 def swap_dp(array, bit):
     count = lax.axis_size("dp")
     return lax.ppermute(array, "dp", [(i, i ^ bit) for i in range(count)])
@@ -614,25 +507,72 @@
     return join_halves(place, mine, swap_dp(mine, bit))
 
 
-SLOTS = 12
-STAGED = 3
+SLOTS = 8
+CORE_SLOTS = 4
+RESULT_SLOTS = 11
+STAGED = 2
+FIRST = 2
 LAGS = dict(core=1, y=3, x=5, outer=7, inner=9, back=11, gather=13, whole=14, stored=15)
-VECTOR_TICKS = (1, 4, 7, 10, 13, 16, 19)
+VECTOR_STEP = 3
+VECTOR_ROWS = 12
 MESH = pl.DeviceIdType.MESH
+FFN_STEPS = 4
+QKV_STEPS = 3
 
 
 def added(left, right):
     return (left.astype(jnp.float32) + right.astype(jnp.float32)).astype(jnp.bfloat16)
 
 
-def reduce_kernel(plan, block, *refs):
-    count = len(plan)
-    chunks = sum(rows * columns for _, rows, columns in plan)
-    operand_refs = refs[: 3 * count]
-    vector_ref = refs[3 * count]
-    out_refs = refs[3 * count + 1 : 4 * count + 1]
-    vector_out = refs[4 * count + 1]
+def backward_kernel(layers, block, hidden_half, *refs):
     (
+        cot_ref,
+        gain_ref,
+        segq_ref,
+        segk_ref,
+        act_ref,
+        slope_ref,
+        normed_two_ref,
+        middle_ref,
+        attended_ref,
+        proj_ref,
+        halo_ref,
+        totals_ref,
+        normed_ref,
+        resid_ref,
+        qkv_own,
+        qkv_other,
+        out_own,
+        out_other,
+        up_own,
+        up_other,
+        down_own,
+        down_other,
+        grad_in_ref,
+        out_down,
+        out_up,
+        out_out,
+        out_qkv,
+        vector_out,
+        grad_branch,
+        grad_attn,
+        grad_before,
+        grad_proj,
+        grad_res,
+        collected,
+        grad_attended,
+        qkv_buf,
+        halo_buf,
+        totals_buf,
+        kept_kv,
+        halo_send,
+        halo_in,
+        rows_weight,
+        columns_weight,
+        slope_buf,
+        wide_buf,
+        bias_buf,
+        sums_buf,
         pair_buf,
         one_buf,
         part_buf,
@@ -648,14 +588,23 @@
         inner_in,
         result,
         vec_in,
+        load_sem,
+        io_sem,
+        halo_send_sem,
+        halo_recv_sem,
         staged_sem,
         send_sems,
         recv_sems,
         store_sem,
         vec_send,
         vec_recv,
-    ) = refs[4 * count + 2 :]
+    ) = refs
     half, quarter = block // 2, block // 4
+    width = 2 * block
+    rows_all = grad_branch.shape[0]
+    pairs_half = block // LANES
+    pairs = 2 * pairs_half
+    low = jnp.bfloat16
     place = lax.axis_index("dp")
     y = lax.axis_index("tensor")
     core = place % 2
@@ -682,22 +631,59 @@
     def _():
         pl.semaphore_wait(barrier, 4)
 
+    blocks_hidden = hidden_half // block
+    plan = (
+        ("rows", blocks_hidden, 2),
+        ("columns", 2, blocks_hidden),
+        ("rows", 1, 2),
+        ("columns", 2, 3),
+    )
     starts = []
-    total = 0
-    for _, rows, columns in plan:
-        starts.append(total)
-        total += rows * columns
+    per_layer = 0
+    for _, down_count, across_count in plan:
+        starts.append(per_layer)
+        per_layer += down_count * across_count
+    chunks = layers * per_layer
+    out_refs = (out_down, out_up, out_out, out_qkv)
+
+    def block_of(index):
+        return pl.ds(pl.multiple_of(index * block, block), block)
 
     def for_matrix(chunk, action):
-        for member, (kind, rows, columns) in enumerate(plan):
-
-            @pl.when((chunk >= starts[member]) & (chunk < starts[member] + rows * columns))
-            def _(member=member, kind=kind, columns=columns):
-                local = chunk - starts[member]
-                action(member, kind, local // columns, local % columns)
-
-    def cut(ref, column):
-        return ref.at[:, pl.ds(pl.multiple_of(column * block, block), block)]
+        layer = layers - 1 - chunk // per_layer
+        inside = chunk % per_layer
+        for member, (_, down_count, across_count) in enumerate(plan):
+            begin = starts[member]
+
+            @pl.when((inside >= begin) & (inside < begin + down_count * across_count))
+            def _(member=member, begin=begin, across_count=across_count):
+                local = inside - begin
+                action(member, layer, local // across_count, local % across_count)
+
+    def operands_of(member, layer, i, j):
+        if member == 0:
+            return (
+                grad_branch.at[:, block_of(j)],
+                act_ref.at[layer, 0, :, block_of(i)],
+                act_ref.at[layer, 1, :, block_of(i)],
+            )
+        if member == 1:
+            return (
+                normed_two_ref.at[layer, :, block_of(i)],
+                grad_before.at[j // 2, :, block_of(j % 2)],
+                grad_before.at[blocks_hidden // 2 + j // 2, :, block_of(j % 2)],
+            )
+        if member == 2:
+            return (
+                grad_attn.at[:, block_of(j)],
+                attended_ref.at[layer, 0, :, block_of(i)],
+                attended_ref.at[layer, 1, :, block_of(i)],
+            )
+        return (
+            normed_ref.at[layer, :, block_of(i)],
+            grad_proj.at[:, block_of(j)],
+            grad_proj.at[:, block_of(3 + j)],
+        )
 
     def staged_copies(chunk, shared, own, other):
         slot = chunk % STAGED
@@ -708,20 +694,11 @@
         )
 
     def stage_operands(chunk):
-        def action(member, kind, i, j):
-            shared, own, other = operand_refs[3 * member : 3 * member + 3]
-            split, single = (i, j) if kind == "rows" else (j, i)
-            for copy in staged_copies(
-                chunk, cut(shared, single), cut(own, split), cut(other, split)
-            ):
+        def action(member, layer, i, j):
+            for copy in staged_copies(chunk, *operands_of(member, layer, i, j)):
                 copy.start()
 
         for_matrix(chunk, action)
-
-    def wait_operands(chunk):
-        slot = chunk % STAGED
-        for copy in staged_copies(chunk, one_buf.at[slot], pair_buf.at[slot, 0], pair_buf.at[slot, 1]):
-            copy.wait()
 
     def remote(step, chunk, source, target, partner):
         slot = chunk % SLOTS
@@ -742,7 +719,7 @@
             0,
             chunk,
             part_buf.at[chunk % STAGED, :, rows_at(1 - core, half)],
-            core_in.at[chunk % SLOTS],
+            core_in.at[chunk % CORE_SLOTS],
             core_partner,
         )
 
@@ -765,41 +742,39 @@
     own_rows = rows_at(2 * core + x, quarter)
 
     def back_copy(chunk):
-        piece = result.at[chunk % SLOTS, own_rows]
+        piece = result.at[chunk % RESULT_SLOTS, own_rows]
         return remote(5, chunk, piece, piece, z_partner)
 
     def gather_copy(chunk):
-        piece = result.at[chunk % SLOTS, own_rows]
+        piece = result.at[chunk % RESULT_SLOTS, own_rows]
         return remote(6, chunk, piece, piece, x_partner)
 
     def whole_copy(chunk):
-        piece = result.at[chunk % SLOTS, rows_at(core, half)]
+        piece = result.at[chunk % RESULT_SLOTS, rows_at(core, half)]
         return remote(7, chunk, piece, piece, core_partner)
 
     def store_copy(chunk, target):
-        slot = chunk % SLOTS
+        slot = chunk % RESULT_SLOTS
         return pltpu.make_async_copy(result.at[slot], target, store_sem.at[slot])
 
     def multiply(chunk):
         slot = chunk % STAGED
-        wait_operands(chunk)
-
-        def action(member, kind, i, j):
+        for copy in staged_copies(chunk, one_buf.at[slot], pair_buf.at[slot, 0], pair_buf.at[slot, 1]):
+            copy.wait()
+        inside = chunk % per_layer
+        by_rows = (inside < starts[1]) | ((inside >= starts[2]) & (inside < starts[3]))
+
+        @pl.when(by_rows)
+        def _():
             single = one_buf[slot]
             for which in range(2):
-                split = pair_buf[slot, which]
-                product = dot_tn(split, single) if kind == "rows" else dot_tn(single, split)
-                part_buf[slot, which] = product.astype(jnp.bfloat16)
-
-        kinds = {}
-        for member, (kind, rows, columns) in enumerate(plan):
-            inside = (chunk >= starts[member]) & (chunk < starts[member] + rows * columns)
-            kinds[kind] = kinds[kind] | inside if kind in kinds else inside
-        for kind, inside in kinds.items():
-
-            @pl.when(inside)
-            def _(kind=kind):
-                action(None, kind, None, None)
+                part_buf[slot, which] = dot_tn(pair_buf[slot, which], single).astype(low)
+
+        @pl.when(jnp.logical_not(by_rows))
+        def _():
+            single = one_buf[slot]
+            for which in range(2):
+                part_buf[slot, which] = dot_tn(single, pair_buf[slot, which]).astype(low)
 
         core_copy(chunk).start()
 
@@ -807,9 +782,9 @@
         slot = chunk % SLOTS
         core_copy(chunk).wait()
         mine = rows_at(core, half)
-        other_kept[slot] = added(part_buf[chunk % STAGED, 1, mine, :], core_in[slot, 1])
+        other_kept[slot] = added(part_buf[chunk % STAGED, 1, mine, :], core_in[chunk % CORE_SLOTS, 1])
         y_copy(chunk).start()
-        own_kept[slot] = added(part_buf[chunk % STAGED, 0, mine, :], core_in[slot, 0])
+        own_kept[slot] = added(part_buf[chunk % STAGED, 0, mine, :], core_in[chunk % CORE_SLOTS, 0])
 
     def after_y(chunk):
         slot = chunk % SLOTS
@@ -847,7 +822,7 @@
         @pl.when(inner == 1)
         def _():
             inner_copy(chunk).wait()
-            result[slot, own_rows, :] = added(z_kept[slot], inner_in[slot])
+            result[chunk % RESULT_SLOTS, own_rows, :] = added(z_kept[slot], inner_in[slot])
             back_copy(chunk).start()
 
     def after_back(chunk):
@@ -868,13 +843,13 @@
     def after_whole(chunk):
         whole_copy(chunk).wait()
 
-        def action(member, kind, i, j):
-            store_copy(chunk, out_refs[member].at[rows_at(i, block), rows_at(j, block)]).start()
+        def action(member, layer, i, j):
+            store_copy(chunk, out_refs[member].at[layer, block_of(i), block_of(j)]).start()
 
         for_matrix(chunk, action)
 
     def after_store(chunk):
-        store_copy(chunk, result.at[chunk % SLOTS]).wait()
+        store_copy(chunk, result.at[chunk % RESULT_SLOTS]).wait()
 
     vector_partners = (core_partner, y_partner, x_partner, z_partner, middle_partner, z_partner)
 
@@ -894,7 +869,6 @@
 
     def vector_tick(step):
         if step == 0:
-            vector_out[...] = vector_ref[...]
             vector_copy(0).start()
         elif step <= 3:
             vector_copy(step - 1).wait()
@@ -937,9 +911,325 @@
             def _():
                 vector_copy(5).wait_recv()
 
+    norm_two_step = FFN_STEPS
+    out_step = norm_two_step + 1
+    attention_step = out_step + 1
+    qkv_step = attention_step + pairs + 1
+    norm_one_step = qkv_step + QKV_STEPS
+    period = norm_one_step + 1
+    jobs = layers * period
+    hidden_step = 2 * hidden_half // FFN_STEPS
+
+    def loads(kind, slot, *sources):
+        targets = {
+            "ffn": (rows_weight.at[slot], columns_weight.at[slot], slope_buf.at[slot]),
+            "wide": (wide_buf,),
+            "out": (rows_weight.at[slot, pl.ds(0, block)], rows_weight.at[slot, pl.ds(block, block)]),
+            "attention": (
+                qkv_buf.at[slot, 0],
+                qkv_buf.at[slot, 1],
+                qkv_buf.at[slot, 2],
+                halo_buf.at[slot, 0],
+                halo_buf.at[slot, 1],
+                totals_buf.at[slot],
+            ),
+            "qkv": (
+                columns_weight.at[slot, :, pl.ds(0, block)],
+                columns_weight.at[slot, :, pl.ds(block, block)],
+            ),
+        }[kind]
+        sources = sources or targets
+        return [
+            pltpu.make_async_copy(source, target, load_sem.at[slot, index])
+            for index, (source, target) in enumerate(zip(sources, targets))
+        ]
+
+    def prefetch(t):
+        slot = t % 2
+        layer = layers - 1 - t // period
+        step = t % period
+
+        for which, (up_ref, down_ref) in enumerate(((up_own, down_own), (up_other, down_other))):
+
+            @pl.when((step < FFN_STEPS) & (step // (FFN_STEPS // 2) == which))
+            def _(which=which, up_ref=up_ref, down_ref=down_ref):
+                cut = rows_at(step % (FFN_STEPS // 2), hidden_step)
+                for copy in loads(
+                    "ffn",
+                    slot,
+                    down_ref.at[layer, cut, :],
+                    up_ref.at[layer, :, cut],
+                    slope_ref.at[layer, which, :, cut],
+                ):
+                    copy.start()
+
+        for at, source in ((norm_two_step, middle_ref), (norm_one_step, resid_ref)):
+
+            @pl.when(step == at)
+            def _(source=source):
+                for copy in loads("wide", slot, source.at[layer]):
+                    copy.start()
+
+        @pl.when(step == out_step)
+        def _():
+            for copy in loads("out", slot, out_own.at[layer], out_other.at[layer]):
+                copy.start()
+
+        @pl.when((step >= attention_step) & (step < attention_step + pairs))
+        def _():
+            pair = step - attention_step
+            which, inside = pair // pairs_half, pair % pairs_half
+
+            def lanes(third):
+                return rows_at(third * pairs_half + inside, LANES)
+
+            for copy in loads(
+                "attention",
+                slot,
+                *[proj_ref.at[layer, which, :, lanes(third)] for third in range(3)],
+                *[halo_ref.at[layer, which, :, lanes(third)] for third in range(2)],
+                totals_ref.at[layer, which],
+            ):
+                copy.start()
+
+        @pl.when((step >= qkv_step) & (step < qkv_step + QKV_STEPS))
+        def _():
+            for part in range(2):
+                index = 2 * (step - qkv_step) + part
+                for which, source in enumerate((qkv_own, qkv_other)):
+
+                    @pl.when(index // 3 == which)
+                    def _(part=part, index=index, source=source):
+                        pltpu.make_async_copy(
+                            source.at[layer, :, block_of(index % 3)],
+                            columns_weight.at[slot, :, pl.ds(part * block, block)],
+                            load_sem.at[slot, part],
+                        ).start()
+
+    def wait_loads(kind, slot):
+        for copy in loads(kind, slot):
+            copy.wait()
+
+    tiles = [slice(r, r + BAND) for r in range(0, rows_all, BAND)]
+    fine_tiles = [slice(r, r + LANES) for r in range(0, rows_all, LANES)]
+
+    def vector_row(layer, row):
+        return pl.ds(layer * VECTOR_ROWS + row, 1)
+
+    def column_sum(values):
+        return jnp.sum(values.astype(jnp.float32), axis=0, keepdims=True)
+
+    def ffn_job(layer, step, slot):
+        wait_loads("ffn", slot)
+        sums = 0.0
+        for tile in tiles:
+            grad_hidden = dot_nt(grad_branch[tile, :], rows_weight[slot])
+            before = (grad_hidden * slope_buf[slot, tile, :].astype(jnp.float32)).astype(low)
+            grad_before[step, tile, :] = before
+            sums = sums + column_sum(before)
+            product = dot_nt(before, columns_weight[slot])
+
+            @pl.when(step == 0)
+            def _(tile=tile, product=product):
+                collected[tile, :] = product
+
+            @pl.when(step > 0)
+            def _(tile=tile, product=product):
+                collected[tile, :] = collected[tile, :] + product
+
+        per_half = FFN_STEPS // 2
+        which = step // per_half
+        owner = which + y - 2 * which * y
+        vector_out[vector_row(layer, 2 + owner * per_half + step % per_half), :] = sums
+
+    def norm_job(layer, index, slot):
+        wait_loads("wide", slot)
+        gain = gain_ref[pl.ds(2 * layer + index, 1), :]
+        gain_sum, shift_sum, attn_sum, branch_sum = 0.0, 0.0, 0.0, 0.0
+        for tile in fine_tiles:
+            incoming = collected[tile, :]
+            values = wide_buf[tile, :]
+            average = jnp.mean(values, axis=-1, keepdims=True)
+            centred = values - average
+            inverse = lax.rsqrt(jnp.mean(centred * centred, axis=-1, keepdims=True) + epsilon)
+            unit = centred * inverse
+            scaled = incoming * gain
+            first_mean = jnp.mean(scaled, axis=-1, keepdims=True)
+            second_mean = jnp.mean(scaled * unit, axis=-1, keepdims=True)
+            total = grad_res[tile, :] + inverse * (scaled - first_mean - unit * second_mean)
+            grad_res[tile, :] = total
+            rounded = total.astype(low)
+            gain_sum = gain_sum + column_sum(incoming * unit)
+            shift_sum = shift_sum + column_sum(incoming)
+            if index == 1:
+                attn_sum = attn_sum + column_sum(rounded)
+                branch_sum = branch_sum + column_sum(grad_branch[tile, :])
+                grad_attn[tile, :] = rounded
+            else:
+                grad_branch[tile, :] = rounded
+        vector_out[vector_row(layer, 8 + index), :] = gain_sum
+        vector_out[vector_row(layer, 10 + index), :] = shift_sum
+        if index == 1:
+            vector_out[vector_row(layer, 6), :] = attn_sum
+            vector_out[vector_row(layer, 7), :] = branch_sum
+
+    def out_job(slot):
+        wait_loads("out", slot)
+        for tile in tiles:
+            grad_attended[tile, :] = dot_nt(grad_attn[tile, :], rows_weight[slot]).astype(low)
+
+    def halo_copy(pair):
+        return pltpu.make_async_remote_copy(
+            src_ref=halo_send.at[pair % 2],
+            dst_ref=halo_in.at[pair],
+            send_sem=halo_send_sem.at[pair],
+            recv_sem=halo_recv_sem.at[pair],
+            device_id=core_partner,
+            device_id_type=MESH,
+        )
+
+    def proj_lanes(pair, third):
+        which, inside = pair // pairs_half, pair % pairs_half
+        return rows_at(which * 3 * pairs_half + third * pairs_half + inside, LANES)
+
+    def attention_job(pair, slot):
+        wait_loads("attention", slot)
+        lane = lax.broadcasted_iota(jnp.int32, (BAND, LANES), 1)
+        scaling = HEAD_DIM ** (-0.5)
+        count = len(tiles)
+        key_parts = [None] * (count + 1)
+        value_parts = [None] * (count + 1)
+        here = rows_at(pair, LANES)
+        for index, tile in enumerate(tiles):
+            query = qkv_buf[slot, 0, tile, :]
+            grad = grad_attended[tile, here]
+            keys = band_rows(halo_buf.at[slot, 0], qkv_buf.at[slot, 1], index)
+            values = band_rows(halo_buf.at[slot, 1], qkv_buf.at[slot, 2], index)
+            grad_query = []
+            grad_keys = 0.0
+            grad_values = 0.0
+            for head in range(2):
+                mine = (lane // HEAD_DIM) == head
+                query_head = jnp.where(mine, query, 0)
+                grad_head = jnp.where(mine, grad, 0)
+                scores = dot_nt(query_head, keys) * scaling + bias_buf[index]
+                total = jnp.sum(
+                    jnp.where(
+                        lane == 2 * (pair % pairs_half) + head, totals_buf[slot, tile, :], 0.0
+                    ),
+                    axis=-1,
+                    keepdims=True,
+                )
+                exact = jnp.exp(scores - total)
+                grad_probs = dot_nt(grad_head, values)
+                row_terms = jnp.sum(exact * grad_probs, axis=-1, keepdims=True)
+                grad_scores = (exact * (grad_probs - row_terms)).astype(low)
+                grad_query.append(jnp.dot(grad_scores, keys, preferred_element_type=jnp.float32))
+                grad_keys = grad_keys + dot_tn(grad_scores, query_head)
+                grad_values = grad_values + dot_tn(exact.astype(low), grad_head)
+            grad_proj[tile, proj_lanes(pair, 0)] = (
+                jnp.where(lane < HEAD_DIM, grad_query[0], grad_query[1]) * scaling
+            ).astype(low)
+            grad_keys = grad_keys * scaling
+            for part in range(2):
+                cut = slice(part * BAND, (part + 1) * BAND)
+                old_k, old_v = key_parts[index + part], value_parts[index + part]
+                key_parts[index + part] = grad_keys[cut] if old_k is None else old_k + grad_keys[cut]
+                value_parts[index + part] = (
+                    grad_values[cut] if old_v is None else old_v + grad_values[cut]
+                )
+        for index in range(count - 1):
+            grad_proj[tiles[index], proj_lanes(pair, 1)] = key_parts[index + 1].astype(low)
+            grad_proj[tiles[index], proj_lanes(pair, 2)] = value_parts[index + 1].astype(low)
+        kept_kv[pair % 2, 0] = key_parts[count]
+        kept_kv[pair % 2, 1] = value_parts[count]
+
+        @pl.when(core == 1)
+        def _():
+            halo_send[pair % 2, 0] = key_parts[0].astype(low)
+            halo_send[pair % 2, 1] = value_parts[0].astype(low)
+            halo_copy(pair).start()
+
+    def finish_pair(pair):
+        last = tiles[-1]
+
+        @pl.when(core == 0)
+        def _():
+            halo_copy(pair).wait_recv()
+            for third in range(2):
+                grad_proj[last, proj_lanes(pair, third + 1)] = (
+                    kept_kv[pair % 2, third] + halo_in[pair, third].astype(jnp.float32)
+                ).astype(low)
+
+        @pl.when(core == 1)
+        def _():
+            halo_copy(pair).wait_send()
+            for third in range(2):
+                grad_proj[last, proj_lanes(pair, third + 1)] = kept_kv[pair % 2, third].astype(low)
+
+    def qkv_job(layer, step, slot):
+        wait_loads("qkv", slot)
+        sums = 0.0
+        for tile in tiles:
+            grad = grad_proj[tile, rows_at(step, width)]
+            sums = sums + column_sum(grad)
+            product = dot_nt(grad, columns_weight[slot])
+
+            @pl.when(step == 0)
+            def _(tile=tile, product=product):
+                collected[tile, :] = product
+
+            @pl.when(step > 0)
+            def _(tile=tile, product=product):
+                collected[tile, :] = collected[tile, :] + product
+
+        sums_buf[...] = sums
+        for when, part, which, row in ((0, 0, 0, 0), (1, 0, 0, 1), (1, 1, 1, 0), (2, 1, 1, 1)):
+
+            @pl.when(step == when)
+            def _(part=part, which=which, row=row):
+                owner = 1 - y if which else y
+                vector_out[vector_row(layer, row), block_of(owner)] = sums_buf[
+                    :, part * block : (part + 1) * block
+                ]
+
+    def job(t):
+        slot = t % 2
+        layer = layers - 1 - t // period
+        step = t % period
+
+        @pl.when(step < FFN_STEPS)
+        def _():
+            ffn_job(layer, step, slot)
+
+        @pl.when(step == norm_two_step)
+        def _():
+            norm_job(layer, 1, slot)
+
+        @pl.when(step == out_step)
+        def _():
+            out_job(slot)
+
+        @pl.when((step > attention_step) & (step <= attention_step + pairs))
+        def _():
+            finish_pair(step - attention_step - 1)
+
+        @pl.when((step >= attention_step) & (step < attention_step + pairs))
+        def _():
+            attention_job(step - attention_step, slot)
+
+        @pl.when((step >= qkv_step) & (step < qkv_step + QKV_STEPS))
+        def _():
+            qkv_job(layer, step - qkv_step, slot)
+
+        @pl.when(step == norm_one_step)
+        def _():
+            norm_job(layer, 0, slot)
+
     stages = (
         (LAGS["core"], after_core),
         (0, multiply),
+        (None, job),
         (LAGS["y"], after_y),
         (LAGS["x"], after_x),
         (LAGS["outer"], after_outer),
@@ -950,21 +1240,41 @@
         (LAGS["whole"], after_whole),
     )
 
-    stage_operands(0)
+    first_load = pltpu.make_async_copy(cot_ref, grad_branch, io_sem.at[0])
+    first_load.start()
+    prefetch(0)
+    fill_band_bias(segq_ref, segk_ref, bias_buf)
+    first_load.wait()
+    for tile in tiles:
+        grad_res[tile, :] = grad_branch[tile, :].astype(jnp.float32)
+    vector_ticks = [jobs + VECTOR_STEP * step for step in range(7)]
 
     def tick(t, carry):
-        @pl.when(t + 1 < chunks)
-        def _():
-            stage_operands(t + 1)
+        @pl.when(t + 1 < jobs)
+        def _():
+            prefetch(t + 1)
+
+        ahead = t + 1 - FIRST
+
+        @pl.when((ahead >= 0) & (ahead < chunks))
+        def _():
+            stage_operands(ahead)
 
         for lag, action in stages:
-            chunk = t - lag
+            if lag is None:
+
+                @pl.when(t < jobs)
+                def _():
+                    job(t)
+
+                continue
+            chunk = t - FIRST - lag
 
             @pl.when((chunk >= 0) & (chunk < chunks))
             def _(chunk=chunk, action=action):
                 action(chunk)
 
-        for step, when in enumerate(VECTOR_TICKS):
+        for step, when in enumerate(vector_ticks):
 
             @pl.when(t == when)
             def _(step=step):
@@ -972,56 +1282,86 @@
 
         return carry
 
-    lax.fori_loop(0, max(chunks + LAGS["stored"], VECTOR_TICKS[-1] + 1), tick, 0)
-
-
-def reduce_grads(plan, operands, vector, block):
+    lax.fori_loop(0, max(chunks + FIRST + LAGS["stored"], vector_ticks[-1] + 1), tick, 0)
+    last_store = pltpu.make_async_copy(grad_branch, grad_in_ref, io_sem.at[1])
+    last_store.start()
+    last_store.wait()
+
+
+def run_backward(cotangent, gain, segq, segk, saved, weights, block):
+    rows, width = cotangent.shape
+    layers, hidden_half = weights[-1].shape[0], weights[-1].shape[1]
     half, quarter = block // 2, block // 4
-    kept = operands[0][0].shape[0]
-    low = jnp.bfloat16
-    shapes = [jax.ShapeDtypeStruct((rows * block, columns * block), low) for _, rows, columns in plan]
-    shapes.append(jax.ShapeDtypeStruct(vector.shape, jnp.float32))
+    low, wide = jnp.bfloat16, jnp.float32
+    pairs = width // LANES
     anywhere = pl.BlockSpec(memory_space=pl.ANY)
     in_vmem = pl.BlockSpec(memory_space=pltpu.VMEM)
-    chunks = sum(rows * columns for _, rows, columns in plan)
+    vector = (layers * VECTOR_ROWS, width)
+    hidden_step = 2 * hidden_half // FFN_STEPS
+    vmem = pltpu.VMEM
     return pl.pallas_call(
-        functools.partial(reduce_kernel, plan, block),
-        in_specs=[anywhere] * (3 * len(plan)) + [in_vmem],
-        out_specs=[anywhere] * len(plan) + [in_vmem],
-        out_shape=shapes,
+        functools.partial(backward_kernel, layers, block, hidden_half),
+        in_specs=[anywhere] + [in_vmem] * 3 + [anywhere] * (len(saved) + len(weights)),
+        out_specs=[anywhere] * 5 + [in_vmem],
+        out_shape=[
+            jax.ShapeDtypeStruct((rows, width), low),
+            jax.ShapeDtypeStruct((layers, hidden_half, width), low),
+            jax.ShapeDtypeStruct((layers, width, hidden_half), low),
+            jax.ShapeDtypeStruct((layers, block, width), low),
+            jax.ShapeDtypeStruct((layers, width, 3 * block), low),
+            jax.ShapeDtypeStruct(vector, wide),
+        ],
         scratch_shapes=[
-            pltpu.VMEM((STAGED, 2, kept, block), low),
-            pltpu.VMEM((STAGED, kept, block), low),
-            pltpu.VMEM((STAGED, 2, block, block), low),
-            pltpu.VMEM((SLOTS, 2, half, block), low),
-            pltpu.VMEM((SLOTS, half, block), low),
-            pltpu.VMEM((SLOTS, half, block), low),
-            pltpu.VMEM((SLOTS, half, block), low),
-            pltpu.VMEM((SLOTS, quarter, block), low),
-            pltpu.VMEM((SLOTS, quarter, block), low),
-            pltpu.VMEM((SLOTS, quarter, block), low),
-            pltpu.VMEM((SLOTS, quarter, block), low),
-            pltpu.VMEM((SLOTS, quarter, block), low),
-            pltpu.VMEM((SLOTS, quarter, block), low),
-            pltpu.VMEM((SLOTS, block, block), low),
-            pltpu.VMEM((5,) + vector.shape, jnp.float32),
+            vmem((rows, width), low),
+            vmem((rows, width), low),
+            vmem((FFN_STEPS, rows, hidden_step), low),
+            vmem((rows, 6 * block), low),
+            vmem((rows, width), wide),
+            vmem((rows, width), wide),
+            vmem((rows, width), low),
+            vmem((2, 3, rows, LANES), low),
+            vmem((2, 2, BAND, LANES), low),
+            vmem((2, rows, LANES), wide),
+            vmem((2, 2, BAND, LANES), wide),
+            vmem((2, 2, BAND, LANES), low),
+            vmem((pairs, 2, BAND, LANES), low),
+            vmem((2, hidden_step, width), low),
+            vmem((2, width, hidden_step), low),
+            vmem((2, rows, hidden_step), low),
+            vmem((rows, width), wide),
+            vmem((rows // BAND, BAND, 2 * BAND), wide),
+            vmem((1, width), wide),
+            vmem((STAGED, 2, rows, block), low),
+            vmem((STAGED, rows, block), low),
+            vmem((STAGED, 2, block, block), low),
+            vmem((CORE_SLOTS, 2, half, block), low),
+            vmem((SLOTS, half, block), low),
+            vmem((SLOTS, half, block), low),
+            vmem((SLOTS, half, block), low),
+            vmem((SLOTS, quarter, block), low),
+            vmem((SLOTS, quarter, block), low),
+            vmem((SLOTS, quarter, block), low),
+            vmem((SLOTS, quarter, block), low),
+            vmem((SLOTS, quarter, block), low),
+            vmem((SLOTS, quarter, block), low),
+            vmem((RESULT_SLOTS, block, block), low),
+            vmem((5,) + vector, wide),
+            pltpu.SemaphoreType.DMA((2, 6)),
+            pltpu.SemaphoreType.DMA((2,)),
+            pltpu.SemaphoreType.DMA((pairs,)),
+            pltpu.SemaphoreType.DMA((pairs,)),
             pltpu.SemaphoreType.DMA((STAGED, 3)),
             pltpu.SemaphoreType.DMA((8, SLOTS)),
             pltpu.SemaphoreType.DMA((8, SLOTS)),
-            pltpu.SemaphoreType.DMA((SLOTS,)),
+            pltpu.SemaphoreType.DMA((RESULT_SLOTS,)),
             pltpu.SemaphoreType.DMA((6,)),
             pltpu.SemaphoreType.DMA((6,)),
         ],
         compiler_params=pltpu.CompilerParams(
             collective_id=0, has_side_effects=True, vmem_limit_bytes=VMEM_ASKED
         ),
-        cost_estimate=pl.CostEstimate(
-            flops=4 * chunks * block * block * kept,
-            bytes_accessed=chunks * block * (3 * kept + block) * 2,
-            transcendentals=0,
-        ),
-        name="reduce_grads",
-    )(*[member for triple in operands for member in triple], vector)
+        name="backward",
+    )(cotangent, gain, segq, segk, *saved, *weights)
 
 
 def dot_low(left, right):
@@ -1056,9 +1396,6 @@
     halo_segments = jnp.where(core == 1, window_segments[:, rows - BAND : rows], -1)
     segq = own_segments.reshape(rows, 1)
     segk = jnp.concatenate([halo_segments, own_segments], axis=1)
-
-    def natural(own, other):
-        return join_halves(y, own, other)
 
     qkv_rows = [w_qkv[l].reshape(width, -1) for l in range(layers)]
     weights = []
@@ -1104,83 +1441,35 @@
         residual = middle + branch + out_bias[l, 1]
     out_act = swap_windows(residual.astype(jnp.bfloat16))
 
-    grad_residual = grad_residual.astype(jnp.float32)
-    triples = []
-    vectors = [None] * layers
-    for l in reversed(range(layers)):
-        qkv, out_w, up, down, qv, upb = weights[l]
-        residual, normed, saved_attention, middle, normed_two, saved_ffn = kept[l]
-        grad_branch = grad_residual.astype(jnp.bfloat16)
-        grad_down, grad_up, grad_up_bias = [], [], []
-        incoming = 0.0
+    def stacked(pick):
+        return jnp.stack([pick(kept[l]) for l in range(layers)])
+
+    def stacked_halves(group, member):
+        return jnp.stack(
+            [jnp.stack([kept[l][group][half][member] for half in range(2)]) for l in range(layers)]
+        )
+
+    saved = (
+        stacked_halves(5, 0),
+        stacked_halves(5, 1),
+        stacked(lambda state: state[4]),
+        stacked(lambda state: state[3]),
+        stacked_halves(2, 2),
+        stacked_halves(2, 0),
+        stacked_halves(2, 1),
+        stacked_halves(2, 3),
+        stacked(lambda state: state[1]),
+        stacked(lambda state: state[0]),
+    )
+    both = []
+    for member in range(4):
         for half in range(2):
-            activated, slope = saved_ffn[half]
-            grad_before = (dot_nt(grad_branch, down[half]) * slope.astype(jnp.float32)).astype(
-                jnp.bfloat16
-            )
-            grad_down.append(activated)
-            grad_up.append(grad_before)
-            grad_up_bias.append(jnp.sum(grad_before, axis=0, dtype=jnp.float32))
-            incoming = incoming + dot_nt(grad_before, up[half])
-        _, unit, inverse = layer_norm(middle, ln_gain[l, 1], ln_bias[l, 1])
-        through, gain_two, shift_two = norm_backward(incoming, unit, inverse, ln_gain[l, 1])
-        grad_middle = grad_residual + through
-        grad_attn = grad_middle.astype(jnp.bfloat16)
-        grad_out, grad_qkv, grad_qv = [], [], []
-        incoming = 0.0
-        for half in range(2):
-            projected, halo, attended, totals = saved_attention[half]
-            grad_out.append(attended)
-            grad_attended = dot_nt(grad_attn, out_w[half]).astype(jnp.bfloat16)
-            dq, dk, dv, dkh, dvh = attention_backward(
-                projected, halo, segq, segk, grad_attended, totals
-            )
-            sent = lax.ppermute(jnp.concatenate([dkh, dvh], axis=1), "dp", to_first)
-            whole = jnp.pad(sent, ((rows - BAND, 0), (0, 0))).astype(jnp.float32)
-            third = dk.shape[1]
-            grad_projected = jnp.concatenate(
-                [
-                    dq,
-                    (dk + whole[:, :third]).astype(jnp.bfloat16),
-                    (dv + whole[:, third:]).astype(jnp.bfloat16),
-                ],
-                axis=1,
-            )
-            grad_qkv.append(grad_projected)
-            sums = jnp.sum(grad_projected, axis=0, dtype=jnp.float32)
-            grad_qv.append(jnp.stack([sums[:third], sums[2 * third :]]))
-            incoming = incoming + dot_nt(grad_projected, qkv[half])
-        _, unit, inverse = layer_norm(residual, ln_gain[l, 0], ln_bias[l, 0])
-        through, gain_one, shift_one = norm_backward(incoming, unit, inverse, ln_gain[l, 0])
-        triples += [
-            (grad_branch, *grad_down),
-            (normed_two, *grad_up),
-            (grad_attn, *grad_out),
-            (normed, *grad_qkv),
-        ]
-        vectors[l] = jnp.concatenate(
-            [
-                natural(grad_qv[0].T, grad_qv[1].T).T.reshape(-1),
-                natural(grad_up_bias[0], grad_up_bias[1]),
-                jnp.sum(grad_attn, axis=0, dtype=jnp.float32),
-                jnp.sum(grad_branch, axis=0, dtype=jnp.float32),
-                gain_one,
-                gain_two,
-                shift_one,
-                shift_two,
-            ]
-        )
-        grad_residual = grad_middle + through
-    grad_in = swap_windows(grad_residual.astype(jnp.bfloat16))
-    block = width // 2
-    plan = []
-    for shared, own, _ in triples:
-        by_rows = shared is not None and len(plan) % 2 == 0
-        split, single = own.shape[1] // block, shared.shape[1] // block
-        plan.append(("rows", split, single) if by_rows else ("columns", single, split))
-    vector = jnp.stack(vectors)
-    *reduced, summed = reduce_grads(tuple(plan), triples, vector.reshape(-1, LANES), block)
-    summed = summed.reshape(vector.shape)
+            both.append(jnp.stack([weights[l][member][half] for l in range(layers)]))
+    grad_in, *reduced, summed = run_backward(
+        grad_residual, ln_gain.reshape(-1, width), segq, segk, saved, both, width // 2
+    )
+    grad_in = swap_windows(grad_in)
+    summed = summed.reshape(layers, -1)
     hidden = 2 * up_bias.shape[1]
     ends = [2 * width, 2 * width + hidden, 4 * width + hidden, 6 * width + hidden]
     qv_sum = summed[:, : ends[0]].reshape(layers, 2, width)
@@ -1188,21 +1477,16 @@
     grad_up_bias = lax.dynamic_slice_in_dim(
         summed[:, ends[0] : ends[1]], y * (hidden // 2), hidden // 2, axis=1
     )
-    stacked = [
-        jnp.stack(
-            [reduced[4 * (layers - 1 - l) + 3 - member] for l in range(layers)]
-        ).astype(jnp.float32)
-        for member in range(4)
-    ]
+    grad_down, grad_up, grad_out, grad_qkv = [member.astype(jnp.float32) for member in reduced]
     return (
         out_act,
         grad_in,
-        stacked[0].reshape(w_qkv.shape),
+        grad_qkv.reshape(w_qkv.shape),
         grad_qv_bias,
-        stacked[1],
-        stacked[2],
+        grad_out,
+        grad_up,
         grad_up_bias,
-        stacked[3],
+        grad_down,
         summed[:, ends[1] : ends[2]].reshape(layers, 2, width),
         summed[:, ends[2] : ends[3]].reshape(layers, 2, width),
         summed[:, ends[3] :].reshape(layers, 2, width),

time: 886 us -> 893 us (level)
  other arithmetic: 79.8 us -> 167 us
  matrix products: 140 us -> 55.2 us
  waiting for transfers between devices: 107 us -> 150 us
  Pallas kernels: 396 us -> 359 us
    another operation x1 -> x34, other arithmetic: 0.09 us -> 89.2 us  [the longest x16 35.3 us: stacked_halves(): jnp.stack([jnp.stack([kept[l][group][half][member] for half in range(2)])...]
    dot_general x16 -> x0, matrix products: 76.9 us -> none  [dot_nt(): lax.dot_general(left, right, (((1,), (1,)), ((), ())), preferred_element_...]
    ppermute x12, waiting for transfers between devices: 36.8 us -> 93.2 us  [swap_y(): return lax.ppermute(array, 'tensor', [(0, 1), (1, 0)])]
    pallas_call x5 -> x1, Pallas kernels: 364 us -> 326 us  [run_backward(): pl.pallas_call(functools.partial(backward_kernel, layers, block, hidden_h...]
    select_n x8 -> x16, other arithmetic: 24 us -> 49.2 us  [join_halves(): jnp.where(bit == 0, jnp.concatenate([mine, other], axis=0), jnp.concatena...]
    convert_element_type x17 -> x3, other arithmetic: 40.4 us -> 25.9 us  [local_split(): member.astype(jnp.float32)]
    ppermute x17, waiting for transfers between devices: 69.3 us -> 56.8 us  [swap_dp(): return lax.ppermute(array, 'dp', [(i, i ^ bit) for i in range(count)])]
    pallas_call x2 -> x0, local copies, waits for them, and re-layouts: 9.29 us -> none  [reduce_grads(): pl.pallas_call(functools.partial(reduce_kernel, plan, block), in_specs=[a...]
  transfers between devices with their start and end apart: 41 -> 37, of which waited for: 11 -> 10; matrix products, arithmetic and copies ran while one was open for 30% -> 33% of each run, Pallas kernels for 44% -> 41%
where the time goes in v3:
time: 893 us; the launch traced here: 883 us
  Pallas kernels  359 us (40%)
  other arithmetic  167 us (19%)
  waiting for transfers between devices  150 us (17%)
  local copies, waits for them, and re-layouts  93.3 us (10%)
  starting transfers between devices  56.8 us (6%)
  matrix products  55.2 us (6%)
    pallas_call x1, Pallas kernels, run_backward(): pl.pallas_call(functools.partial(backward_kernel, layers, block, hidden_h...  326 us
    ppermute x12, waiting for transfers between devices, swap_y(): return lax.ppermute(array, 'tensor', [(0, 1), (1, 0)])  93.2 us
    ppermute x17, waiting for transfers between devices, swap_dp(): return lax.ppermute(array, 'dp', [(i, i ^ bit) for i in range(count)])  56.8 us
    dot_general x16, matrix products, dot_low(): return jnp.dot(left, right, preferred_element_type=jnp.float32)  55.2 us
    select_n x16, other arithmetic, join_halves(): jnp.where(bit == 0, jnp.concatenate([mine, other], axis=0), jnp.concatena...  49.2 us
    another operation x16, other arithmetic, stacked_halves(): jnp.stack([jnp.stack([kept[l][group][half][member] for half in range(2)])...  35.3 us
    pallas_call x4, Pallas kernels, attention_forward(): pl.pallas_call(attention_forward_kernel, grid=(pairs,), in_specs=attentio...  32.6 us
    unnamed x158, local copies, waits for them, and re-layouts  31.5 us
  transfers between devices with their start and end apart: 37, of which 10 were waited for; matrix products, arithmetic and copies ran while one was open for 33% of the time, Pallas kernels for 41%

profile of v3, /device:TPU:0, one launch (start us, length us, event | category | flops | bytes accessed | tf_op | source)
XLA Modules:
  0.0 883.0 jit_solution(11531748599887595579)
XLA Ops:
  0.7 6.3 fusion.130
  26.2 6.0 fusion.129
  32.2 5.3 fusion.128
  62.9 6.0 pad_maximum_fusion.5.refs_14_
  73.5 6.5 collective-permute-done.8
  82.6 24.8 %collective-permute-done.24 = bf16[128,1024]{1,0:T(8,128)(2,1)S(1)} collective-permute-done((bf16[128,1024]{1,0:T(8,128)(2,1)S(1)}, bf16[128,1024]{1,0:T(8,128)(2,1)S(1)}, u32[]{:S(2)}, u32[]{:S(2)}) %collective-permute-start.24) | collective-permute-done | bytes 262176 | tf_op jit(solution)/shard_map/ppermute | solution.py:479
  119.8 33.4 %collective-permute-done.19 = bf16[256,1536]{1,0:T(8,128)(2,1)S(1)} collective-permute-done((bf16[256,1536]{1,0:T(8,128)(2,1)S(1)}, bf16[256,1536]{1,0:T(8,128)(2,1)S(1)}, u32[]{:S(2)}, u32[]{:S(2)}) %collective-permute-start.19) | collective-permute-done | bytes 786464 | tf_op jit(solution)/shard_map/ppermute | solution.py:479
  161.5 14.2 %collective-permute-done.31 = bf16[512,1024]{1,0:T(8,128)(2,1)} collective-permute-done((bf16[512,1024]{1,0:T(8,128)(2,1)}, bf16[512,1024]{1,0:T(8,128)(2,1)}, u32[]{:S(2)}, u32[]{:S(2)}) %collective-permute-start.31) | collective-permute-done | bytes 1048608 | tf_op jit(solution)/shard_map/ppermute | solution.py:479
  181.6 14.3 %collective-permute-done.27 = bf16[256,2048]{1,0:T(8,128)(2,1)} collective-permute-done((bf16[256,2048]{1,0:T(8,128)(2,1)}, bf16[256,2048]{1,0:T(8,128)(2,1)}, u32[]{:S(2)}, u32[]{:S(2)}) %collective-permute-start.27) | collective-permute-done | bytes 1048608 | tf_op jit(solution)/shard_map/ppermute | solution.py:479
  200.8 8.0 attention_forward.4
  218.3 17.9 %collective-permute-done.32 = bf16[512,1024]{1,0:T(8,128)(2,1)} collective-permute-done((bf16[512,1024]{1,0:T(8,128)(2,1)}, bf16[512,1024]{1,0:T(8,128)(2,1)}, u32[]{:S(2)}, u32[]{:S(2)}) %collective-permute-start.32) | collective-permute-done | bytes 1048608 | tf_op jit(solution)/shard_map/ppermute | solution.py:475
  242.4 16.2 %collective-permute-done.12 = bf16[256,2048]{1,0:T(8,128)(2,1)} collective-permute-done((bf16[256,2048]{1,0:T(8,128)(2,1)}, bf16[256,2048]{1,0:T(8,128)(2,1)}, u32[]{:S(2)}, u32[]{:S(2)}) %collective-permute-start.12) | collective-permute-done | bytes 1048608 | tf_op jit(solution)/shard_map/ppermute | solution.py:475
  264.8 15.8 %collective-permute-done.28 = bf16[256,2048]{1,0:T(8,128)(2,1)} collective-permute-done((bf16[256,2048]{1,0:T(8,128)(2,1)}, bf16[256,2048]{1,0:T(8,128)(2,1)}, u32[]{:S(2)}, u32[]{:S(2)}) %collective-permute-start.28) | collective-permute-done | bytes 1048608 | tf_op jit(solution)/shard_map/ppermute | solution.py:475
  280.6 9.5 %collective-permute-start.35 = (bf16[512,1024]{1,0:T(8,128)(2,1)}, bf16[512,1024]{1,0:T(8,128)(2,1)}, u32[]{:S(2)}, u32[]{:S(2)}) collective-permute-start(bf16[512,1024]{1,0:T(8,128)(2,1)} %param.23), channel_id=1, source_target_pairs={{0,0},{1,2},{2,1},{3,3},{4,4},{5,6},{6,5},{7,7},{8,8},{9,10},{10,9... | collective-permute-start | bytes 3145736 | tf_op jit(solution)/shard_map/ppermute | solution.py:488
  310.9 8.0 attention_forward.5
  342.2 7.5 fusion.141
  364.7 6.0 maximum_select_fusion.8
  373.9 7.6 pad_maximum_fusion.2.refs_19_
  381.5 5.5 maximum_select_fusion.11
  387.0 5.6 maximum_select_fusion.10
  392.6 7.6 pad_maximum_fusion.3.refs_21_
  414.0 8.1 attention_forward.7
  426.0 8.4 attention_forward.6
  452.6 7.8 add_convert_fusion
  478.3 7.8 pad_maximum_fusion.refs_4_
  486.1 6.3 pad_maximum_fusion.1.refs_5_
  492.4 326.1 %backward.1 = (bf16[512,1024]{1,0:T(8,128)(2,1)}, bf16[2,2048,1024]{2,1,0:T(8,128)(2,1)}, bf16[2,1024,2048]{2,1,0:T(8,128)(2,1)}, bf16[2,512,1024]{2,1,0:T(8,128...) custom-call(bf16[512,1024]{1,0:T(8,128)(2,1)} %collective-permute-done.35.refs_0_, ...), custom_call_target="tpu_custom_call" | custom-call | tf_op jit(solution)/shard_map/backward/pallas_call | solution.py:1302
  818.5 9.5 %collective-permute-start.36 = (bf16[512,1024]{1,0:T(8,128)(2,1)}, bf16[512,1024]{1,0:T(8,128)(2,1)}, u32[]{:S(2)}, u32[]{:S(2)}) collective-permute-start(bf16[512,1024]{1,0:T(8,128)(2,1)} %get-tuple-element.33), channel_id=1, source_target_pairs={{0,0},{1,2},{2,1},{3,3},{4,4},{5,6},{6,5},{7,7},{8,8},{9,10},{10,9... | collective-permute-start | bytes 3145736 | tf_op jit(solution)/shard_map/ppermute | solution.py:488
  828.0 9.4 %copy.39 = f32[2,1024,1536]{1,2,0:T(8,128)} copy(bf16[2,1024,1536]{2,1,0:T(8,128)(2,1)} %get-tuple-element.34) | data formatting | bytes 18874368 | tf_op jit(solution)/shard_map/reshape | solution.py:1484
  837.4 12.8 %copy.40 = f32[2,1024,3,512]{3,1,2,0:T(8,128)} copy(f32[2,1024,3,512]{1,3,2,0:T(8,128)} %bitcast.162) | data formatting | bytes 25165824
  852.8 11.7 %convert_element_type.83 = f32[2,1024,2048]{2,1,0:T(8,128)} convert(bf16[2,1024,2048]{2,1,0:T(8,128)(2,1)} %get-tuple-element.37) | non-fusion elementwise | flops 4194304 | bytes 25165824 | tf_op jit(solution)/shard_map/convert_element_type | solution.py:1480
  864.5 11.7 %convert_element_type.84 = f32[2,2048,1024]{2,1,0:T(8,128)} convert(bf16[2,2048,1024]{2,1,0:T(8,128)(2,1)} %get-tuple-element.38) | non-fusion elementwise | flops 4194304 | bytes 25165824 | tf_op jit(solution)/shard_map/convert_element_type | solution.py:1480
  (335 shorter events, 229.1 us)
Async XLA Ops:
  14.1 104.6 %collective-permute-start.3 = (bf16[256,1536]{1,0:T(8,128)(2,1)}, bf16[256,1536]{1,0:T(8,128)(2,1)}, u32[]{:S(2)}, u32[]{:S(2)}) collective-permute-start(bf16[256,1536]{1,0:T(8,128)(2,1)} %copy.42), channel_id=1, source_target_pairs={{0,1},{1,0},{2,3},{3,2},{4,5},{5,4},{6,7},{7,6},{8,9},{9,8},{10,11... | collective-permute-start | bytes 2359304 | tf_op jit(solution)/shard_map/ppermute | solution.py:479
  17.1 54.3 %collective-permute-start.6 = (f32[1024]{0:T(1024)S(1)}, f32[1024]{0:T(1024)S(1)}, u32[]{:S(2)}, u32[]{:S(2)}) collective-permute-start(f32[1024]{0:T(1024)S(1)} %bitcast.239), channel_id=1, source_target_pairs={{0,1},{1,0},{2,3},{3,2},{4,5},{5,4},{6,7},{7,6},{8,9},{9,8},{10,11... | collective-permute-start | bytes 12296 | tf_op jit(solution)/shard_map/ppermute | solution.py:479
  17.2 55.8 %collective-permute-start.22 = (f32[1024]{0:T(1024)S(1)}, f32[1024]{0:T(1024)S(1)}, u32[]{:S(2)}, u32[]{:S(2)}) collective-permute-start(f32[1024]{0:T(1024)S(1)} %bitcast.238), channel_id=1, source_target_pairs={{0,1},{1,0},{2,3},{3,2},{4,5},{5,4},{6,7},{7,6},{8,9},{9,8},{10,11... | collective-permute-start | bytes 12296 | tf_op jit(solution)/shard_map/ppermute | solution.py:479
  19.2 98.8 %collective-permute-start = (bf16[512,1024]{1,0:T(8,128)(2,1)}, bf16[512,1024]{1,0:T(8,128)(2,1)S(1)}, u32[]{:S(2)}, u32[]{:S(2)}) collective-permute-start(bf16[512,1024]{1,0:T(8,128)(2,1)} %param.12), channel_id=1, source_target_pairs={{0,0},{1,2},{2,1},{3,3},{4,4},{5,6},{6,5},{7,7},{8,8},{9,10},{10,9... | collective-permute-start | bytes 3145736 | tf_op jit(solution)/shard_map/ppermute | solution.py:488
  21.0 49.8 %collective-permute-start.2 = (s32[1,1024]{1,0:T(1,128)S(1)}, s32[1,1024]{1,0:T(1,128)S(1)}, u32[]{:S(2)}, u32[]{:S(2)}) collective-permute-start(s32[1,1024]{1,0:T(1,128)S(1)} %copy-done.66), channel_id=1, source_target_pairs={{0,2},{2,0},{4,6},{6,4},{8,10},{10,8},{12,14},{14,12},{16,18},{18,... | collective-permute-start | bytes 12296 | tf_op jit(solution)/shard_map/ppermute | solution.py:475
  71.4 82.2 %collective-permute-start.15 = (bf16[512,1024]{1,0:T(8,128)(2,1)}, bf16[512,1024]{1,0:T(8,128)(2,1)}, u32[]{:S(2)}, u32[]{:S(2)}) collective-permute-start(bf16[512,1024]{1,0:T(8,128)(2,1)} %dynamic-slice_bitcast_fusion.2), channel_id=1, source_target_pairs={{0,1},{1,0},{2,3},{3,2},{4,5},{5,4},{6,7},{7,6},{8,9},{9,8},{10,11... | collective-permute-start | bytes 3145736 | tf_op jit(solution)/shard_map/ppermute | solution.py:479
  73.0 34.4 %collective-permute-start.24 = (bf16[128,1024]{1,0:T(8,128)(2,1)S(1)}, bf16[128,1024]{1,0:T(8,128)(2,1)S(1)}, u32[]{:S(2)}, u32[]{:S(2)}) collective-permute-start(bf16[128,1024]{1,0:T(8,128)(2,1)S(1)} %dynamic-slice_bitcast_fusion.4), channel_id=1, source_target_pairs={{0,1},{1,0},{2,3},{3,2},{4,5},{5,4},{6,7},{7,6},{8,9},{9,8},{10,11... | collective-permute-start | bytes 786440 | tf_op jit(solution)/shard_map/ppermute | solution.py:479
  80.0 29.9 %collective-permute-start.9 = (bf16[128,1024]{1,0:T(8,128)(2,1)S(1)}, bf16[128,1024]{1,0:T(8,128)(2,1)S(1)}, u32[]{:S(2)}, u32[]{:S(2)}) collective-permute-start(bf16[128,1024]{1,0:T(8,128)(2,1)S(1)} %collective-permute-done.8), channel_id=1, source_target_pairs={{0,4},{2,6},{4,0},{6,2},{8,12},{10,14},{12,8},{14,10},{16,20},{18,... | collective-permute-start | bytes 786440 | tf_op jit(solution)/shard_map/ppermute | solution.py:475
  109.9 48.3 %collective-permute-start.11 = (bf16[256,2048]{1,0:T(8,128)(2,1)}, bf16[256,2048]{1,0:T(8,128)(2,1)}, u32[]{:S(2)}, u32[]{:S(2)}) collective-permute-start(bf16[256,2048]{1,0:T(8,128)(2,1)} %dynamic-slice_bitcast_fusion.3), channel_id=1, source_target_pairs={{0,1},{1,0},{2,3},{3,2},{4,5},{5,4},{6,7},{7,6},{8,9},{9,8},{10,11... | collective-permute-start | bytes 3145736 | tf_op jit(solution)/shard_map/ppermute | solution.py:479
  115.7 37.4 %collective-permute-start.19 = (bf16[256,1536]{1,0:T(8,128)(2,1)S(1)}, bf16[256,1536]{1,0:T(8,128)(2,1)S(1)}, u32[]{:S(2)}, u32[]{:S(2)}) collective-permute-start(bf16[256,1536]{1,0:T(8,128)(2,1)S(1)} %copy.44), channel_id=1, source_target_pairs={{0,1},{1,0},{2,3},{3,2},{4,5},{5,4},{6,7},{7,6},{8,9},{9,8},{10,11... | collective-permute-start | bytes 2359304 | tf_op jit(solution)/shard_map/ppermute | solution.py:479
  118.0 35.6 %collective-permute-start.10 = (bf16[256,1024]{1,0:T(8,128)(2,1)S(1)}, bf16[256,1024]{1,0:T(8,128)(2,1)S(1)}, u32[]{:S(2)}, u32[]{:S(2)}) collective-permute-start(bf16[256,1024]{1,0:T(8,128)(2,1)S(1)} %maximum_select_fusion.38), channel_id=1, source_target_pairs={{0,2},{2,0},{4,6},{6,4},{8,10},{10,8},{12,14},{14,12},{16,18},{18,... | collective-permute-start | bytes 1572872 | tf_op jit(solution)/shard_map/ppermute | solution.py:475
  118.7 57.0 %collective-permute-start.31 = (bf16[512,1024]{1,0:T(8,128)(2,1)}, bf16[512,1024]{1,0:T(8,128)(2,1)}, u32[]{:S(2)}, u32[]{:S(2)}) collective-permute-start(bf16[512,1024]{1,0:T(8,128)(2,1)} %dynamic-slice_bitcast_fusion), channel_id=1, source_target_pairs={{0,1},{1,0},{2,3},{3,2},{4,5},{5,4},{6,7},{7,6},{8,9},{9,8},{10,11... | collective-permute-start | bytes 3145736 | tf_op jit(solution)/shard_map/ppermute | solution.py:479
  153.1 42.7 %collective-permute-start.27 = (bf16[256,2048]{1,0:T(8,128)(2,1)}, bf16[256,2048]{1,0:T(8,128)(2,1)}, u32[]{:S(2)}, u32[]{:S(2)}) collective-permute-start(bf16[256,2048]{1,0:T(8,128)(2,1)} %dynamic-slice_bitcast_fusion.1), channel_id=1, source_target_pairs={{0,1},{1,0},{2,3},{3,2},{4,5},{5,4},{6,7},{7,6},{8,9},{9,8},{10,11... | collective-permute-start | bytes 3145736 | tf_op jit(solution)/shard_map/ppermute | solution.py:479
  153.6 24.4 %collective-permute-start.4 = (bf16[256,1536]{1,0:T(8,128)(2,1)}, bf16[256,1536]{1,0:T(8,128)(2,1)S(1)}, u32[]{:S(2)}, u32[]{:S(2)}) collective-permute-start(bf16[256,1536]{1,0:T(8,128)(2,1)} %collective-permute-done.3), channel_id=1, source_target_pairs={{0,4},{2,6},{4,0},{6,2},{8,12},{10,14},{12,8},{14,10},{16,20},{18,... | collective-permute-start | bytes 2359304 | tf_op jit(solution)/shard_map/ppermute | solution.py:475
  158.2 39.0 %collective-permute-start.20 = (bf16[256,1536]{1,0:T(8,128)(2,1)S(1)}, bf16[256,1536]{1,0:T(8,128)(2,1)S(1)}, u32[]{:S(2)}, u32[]{:S(2)}) collective-permute-start(bf16[256,1536]{1,0:T(8,128)(2,1)S(1)} %collective-permute-done.19), channel_id=1, source_target_pairs={{0,4},{2,6},{4,0},{6,2},{8,12},{10,14},{12,8},{14,10},{16,20},{18,... | collective-permute-start | bytes 2359304 | tf_op jit(solution)/shard_map/ppermute | solution.py:475
  159.5 37.2 %collective-permute-start.1 = (bf16[256,1024]{1,0:T(8,128)(2,1)S(1)}, bf16[256,1024]{1,0:T(8,128)(2,1)S(1)}, u32[]{:S(2)}, u32[]{:S(2)}) collective-permute-start(bf16[256,1024]{1,0:T(8,128)(2,1)S(1)} %slice.191), channel_id=1, source_target_pairs={{0,2},{4,6},{8,10},{12,14},{16,18},{20,22},{24,26},{28,30},{1,3},{... | collective-permute-start | bytes 1572872 | tf_op jit(solution)/shard_map/ppermute | solution.py:1425
  175.7 37.9 %collective-permute-start.16 = (bf16[512,1024]{1,0:T(8,128)(2,1)}, bf16[512,1024]{1,0:T(8,128)(2,1)}, u32[]{:S(2)}, u32[]{:S(2)}) collective-permute-start(bf16[512,1024]{1,0:T(8,128)(2,1)} %collective-permute-done.15), channel_id=1, source_target_pairs={{0,4},{2,6},{4,0},{6,2},{8,12},{10,14},{12,8},{14,10},{16,20},{18,... | collective-permute-start | bytes 3145736 | tf_op jit(solution)/shard_map/ppermute | solution.py:475
  178.1 58.1 %collective-permute-start.32 = (bf16[512,1024]{1,0:T(8,128)(2,1)}, bf16[512,1024]{1,0:T(8,128)(2,1)}, u32[]{:S(2)}, u32[]{:S(2)}) collective-permute-start(bf16[512,1024]{1,0:T(8,128)(2,1)} %collective-permute-done.31), channel_id=1, source_target_pairs={{0,4},{2,6},{4,0},{6,2},{8,12},{10,14},{12,8},{14,10},{16,20},{18,... | collective-permute-start | bytes 3145736 | tf_op jit(solution)/shard_map/ppermute | solution.py:475
  195.9 62.7 %collective-permute-start.12 = (bf16[256,2048]{1,0:T(8,128)(2,1)}, bf16[256,2048]{1,0:T(8,128)(2,1)}, u32[]{:S(2)}, u32[]{:S(2)}) collective-permute-start(bf16[256,2048]{1,0:T(8,128)(2,1)} %collective-permute-done.11), channel_id=1, source_target_pairs={{0,4},{2,6},{4,0},{6,2},{8,12},{10,14},{12,8},{14,10},{16,20},{18,... | collective-permute-start | bytes 3145736 | tf_op jit(solution)/shard_map/ppermute | solution.py:475
  196.7 98.0 %collective-permute-start.5 = (bf16[512,1536]{1,0:T(8,128)(2,1)S(1)}, bf16[512,1536]{1,0:T(8,128)(2,1)}, u32[]{:S(2)}, u32[]{:S(2)}) collective-permute-start(bf16[512,1536]{1,0:T(8,128)(2,1)S(1)} %maximum_select_fusion.30), channel_id=1, source_target_pairs={{0,2},{2,0},{4,6},{6,4},{8,10},{10,8},{12,14},{14,12},{16,18},{18,... | collective-permute-start | bytes 4718600 | tf_op jit(solution)/shard_map/ppermute | solution.py:475
  198.1 82.5 %collective-permute-start.28 = (bf16[256,2048]{1,0:T(8,128)(2,1)}, bf16[256,2048]{1,0:T(8,128)(2,1)}, u32[]{:S(2)}, u32[]{:S(2)}) collective-permute-start(bf16[256,2048]{1,0:T(8,128)(2,1)} %collective-permute-done.27), channel_id=1, source_target_pairs={{0,4},{2,6},{4,0},{6,2},{8,12},{10,14},{12,8},{14,10},{16,20},{18,... | collective-permute-start | bytes 3145736 | tf_op jit(solution)/shard_map/ppermute | solution.py:475
  213.7 85.1 %collective-permute-start.21 = (bf16[512,1536]{1,0:T(8,128)(2,1)S(1)}, bf16[512,1536]{1,0:T(8,128)(2,1)S(1)}, u32[]{:S(2)}, u32[]{:S(2)}) collective-permute-start(bf16[512,1536]{1,0:T(8,128)(2,1)S(1)} %maximum_select_fusion.31), channel_id=1, source_target_pairs={{0,2},{2,0},{4,6},{6,4},{8,10},{10,8},{12,14},{14,12},{16,18},{18,... | collective-permute-start | bytes 4718600 | tf_op jit(solution)/shard_map/ppermute | solution.py:475
  236.1 105.5 %collective-permute-start.14 = (f32[2048]{0:T(1024)S(1)}, f32[2048]{0:T(1024)S(1)}, u32[]{:S(2)}, u32[]{:S(2)}) collective-permute-start(f32[2048]{0:T(1024)S(1)} %bitcast.205), channel_id=1, source_target_pairs={{0,1},{1,0},{2,3},{3,2},{4,5},{5,4},{6,7},{7,6},{8,9},{9,8},{10,11... | collective-permute-start | bytes 24584 | tf_op jit(solution)/shard_map/ppermute | solution.py:479
  258.6 193.7 %collective-permute-start.30 = (f32[2048]{0:T(1024)S(1)}, f32[2048]{0:T(1024)S(1)}, u32[]{:S(2)}, u32[]{:S(2)}) collective-permute-start(f32[2048]{0:T(1024)S(1)} %bitcast.202), channel_id=1, source_target_pairs={{0,1},{1,0},{2,3},{3,2},{4,5},{5,4},{6,7},{7,6},{8,9},{9,8},{10,11... | collective-permute-start | bytes 24584 | tf_op jit(solution)/shard_map/ppermute | solution.py:479
  280.6 211.8 %collective-permute-start.35 = (bf16[512,1024]{1,0:T(8,128)(2,1)}, bf16[512,1024]{1,0:T(8,128)(2,1)}, u32[]{:S(2)}, u32[]{:S(2)}) collective-permute-start(bf16[512,1024]{1,0:T(8,128)(2,1)} %param.23), channel_id=1, source_target_pairs={{0,0},{1,2},{2,1},{3,3},{4,4},{5,6},{6,5},{7,7},{8,8},{9,10},{10,9... | collective-permute-start | bytes 3145736 | tf_op jit(solution)/shard_map/ppermute | solution.py:488
  294.7 47.5 %collective-permute-start.17 = (bf16[1024,1024]{1,0:T(8,128)(2,1)}, bf16[1024,1024]{1,0:T(8,128)(2,1)}, u32[]{:S(2)}, u32[]{:S(2)}) collective-permute-start(bf16[1024,1024]{1,0:T(8,128)(2,1)} %maximum_select_fusion.23), channel_id=1, source_target_pairs={{0,2},{2,0},{4,6},{6,4},{8,10},{10,8},{12,14},{14,12},{16,18},{18,... | collective-permute-start | bytes 6291464 | tf_op jit(solution)/shard_map/ppermute | solution.py:475
  310.1 26.3 %collective-permute-start.13 = (bf16[512,2048]{1,0:T(8,128)(2,1)}, bf16[512,2048]{1,0:T(8,128)(2,1)}, u32[]{:S(2)}, u32[]{:S(2)}) collective-permute-start(bf16[512,2048]{1,0:T(8,128)(2,1)} %maximum_select_fusion.22), channel_id=1, source_target_pairs={{0,2},{2,0},{4,6},{6,4},{8,10},{10,8},{12,14},{14,12},{16,18},{18,... | collective-permute-start | bytes 6291464 | tf_op jit(solution)/shard_map/ppermute | solution.py:475
  336.4 45.1 %collective-permute-start.33 = (bf16[1024,1024]{1,0:T(8,128)(2,1)}, bf16[1024,1024]{1,0:T(8,128)(2,1)}, u32[]{:S(2)}, u32[]{:S(2)}) collective-permute-start(bf16[1024,1024]{1,0:T(8,128)(2,1)} %maximum_select_fusion.25), channel_id=1, source_target_pairs={{0,2},{2,0},{4,6},{6,4},{8,10},{10,8},{12,14},{14,12},{16,18},{18,... | collective-permute-start | bytes 6291464 | tf_op jit(solution)/shard_map/ppermute | solution.py:475
  353.1 60.9 %collective-permute-start.23 = (bf16[256,1024]{1,0:T(8,128)(2,1)}, bf16[256,1024]{1,0:T(8,128)(2,1)}, u32[]{:S(2)}, u32[]{:S(2)}) collective-permute-start(bf16[256,1024]{1,0:T(8,128)(2,1)} %slice.195), channel_id=1, source_target_pairs={{0,2},{4,6},{8,10},{12,14},{16,18},{20,22},{24,26},{28,30},{1,3},{... | collective-permute-start | bytes 1572872 | tf_op jit(solution)/shard_map/ppermute | solution.py:1425
  359.6 65.6 %collective-permute-start.18 = (bf16[256,1024]{1,0:T(8,128)(2,1)}, bf16[256,1024]{1,0:T(8,128)(2,1)S(1)}, u32[]{:S(2)}, u32[]{:S(2)}) collective-permute-start(bf16[256,1024]{1,0:T(8,128)(2,1)} %slice.194), channel_id=1, source_target_pairs={{0,2},{4,6},{8,10},{12,14},{16,18},{20,22},{24,26},{28,30},{1,3},{... | collective-permute-start | bytes 1572872 | tf_op jit(solution)/shard_map/ppermute | solution.py:1425
  460.4 418.9 %collective-permute-start.34 = (bf16[512,1024]{1,0:T(8,128)(2,1)}, bf16[512,1024]{1,0:T(8,128)(2,1)S(1)}, u32[]{:S(2)}, u32[]{:S(2)}) collective-permute-start(bf16[512,1024]{1,0:T(8,128)(2,1)} %add_convert_fusion), channel_id=1, source_target_pairs={{0,0},{1,2},{2,1},{3,3},{4,4},{5,6},{6,5},{7,7},{8,8},{9,10},{10,9... | collective-permute-start | bytes 3145736 | tf_op jit(solution)/shard_map/ppermute | solution.py:488
  818.5 60.8 %collective-permute-start.36 = (bf16[512,1024]{1,0:T(8,128)(2,1)}, bf16[512,1024]{1,0:T(8,128)(2,1)}, u32[]{:S(2)}, u32[]{:S(2)}) collective-permute-start(bf16[512,1024]{1,0:T(8,128)(2,1)} %get-tuple-element.33), channel_id=1, source_target_pairs={{0,0},{1,2},{2,1},{3,3},{4,4},{5,6},{6,5},{7,7},{8,8},{9,10},{10,9... | collective-permute-start | bytes 3145736 | tf_op jit(solution)/shard_map/ppermute | solution.py:488
  (80 other events, 883.4 us)

commit v4 on v3

--- a/solution.py
+++ b/solution.py
@@ -366,9 +366,6 @@
     return (out_act, grad_in) + tuple(spread_stack) + tuple(shared_stack)
 
 
-CORE_BIT = 1
-X_BIT = 2
-Z_BIT = 4
 BAND = 256
 LANES = 128
 VMEM_ASKED = 60 * 2**20
@@ -382,129 +379,632 @@
     return lax.dot_general(left, right, (((0,), (0,)), ((), ())), preferred_element_type=jnp.float32)
 
 
-def fill_band_bias(segq_ref, segk_ref, bias_ref):
-    blocks = bias_ref.shape[0]
-    for block in range(blocks):
-        rows = slice(block * BAND, (block + 1) * BAND)
-        columns = slice(block * BAND, (block + 2) * BAND)
+def dot_low(left, right):
+    return jnp.dot(left, right, preferred_element_type=jnp.float32)
+
+
+UNITS_LAYER = 12
+BEATS_EVERY_TICK = 18
+Y_AHEAD = 2
+
+
+def fill_band_bias(segk_ref, bias_ref):
+    wide = segk_ref.shape[1]
+    values = lax.broadcasted_iota(jnp.int32, (16, wide), 0)
+    member = (values == segk_ref[...]).astype(jnp.float32).astype(jnp.bfloat16)
+    for block in range(bias_ref.shape[0]):
+        queries = member[:, (block + 1) * BAND : (block + 2) * BAND]
+        keys = member[:, block * BAND : (block + 2) * BAND]
         row_place = lax.broadcasted_iota(jnp.int32, (BAND, 2 * BAND), 0) + BAND
         column_place = lax.broadcasted_iota(jnp.int32, (BAND, 2 * BAND), 1)
-        allowed = (segq_ref[rows, :] == segk_ref[:, columns]) & (column_place <= row_place)
+        allowed = (dot_tn(queries, keys) > 0.5) & (column_place <= row_place)
         bias_ref[block] = jnp.where(allowed, 0.0, masked_score)
 
 
-def band_rows(halo_ref, rows_ref, block):
+def band_rows(halo, rows, block):
     if block == 0:
-        return jnp.concatenate([halo_ref[...], rows_ref[0:BAND, :]], axis=0)
-    return rows_ref[(block - 1) * BAND : (block + 1) * BAND, :]
-
-
-def attention_forward_kernel(
-    q_ref, k_ref, v_ref, kh_ref, vh_ref, segq_ref, segk_ref, out_ref, total_ref, bias_ref
-):
-    pair = pl.program_id(0)
-
-    @pl.when(pair == 0)
+        return jnp.concatenate([halo, rows[0:BAND, :]], axis=0)
+    return rows[(block - 1) * BAND : (block + 1) * BAND, :]
+
+
+def aligned(index, size):
+    return pl.ds(pl.multiple_of(index * size, size), size)
+
+
+def forward_kernel(layers, block, hidden_half, *refs):
+    (
+        tokens_ref,
+        cot_ref,
+        segments_ref,
+        qkv_own,
+        out_own,
+        up_own,
+        down_own,
+        qv_bias_ref,
+        up_bias_ref,
+        out_bias_ref,
+        gain_ref,
+        shift_ref,
+        out_act_ref,
+        cot_out,
+        segk_out,
+        qkv_other,
+        out_other,
+        up_other,
+        down_other,
+        act_out,
+        slope_out,
+        normed_two_out,
+        middle_out,
+        attended_out,
+        proj_out,
+        halo_out,
+        totals_out,
+        normed_out,
+        resid_out,
+        tokens_buf,
+        segments_in,
+        qv_bias_in,
+        up_bias_in,
+        resid,
+        collected,
+        normed,
+        normed_two,
+        proj,
+        halo,
+        attended,
+        totals,
+        act_buf,
+        slope_buf,
+        qkv_weight,
+        out_weight,
+        up_weight,
+        down_weight,
+        bias_buf,
+        start_send,
+        start_recv,
+        swap_sem,
+        relay_send,
+        relay_recv,
+        halo_send_sem,
+        halo_recv_sem,
+        load_sem,
+        store_sem,
+        pair_store_sem,
+    ) = refs
+    width = 2 * block
+    rows_all = tokens_buf.shape[0]
+    pairs_half = block // LANES
+    blocks_hidden = hidden_half // block
+    low = jnp.bfloat16
+    place = lax.axis_index("dp")
+    y = lax.axis_index("tensor")
+    core = place % 2
+    x = (place // 2) % 2
+    z = place // 4
+    z_low = z % 2
+    core_partner = {"dp": place + 1 - 2 * core, "tensor": y}
+    x_partner = {"dp": place + 2 - 4 * x, "tensor": y}
+    y_partner = {"dp": place, "tensor": 1 - y}
+    z_partner = {"dp": place + 4 - 8 * z_low, "tensor": y}
+    swap_partner = {"dp": place + 1 - 2 * core, "tensor": 1 - y}
+    swaps = core + y - 2 * core * y
+
+    barrier = pltpu.get_barrier_semaphore()
+    for partner in (core_partner, x_partner, y_partner, z_partner, swap_partner):
+        pl.semaphore_signal(barrier, inc=1, device_id=partner, device_id_type=MESH)
+    pl.semaphore_wait(barrier, 5)
+
+    def remote(source, target, send, recv, partner):
+        return pltpu.make_async_remote_copy(
+            src_ref=source,
+            dst_ref=target,
+            send_sem=send,
+            recv_sem=recv,
+            device_id=partner,
+            device_id_type=MESH,
+        )
+
+    def swap_copy(index, source, target):
+        return remote(source, target, start_send.at[index], start_recv.at[index], swap_partner)
+
+    def swap_start(index, source, target):
+        @pl.when(swaps == 1)
+        def _():
+            swap_copy(index, source, target).start()
+
+        @pl.when(swaps == 0)
+        def _():
+            pltpu.make_async_copy(source, target, swap_sem.at[index]).start()
+
+    def swap_wait(index, source, target):
+        @pl.when(swaps == 1)
+        def _():
+            swap_copy(index, source, target).wait()
+
+        @pl.when(swaps == 0)
+        def _():
+            pltpu.make_async_copy(source, target, swap_sem.at[index]).wait()
+
+    segments_copy = remote(
+        segments_ref, segments_in, start_send.at[2], start_recv.at[2], core_partner
+    )
+    qv_copy = remote(qv_bias_ref, qv_bias_in, start_send.at[3], start_recv.at[3], y_partner)
+    up_copy = remote(up_bias_ref, up_bias_in, start_send.at[4], start_recv.at[4], y_partner)
+
+    units = layers * UNITS_LAYER
+
+    def for_unit(unit, action):
+        layer, inside = unit // UNITS_LAYER, unit % UNITS_LAYER
+
+        @pl.when(inside < 3)
+        def _():
+            action(qkv_own.at[layer, inside], qkv_other.at[layer, inside])
+
+        @pl.when(inside == 3)
+        def _():
+            action(out_own.at[layer], out_other.at[layer])
+
+        @pl.when((inside >= 4) & (inside % 2 == 0))
+        def _():
+            cut = aligned((inside - 4) // 2, block)
+            action(up_own.at[layer, :, cut], up_other.at[layer, :, cut])
+
+        @pl.when((inside >= 4) & (inside % 2 == 1))
+        def _():
+            cut = aligned((inside - 4) // 2, block)
+            action(down_own.at[layer, cut, :], down_other.at[layer, cut, :])
+
+    def hop_copy(hop, unit, source, target):
+        partner = (y_partner, x_partner, z_partner, core_partner)[hop]
+        return remote(source, target, relay_send.at[hop, unit], relay_recv.at[hop, unit], partner)
+
+    def piece_of(view, hop, short):
+        rows = view.shape[0]
+        if hop == 3:
+            return view.at[aligned(core, rows // 2)]
+        if hop == 2:
+            return view.at[aligned(2 * core + z_low, rows // 4)]
+        if short:
+            return view.at[aligned(4 * core + 2 * z_low + x, rows // 8)]
+        return view.at[aligned(2 * core + x, rows // 4)]
+
+    def by_length(unit, hop, action):
+        if hop == 3:
+            action(False)
+            return
+
+        @pl.when(unit % 3 != 0)
+        def _():
+            action(True)
+
+        if hop < 2:
+
+            @pl.when(unit % 3 == 0)
+            def _():
+                action(False)
+
+    def hop_start(hop, unit):
+        def go(own, other):
+            def one(short):
+                source = piece_of(own if hop == 0 else other, hop, short)
+                hop_copy(hop, unit, source, piece_of(other, hop, short)).start()
+
+            by_length(unit, hop, one)
+
+        for_unit(unit, go)
+
+    def hop_wait(hop, unit):
+        def one(short):
+            piece = piece_of(down_other.at[0, pl.ds(0, block), :], hop, short)
+            hop_copy(hop, unit, piece, piece).wait()
+
+        by_length(unit, hop, one)
+
+    def when_unit(unit, action):
+        @pl.when((unit >= 0) & (unit < units))
+        def _():
+            action(unit)
+
+    def beat(b):
+        def after_y(unit):
+            hop_wait(0, unit)
+            hop_start(1, unit)
+
+        def after_x(unit):
+            hop_wait(1, unit)
+            hop_start(2, unit)
+
+        def after_z(unit):
+            hop_wait(2, unit)
+            hop_start(3, unit)
+
+        when_unit(b + Y_AHEAD, lambda unit: hop_start(0, unit))
+        when_unit(b - 1, after_y)
+        when_unit(b - 2, after_x)
+        when_unit(b - 3, after_z)
+        when_unit(b - 4, lambda unit: hop_wait(3, unit))
+
+    other_step = 3 + pairs_half
+    out_step = other_step + 1 + pairs_half
+    norm_two_step = out_step + 1
+    ffn_step = norm_two_step + 1
+    end_step = ffn_step + 2 * blocks_hidden
+    period = end_step + 1
+    jobs = layers * period
+
+    def loads(kind, slot, *sources):
+        targets = {
+            "qkv": (qkv_weight,),
+            "out": (out_weight.at[0], out_weight.at[1]),
+            "ffn": (up_weight.at[slot], down_weight.at[slot]),
+        }[kind]
+        sources = sources or targets
+        return [
+            pltpu.make_async_copy(source, target, load_sem.at[slot, index])
+            for index, (source, target) in enumerate(zip(sources, targets))
+        ]
+
+    def start_all(copies):
+        for copy in copies:
+            copy.start()
+
+    def wait_all(copies):
+        for copy in copies:
+            copy.wait()
+
+    def prefetch(t):
+        slot = t % 2
+        layer, step = t // period, t % period
+        for at, source in ((1, qkv_own), (other_step, qkv_other)):
+
+            @pl.when(step == at)
+            def _(source=source):
+                start_all(loads("qkv", slot, source.at[layer]))
+
+        @pl.when(step == out_step)
+        def _():
+            start_all(loads("out", slot, out_own.at[layer], out_other.at[layer]))
+
+        for which, (up_ref, down_ref) in enumerate(((up_own, down_own), (up_other, down_other))):
+            begin = ffn_step + which * blocks_hidden
+
+            @pl.when((step >= begin) & (step < begin + blocks_hidden))
+            def _(begin=begin, up_ref=up_ref, down_ref=down_ref):
+                cut = aligned(step - begin, block)
+                start_all(loads("ffn", slot, up_ref.at[layer, :, cut], down_ref.at[layer, cut, :]))
+
+    tiles = [slice(r, r + BAND) for r in range(0, rows_all, BAND)]
+    fine_tiles = [slice(r, r + LANES) for r in range(0, rows_all, LANES)]
+
+    def normalize(layer, index, target):
+        gain = gain_ref[pl.ds(2 * layer + index, 1), :]
+        shift = shift_ref[pl.ds(2 * layer + index, 1), :]
+        for tile in fine_tiles:
+            values, _, _ = layer_norm(resid[tile, :], gain, shift)
+            target[tile, :] = values.astype(low)
+
+    def store(index, source, target):
+        return pltpu.make_async_copy(source, target, store_sem.at[index])
+
+    def first_stores(layer):
+        return [store(0, resid, resid_out.at[layer]), store(1, normed, normed_out.at[layer])]
+
+    def proj_stores(layer, which):
+        return [
+            store(
+                2 + 3 * which + third,
+                proj.at[which, third],
+                proj_out.at[layer, which, :, pl.ds(third * block, block)],
+            )
+            for third in range(3)
+        ]
+
+    def halo_store(layer, which):
+        return store(8 + which, halo.at[layer, which], halo_out.at[layer, which])
+
+    def attended_stores(layer, which):
+        return [
+            store(10 + which, attended.at[which], attended_out.at[layer, which]),
+            store(12 + which, totals.at[which], totals_out.at[layer, which]),
+        ]
+
+    def second_stores(layer):
+        return [
+            store(14, resid, middle_out.at[layer]),
+            store(15, normed_two, normed_two_out.at[layer]),
+        ]
+
+    def ffn_stores(layer, index, slot):
+        which, inside = index // blocks_hidden, index % blocks_hidden
+        cut = aligned(inside, block)
+        return [
+            pltpu.make_async_copy(
+                buf.at[slot], out.at[layer, which, :, cut], pair_store_sem.at[slot, kind]
+            )
+            for kind, (buf, out) in enumerate(((act_buf, act_out), (slope_buf, slope_out)))
+        ]
+
+    def halo_copy(layer, which):
+        return remote(
+            proj.at[which, pl.ds(1, 2), pl.ds(rows_all - BAND, BAND)],
+            halo.at[layer, which],
+            halo_send_sem.at[layer, which],
+            halo_recv_sem.at[layer, which],
+            core_partner,
+        )
+
+    def first_job(layer):
+        normalize(layer, 0, normed)
+        start_all(first_stores(layer))
+
+    def qkv_job(layer, which, slot):
+        wait_all(loads("qkv", slot))
+        bias = qv_bias_in if which else qv_bias_ref
+        for third in range(3):
+            for tile in tiles:
+                product = dot_low(normed[tile, :], qkv_weight[third])
+                if third != 1:
+                    product = product + bias[pl.ds(2 * layer + third // 2, 1), :]
+                proj[which, third, tile, :] = product.astype(low)
+
+        @pl.when(core == 0)
+        def _():
+            halo_copy(layer, which).start()
+
+        start_all(proj_stores(layer, which))
+
+    def attention_job(layer, which, pair):
+        @pl.when(pair == 0)
+        def _():
+            @pl.when(core == 0)
+            def _():
+                halo_copy(layer, which).wait_send()
+
+            @pl.when(core == 1)
+            def _():
+                halo_copy(layer, which).wait_recv()
+
+            halo_store(layer, which).start()
+            totals[which] = jnp.zeros_like(totals[which])
+
+        lane = lax.broadcasted_iota(jnp.int32, (BAND, LANES), 1)
+        here = aligned(pair, LANES)
+        for index, tile in enumerate(tiles):
+            query = proj[which, 0, tile, here]
+            keys = band_rows(halo[layer, which, 0, :, here], proj[which, 1, :, here], index)
+            values = band_rows(halo[layer, which, 1, :, here], proj[which, 2, :, here], index)
+            parts = []
+            kept = totals[which, tile, :]
+            for head in range(2):
+                mine = (lane // HEAD_DIM) == head
+                scores = (
+                    dot_nt(jnp.where(mine, query, 0), keys) * HEAD_DIM ** (-0.5) + bias_buf[index]
+                )
+                highest = jnp.max(scores, axis=-1, keepdims=True)
+                raised = jnp.exp(scores - highest)
+                summed = jnp.sum(raised, axis=-1, keepdims=True)
+                parts.append(dot_low(raised.astype(low), values) / summed)
+                kept = jnp.where(lane == 2 * pair + head, highest + jnp.log(summed), kept)
+            totals[which, tile, :] = kept
+            attended[which, tile, here] = jnp.where(lane < HEAD_DIM, parts[0], parts[1]).astype(low)
+
+        @pl.when(pair == pairs_half - 1)
+        def _():
+            start_all(attended_stores(layer, which))
+
+    def out_job(layer, slot):
+        wait_all(loads("out", slot))
+        wait_all(first_stores(layer))
+        for which in range(2):
+            wait_all(proj_stores(layer, which))
+            halo_store(layer, which).wait()
+        bias = out_bias_ref[pl.ds(2 * layer, 1), :]
+        for tile in tiles:
+            branch = dot_low(attended[0, tile, :], out_weight[0])
+            branch = branch + dot_low(attended[1, tile, :], out_weight[1])
+            resid[tile, :] = resid[tile, :] + branch + bias
+
+    def second_job(layer):
+        normalize(layer, 1, normed_two)
+        start_all(second_stores(layer))
+
+    def ffn_job(layer, which, inside, slot):
+        index = which * blocks_hidden + inside
+        wait_all(loads("ffn", slot))
+
+        @pl.when(index >= 2)
+        def _():
+            wait_all(ffn_stores(layer, index - 2, slot))
+
+        bias = (up_bias_in if which else up_bias_ref)[pl.ds(layer, 1), aligned(inside, block)]
+        for tile in tiles:
+            before = dot_low(normed_two[tile, :], up_weight[slot]) + bias
+            square = before * before
+            tangent = jnp.tanh(gelu_coeff * before * (1.0 + cubic_coeff * square))
+            raised = 0.5 * (1.0 + tangent)
+            activated = (before * raised).astype(low)
+            act_buf[slot, tile, :] = activated
+            slope_buf[slot, tile, :] = (
+                raised
+                + 0.5
+                * before
+                * (1.0 - tangent * tangent)
+                * gelu_coeff
+                * (1.0 + 3.0 * cubic_coeff * square)
+            ).astype(low)
+            product = dot_low(activated, down_weight[slot])
+            if which:
+                collected[tile, :] = collected[tile, :] + product
+                continue
+
+            @pl.when(inside == 0)
+            def _(tile=tile, product=product):
+                collected[tile, :] = product
+
+            @pl.when(inside > 0)
+            def _(tile=tile, product=product):
+                collected[tile, :] = collected[tile, :] + product
+
+        start_all(ffn_stores(layer, index, slot))
+
+    def end_job(layer, slot):
+        wait_all(ffn_stores(layer, 2 * blocks_hidden - 2, slot))
+        wait_all(ffn_stores(layer, 2 * blocks_hidden - 1, 1 - slot))
+        wait_all(second_stores(layer))
+        for which in range(2):
+            wait_all(attended_stores(layer, which))
+        bias = out_bias_ref[pl.ds(2 * layer + 1, 1), :]
+        for tile in tiles:
+            resid[tile, :] = resid[tile, :] + collected[tile, :] + bias
+
+    def job(t):
+        slot = t % 2
+        layer, step = t // period, t % period
+
+        def at(first, count, action):
+            @pl.when((step >= first) & (step < first + count))
+            def _():
+                action(step - first)
+
+        at(0, 1, lambda _: first_job(layer))
+        at(1, 1, lambda _: qkv_job(layer, 0, slot))
+        at(2, pairs_half, lambda pair: attention_job(layer, 0, pair))
+        at(other_step, 1, lambda _: qkv_job(layer, 1, slot))
+        at(other_step + 1, pairs_half, lambda pair: attention_job(layer, 1, pair))
+        at(out_step, 1, lambda _: out_job(layer, slot))
+        at(norm_two_step, 1, lambda _: second_job(layer))
+        at(ffn_step, blocks_hidden, lambda inside: ffn_job(layer, 0, inside, slot))
+        at(ffn_step + blocks_hidden, blocks_hidden, lambda inside: ffn_job(layer, 1, inside, slot))
+        at(end_step, 1, lambda _: end_job(layer, slot))
+
+    swap_start(0, tokens_ref, tokens_buf)
+    halo[...] = jnp.zeros_like(halo)
+    segments_copy.start()
+    qv_copy.start()
+    up_copy.start()
+    for unit in range(Y_AHEAD):
+        hop_start(0, unit)
+    segments_copy.wait()
+    window = jnp.where(core == y, segments_ref[...], segments_in[...])
+
+    @pl.when(core == 0)
     def _():
-        fill_band_bias(segq_ref, segk_ref, bias_ref)
-        total_ref[...] = jnp.zeros_like(total_ref)
-
-    lane = lax.broadcasted_iota(jnp.int32, (BAND, LANES), 1)
-    for block in range(bias_ref.shape[0]):
-        rows = slice(block * BAND, (block + 1) * BAND)
-        query = q_ref[rows, :]
-        keys = band_rows(kh_ref, k_ref, block)
-        values = band_rows(vh_ref, v_ref, block)
-        parts = []
-        kept = total_ref[rows, :]
-        for head in range(2):
-            mine = (lane // HEAD_DIM) == head
-            scores = dot_nt(jnp.where(mine, query, 0), keys) * HEAD_DIM ** (-0.5) + bias_ref[block]
-            highest = jnp.max(scores, axis=-1, keepdims=True)
-            raised = jnp.exp(scores - highest)
-            summed = jnp.sum(raised, axis=-1, keepdims=True)
-            weighted = jnp.dot(
-                raised.astype(jnp.bfloat16), values, preferred_element_type=jnp.float32
-            )
-            parts.append(weighted / summed)
-            kept = jnp.where(lane == 2 * pair + head, highest + jnp.log(summed), kept)
-        total_ref[rows, :] = kept
-        out_ref[rows, :] = jnp.where(lane < HEAD_DIM, parts[0], parts[1]).astype(out_ref.dtype)
-
-
-def attention_specs(rows, pairs):
-    whole = lambda pair: (0, 0)
-    return [
-        pl.BlockSpec((rows, LANES), lambda pair: (0, pair)),
-        pl.BlockSpec((rows, LANES), lambda pair: (0, pairs + pair)),
-        pl.BlockSpec((rows, LANES), lambda pair: (0, 2 * pairs + pair)),
-        pl.BlockSpec((BAND, LANES), lambda pair: (0, pair)),
-        pl.BlockSpec((BAND, LANES), lambda pair: (0, pairs + pair)),
-        pl.BlockSpec((rows, 1), whole),
-        pl.BlockSpec((1, rows + BAND), whole),
+        segk_out[:, 0:BAND] = jnp.full((1, BAND), -1, jnp.int32)
+        segk_out[:, BAND:] = window[:, 0:rows_all]
+
+    @pl.when(core == 1)
+    def _():
+        segk_out[...] = window[:, rows_all - BAND :]
+
+    fill_band_bias(segk_out, bias_buf)
+    qv_copy.wait()
+    up_copy.wait()
+    swap_wait(0, tokens_ref, tokens_buf)
+    for tile in tiles:
+        resid[tile, :] = tokens_buf[tile, :].astype(jnp.float32)
+    cot_tick = BEATS_EVERY_TICK + 6
+
+    def tick(t, carry):
+        @pl.when(t <= BEATS_EVERY_TICK)
+        def _():
+            beat(t)
+
+        late = t - BEATS_EVERY_TICK
+
+        @pl.when((late > 0) & (late % 2 == 0))
+        def _():
+            beat(BEATS_EVERY_TICK + late // 2)
+
+        @pl.when(t == cot_tick)
+        def _():
+            swap_start(1, cot_ref, cot_out)
+
+        @pl.when(t + 1 < jobs)
+        def _():
+            prefetch(t + 1)
+
+        job(t)
+        return carry
+
+    lax.fori_loop(0, jobs, tick, 0)
+    for tile in tiles:
+        normed_two[tile, :] = resid[tile, :].astype(low)
+    last_store = store(0, normed_two, out_act_ref)
+    last_store.start()
+    last_store.wait()
+    swap_wait(1, cot_ref, cot_out)
+
+
+def run_forward(tokens, cotangent, segments, weights, biases, out_bias, gain, shift, block):
+    rows, width = tokens.shape
+    layers, hidden_half = weights[-1].shape[0], weights[-1].shape[1]
+    low, wide = jnp.bfloat16, jnp.float32
+    anywhere = pl.BlockSpec(memory_space=pl.ANY)
+    in_vmem = pl.BlockSpec(memory_space=pltpu.VMEM)
+    vmem = pltpu.VMEM
+    units = layers * UNITS_LAYER
+    shape = jax.ShapeDtypeStruct
+    saved = [
+        shape((layers, 2, rows, hidden_half), low),
+        shape((layers, 2, rows, hidden_half), low),
+        shape((layers, rows, width), low),
+        shape((layers, rows, width), wide),
+        shape((layers, 2, rows, block), low),
+        shape((layers, 2, rows, 3 * block), low),
+        shape((layers, 2, 2, BAND, block), low),
+        shape((layers, 2, rows, LANES), wide),
+        shape((layers, rows, width), low),
+        shape((layers, rows, width), wide),
     ]
-
-
-def attention_forward(projected, halo, segq, segk):
-    rows, wide = projected.shape
-    width = wide // 3
-    pairs = width // LANES
+    others = [shape(member.shape, low) for member in weights]
     return pl.pallas_call(
-        attention_forward_kernel,
-        grid=(pairs,),
-        in_specs=attention_specs(rows, pairs),
-        out_specs=[
-            pl.BlockSpec((rows, LANES), lambda pair: (0, pair)),
-            pl.BlockSpec((rows, LANES), lambda pair: (0, 0)),
+        functools.partial(forward_kernel, layers, block, hidden_half),
+        in_specs=[anywhere] * 2 + [in_vmem] + [anywhere] * 4 + [in_vmem] * 5,
+        out_specs=[anywhere] * 2 + [in_vmem] + [anywhere] * (len(others) + len(saved)),
+        out_shape=[
+            shape((rows, width), low),
+            shape((rows, width), low),
+            shape((1, rows + BAND), jnp.int32),
+        ]
+        + others
+        + saved,
+        scratch_shapes=[
+            vmem((rows, width), low),
+            vmem(segments.shape, jnp.int32),
+            vmem(biases[0].shape, wide),
+            vmem(biases[1].shape, wide),
+            vmem((rows, width), wide),
+            vmem((rows, width), wide),
+            vmem((rows, width), low),
+            vmem((rows, width), low),
+            vmem((2, 3, rows, block), low),
+            vmem((layers, 2, 2, BAND, block), low),
+            vmem((2, rows, block), low),
+            vmem((2, rows, LANES), wide),
+            vmem((2, rows, block), low),
+            vmem((2, rows, block), low),
+            vmem((3, width, block), low),
+            vmem((2, block, width), low),
+            vmem((2, width, block), low),
+            vmem((2, block, width), low),
+            vmem((rows // BAND, BAND, 2 * BAND), wide),
+            pltpu.SemaphoreType.DMA((5,)),
+            pltpu.SemaphoreType.DMA((5,)),
+            pltpu.SemaphoreType.DMA((2,)),
+            pltpu.SemaphoreType.DMA((4, units)),
+            pltpu.SemaphoreType.DMA((4, units)),
+            pltpu.SemaphoreType.DMA((layers, 2)),
+            pltpu.SemaphoreType.DMA((layers, 2)),
+            pltpu.SemaphoreType.DMA((2, 2)),
+            pltpu.SemaphoreType.DMA((16,)),
+            pltpu.SemaphoreType.DMA((2, 2)),
         ],
-        out_shape=[
-            jax.ShapeDtypeStruct((rows, width), jnp.bfloat16),
-            jax.ShapeDtypeStruct((rows, LANES), jnp.float32),
-        ],
-        scratch_shapes=[pltpu.VMEM((rows // BAND, BAND, 2 * BAND), jnp.float32)],
-        compiler_params=pltpu.CompilerParams(vmem_limit_bytes=VMEM_ASKED),
-        cost_estimate=pl.CostEstimate(
-            flops=8 * rows * BAND * width, bytes_accessed=10 * rows * width, transcendentals=rows * width * 8
+        compiler_params=pltpu.CompilerParams(
+            collective_id=1, has_side_effects=True, vmem_limit_bytes=VMEM_ASKED
         ),
-        name="attention_forward",
-    )(projected, projected, projected, halo, halo, segq, segk)
-
-
-def swap_dp(array, bit):
-    count = lax.axis_size("dp")
-    return lax.ppermute(array, "dp", [(i, i ^ bit) for i in range(count)])
-
-
-def swap_y(array):
-    return lax.ppermute(array, "tensor", [(0, 1), (1, 0)])
-
-
-def swap_windows(array):
-    pairs = []
-    for group in range(lax.axis_size("dp") // 2):
-        for core in range(2):
-            for y in range(2):
-                pairs.append(((2 * group + core) * 2 + y, (2 * group + y) * 2 + core))
-    return lax.ppermute(array, ("dp", "tensor"), pairs)
-
-
-def half_of(array, bit):
-    rows = array.shape[0] // 2
-    return lax.dynamic_slice_in_dim(array, bit * rows, rows, axis=0)
-
-
-def join_halves(bit, mine, other):
-    return jnp.where(
-        bit == 0, jnp.concatenate([mine, other], axis=0), jnp.concatenate([other, mine], axis=0)
-    )
-
-
-def other_half(array, hops):
-    if not hops:
-        return swap_y(array)
-    bit, place = hops[-1]
-    mine = other_half(half_of(array, place), hops[:-1])
-    return join_halves(place, mine, swap_dp(mine, bit))
+        name="forward",
+    )(tokens, cotangent, segments, *weights, *biases, out_bias, gain, shift)
 
 
 SLOTS = 8
@@ -528,8 +1028,8 @@
     (
         cot_ref,
         gain_ref,
-        segq_ref,
         segk_ref,
+        out_act_ref,
         act_ref,
         slope_ref,
         normed_two_ref,
@@ -548,6 +1048,7 @@
         up_other,
         down_own,
         down_other,
+        out_act_out,
         grad_in_ref,
         out_down,
         out_up,
@@ -598,6 +1099,8 @@
         store_sem,
         vec_send,
         vec_recv,
+        swap_send,
+        swap_recv,
     ) = refs
     half, quarter = block // 2, block // 4
     width = 2 * block
@@ -617,19 +1120,20 @@
     y_partner = {"dp": place, "tensor": 1 - y}
     z_partner = {"dp": place + 4 - 8 * z_low, "tensor": y}
     middle_partner = {"dp": place + 4 * (3 - 2 * z), "tensor": y}
+    swap_partner = {"dp": place + 1 - 2 * core, "tensor": 1 - y}
 
     barrier = pltpu.get_barrier_semaphore()
-    for partner in (core_partner, x_partner, y_partner, z_partner):
+    for partner in (core_partner, x_partner, y_partner, z_partner, swap_partner):
         pl.semaphore_signal(barrier, inc=1, device_id=partner, device_id_type=MESH)
 
     @pl.when(inner == 1)
     def _():
         pl.semaphore_signal(barrier, inc=1, device_id=middle_partner, device_id_type=MESH)
-        pl.semaphore_wait(barrier, 5)
+        pl.semaphore_wait(barrier, 6)
 
     @pl.when(inner == 0)
     def _():
-        pl.semaphore_wait(barrier, 4)
+        pl.semaphore_wait(barrier, 5)
 
     blocks_hidden = hidden_half // block
     plan = (
@@ -711,14 +1215,11 @@
             device_id_type=MESH,
         )
 
-    def rows_at(index, size):
-        return pl.ds(pl.multiple_of(index * size, size), size)
-
     def core_copy(chunk):
         return remote(
             0,
             chunk,
-            part_buf.at[chunk % STAGED, :, rows_at(1 - core, half)],
+            part_buf.at[chunk % STAGED, :, aligned(1 - core, half)],
             core_in.at[chunk % CORE_SLOTS],
             core_partner,
         )
@@ -739,7 +1240,7 @@
         slot = chunk % SLOTS
         return remote(4, chunk, z_kept.at[slot], inner_in.at[slot], middle_partner)
 
-    own_rows = rows_at(2 * core + x, quarter)
+    own_rows = aligned(2 * core + x, quarter)
 
     def back_copy(chunk):
         piece = result.at[chunk % RESULT_SLOTS, own_rows]
@@ -750,7 +1251,7 @@
         return remote(6, chunk, piece, piece, x_partner)
 
     def whole_copy(chunk):
-        piece = result.at[chunk % RESULT_SLOTS, rows_at(core, half)]
+        piece = result.at[chunk % RESULT_SLOTS, aligned(core, half)]
         return remote(7, chunk, piece, piece, core_partner)
 
     def store_copy(chunk, target):
@@ -781,7 +1282,7 @@
     def after_core(chunk):
         slot = chunk % SLOTS
         core_copy(chunk).wait()
-        mine = rows_at(core, half)
+        mine = aligned(core, half)
         other_kept[slot] = added(part_buf[chunk % STAGED, 1, mine, :], core_in[chunk % CORE_SLOTS, 1])
         y_copy(chunk).start()
         own_kept[slot] = added(part_buf[chunk % STAGED, 0, mine, :], core_in[chunk % CORE_SLOTS, 0])
@@ -789,7 +1290,7 @@
     def after_y(chunk):
         slot = chunk % SLOTS
         y_copy(chunk).wait()
-        away, here = rows_at(1 - x, quarter), rows_at(x, quarter)
+        away, here = aligned(1 - x, quarter), aligned(x, quarter)
         x_out[slot] = added(own_kept[slot, away, :], y_in[slot, away, :])
         x_copy(chunk).start()
         x_kept[slot] = added(own_kept[slot, here, :], y_in[slot, here, :])
@@ -844,7 +1345,11 @@
         whole_copy(chunk).wait()
 
         def action(member, layer, i, j):
-            store_copy(chunk, out_refs[member].at[layer, block_of(i), block_of(j)]).start()
+            if member == 3:
+                target = out_qkv.at[layer, j, block_of(i)]
+            else:
+                target = out_refs[member].at[layer, block_of(i), block_of(j)]
+            store_copy(chunk, target).start()
 
         for_matrix(chunk, action)
 
@@ -953,7 +1458,7 @@
 
             @pl.when((step < FFN_STEPS) & (step // (FFN_STEPS // 2) == which))
             def _(which=which, up_ref=up_ref, down_ref=down_ref):
-                cut = rows_at(step % (FFN_STEPS // 2), hidden_step)
+                cut = aligned(step % (FFN_STEPS // 2), hidden_step)
                 for copy in loads(
                     "ffn",
                     slot,
@@ -981,13 +1486,13 @@
             which, inside = pair // pairs_half, pair % pairs_half
 
             def lanes(third):
-                return rows_at(third * pairs_half + inside, LANES)
+                return aligned(third * pairs_half + inside, LANES)
 
             for copy in loads(
                 "attention",
                 slot,
                 *[proj_ref.at[layer, which, :, lanes(third)] for third in range(3)],
-                *[halo_ref.at[layer, which, :, lanes(third)] for third in range(2)],
+                *[halo_ref.at[layer, which, third, :, lanes(0)] for third in range(2)],
                 totals_ref.at[layer, which],
             ):
                 copy.start()
@@ -1001,7 +1506,7 @@
                     @pl.when(index // 3 == which)
                     def _(part=part, index=index, source=source):
                         pltpu.make_async_copy(
-                            source.at[layer, :, block_of(index % 3)],
+                            source.at[layer, index % 3],
                             columns_weight.at[slot, :, pl.ds(part * block, block)],
                             load_sem.at[slot, part],
                         ).start()
@@ -1090,7 +1595,7 @@
 
     def proj_lanes(pair, third):
         which, inside = pair // pairs_half, pair % pairs_half
-        return rows_at(which * 3 * pairs_half + third * pairs_half + inside, LANES)
+        return aligned(which * 3 * pairs_half + third * pairs_half + inside, LANES)
 
     def attention_job(pair, slot):
         wait_loads("attention", slot)
@@ -1099,12 +1604,12 @@
         count = len(tiles)
         key_parts = [None] * (count + 1)
         value_parts = [None] * (count + 1)
-        here = rows_at(pair, LANES)
+        here = aligned(pair, LANES)
         for index, tile in enumerate(tiles):
             query = qkv_buf[slot, 0, tile, :]
             grad = grad_attended[tile, here]
-            keys = band_rows(halo_buf.at[slot, 0], qkv_buf.at[slot, 1], index)
-            values = band_rows(halo_buf.at[slot, 1], qkv_buf.at[slot, 2], index)
+            keys = band_rows(halo_buf[slot, 0], qkv_buf[slot, 1], index)
+            values = band_rows(halo_buf[slot, 1], qkv_buf[slot, 2], index)
             grad_query = []
             grad_keys = 0.0
             grad_values = 0.0
@@ -1171,7 +1676,7 @@
         wait_loads("qkv", slot)
         sums = 0.0
         for tile in tiles:
-            grad = grad_proj[tile, rows_at(step, width)]
+            grad = grad_proj[tile, aligned(step, width)]
             sums = sums + column_sum(grad)
             product = dot_nt(grad, columns_weight[slot])
 
@@ -1240,13 +1745,44 @@
         (LAGS["whole"], after_whole),
     )
 
+    swaps = core + y - 2 * core * y
+
+    def swap_copy(index, source, target):
+        return pltpu.make_async_remote_copy(
+            src_ref=source,
+            dst_ref=target,
+            send_sem=swap_send.at[index],
+            recv_sem=swap_recv.at[index],
+            device_id=swap_partner,
+            device_id_type=MESH,
+        )
+
+    def swap_start(index, source, target):
+        @pl.when(swaps == 1)
+        def _():
+            swap_copy(index, source, target).start()
+
+        @pl.when(swaps == 0)
+        def _():
+            pltpu.make_async_copy(source, target, io_sem.at[1 + index]).start()
+
+    def swap_wait(index, source, target):
+        @pl.when(swaps == 1)
+        def _():
+            swap_copy(index, source, target).wait()
+
+        @pl.when(swaps == 0)
+        def _():
+            pltpu.make_async_copy(source, target, io_sem.at[1 + index]).wait()
+
     first_load = pltpu.make_async_copy(cot_ref, grad_branch, io_sem.at[0])
     first_load.start()
     prefetch(0)
-    fill_band_bias(segq_ref, segk_ref, bias_buf)
+    fill_band_bias(segk_ref, bias_buf)
     first_load.wait()
     for tile in tiles:
         grad_res[tile, :] = grad_branch[tile, :].astype(jnp.float32)
+    swap_start(0, out_act_ref, out_act_out)
     vector_ticks = [jobs + VECTOR_STEP * step for step in range(7)]
 
     def tick(t, carry):
@@ -1274,6 +1810,10 @@
             def _(chunk=chunk, action=action):
                 action(chunk)
 
+        @pl.when(t == jobs)
+        def _():
+            swap_start(1, grad_branch, grad_in_ref)
+
         for step, when in enumerate(vector_ticks):
 
             @pl.when(t == when)
@@ -1283,12 +1823,11 @@
         return carry
 
     lax.fori_loop(0, max(chunks + FIRST + LAGS["stored"], vector_ticks[-1] + 1), tick, 0)
-    last_store = pltpu.make_async_copy(grad_branch, grad_in_ref, io_sem.at[1])
-    last_store.start()
-    last_store.wait()
-
-
-def run_backward(cotangent, gain, segq, segk, saved, weights, block):
+    swap_wait(0, out_act_ref, out_act_out)
+    swap_wait(1, grad_branch, grad_in_ref)
+
+
+def run_backward(cotangent, gain, segk, out_act, saved, weights, block):
     rows, width = cotangent.shape
     layers, hidden_half = weights[-1].shape[0], weights[-1].shape[1]
     half, quarter = block // 2, block // 4
@@ -1301,14 +1840,15 @@
     vmem = pltpu.VMEM
     return pl.pallas_call(
         functools.partial(backward_kernel, layers, block, hidden_half),
-        in_specs=[anywhere] + [in_vmem] * 3 + [anywhere] * (len(saved) + len(weights)),
-        out_specs=[anywhere] * 5 + [in_vmem],
+        in_specs=[anywhere] + [in_vmem] * 2 + [anywhere] * (1 + len(saved) + len(weights)),
+        out_specs=[anywhere] * 6 + [in_vmem],
         out_shape=[
+            jax.ShapeDtypeStruct((rows, width), low),
             jax.ShapeDtypeStruct((rows, width), low),
             jax.ShapeDtypeStruct((layers, hidden_half, width), low),
             jax.ShapeDtypeStruct((layers, width, hidden_half), low),
             jax.ShapeDtypeStruct((layers, block, width), low),
-            jax.ShapeDtypeStruct((layers, width, 3 * block), low),
+            jax.ShapeDtypeStruct((layers, 3, width, block), low),
             jax.ShapeDtypeStruct(vector, wide),
         ],
         scratch_shapes=[
@@ -1347,7 +1887,7 @@
             vmem((RESULT_SLOTS, block, block), low),
             vmem((5,) + vector, wide),
             pltpu.SemaphoreType.DMA((2, 6)),
-            pltpu.SemaphoreType.DMA((2,)),
+            pltpu.SemaphoreType.DMA((3,)),
             pltpu.SemaphoreType.DMA((pairs,)),
             pltpu.SemaphoreType.DMA((pairs,)),
             pltpu.SemaphoreType.DMA((STAGED, 3)),
@@ -1356,16 +1896,14 @@
             pltpu.SemaphoreType.DMA((RESULT_SLOTS,)),
             pltpu.SemaphoreType.DMA((6,)),
             pltpu.SemaphoreType.DMA((6,)),
+            pltpu.SemaphoreType.DMA((2,)),
+            pltpu.SemaphoreType.DMA((2,)),
         ],
         compiler_params=pltpu.CompilerParams(
             collective_id=0, has_side_effects=True, vmem_limit_bytes=VMEM_ASKED
         ),
         name="backward",
-    )(cotangent, gain, segq, segk, *saved, *weights)
-
-
-def dot_low(left, right):
-    return jnp.dot(left, right, preferred_element_type=jnp.float32)
+    )(cotangent, gain, segk, out_act, *saved, *weights)
 
 
 def local_split(
@@ -1383,92 +1921,26 @@
     cotangent,
 ):
     layers, width = w_qkv.shape[0], w_qkv.shape[1]
-    rows = tokens_in.shape[0]
-    place = lax.axis_index("dp")
+    block = w_qkv.shape[3]
     y = lax.axis_index("tensor")
-    core, x = place % 2, (place // 2) % 2
-    hops = [(X_BIT, x), (CORE_BIT, core)]
-
-    residual = swap_windows(tokens_in).astype(jnp.float32)
-    grad_residual = swap_windows(cotangent)
-    window_segments = jnp.where(core == y, segments, swap_dp(segments, CORE_BIT))
-    own_segments = lax.dynamic_slice_in_dim(window_segments, core * rows, rows, axis=1)
-    halo_segments = jnp.where(core == 1, window_segments[:, rows - BAND : rows], -1)
-    segq = own_segments.reshape(rows, 1)
-    segk = jnp.concatenate([halo_segments, own_segments], axis=1)
-
-    qkv_rows = [w_qkv[l].reshape(width, -1) for l in range(layers)]
-    weights = []
-    for l in range(layers):
-        own = (qkv_rows[l], w_out[l], w_up[l], w_down[l])
-        other = tuple(other_half(member, hops) for member in own)
-        bias_own = (qv_bias[l].reshape(-1), up_bias[l])
-        bias_other = tuple(swap_y(member) for member in bias_own)
-        weights.append(tuple(zip(own + bias_own, other + bias_other)))
-
-    kept = []
-    count = lax.axis_size("dp")
-    to_second = [(2 * i, 2 * i + 1) for i in range(count // 2)]
-    to_first = [(2 * i + 1, 2 * i) for i in range(count // 2)]
-    for l in range(layers):
-        qkv, out_w, up, down, qv, upb = weights[l]
-        normed, _, _ = layer_norm(residual, ln_gain[l, 0], ln_bias[l, 0])
-        normed = normed.astype(jnp.bfloat16)
-        saved_attention = []
-        branch = 0.0
-        for half in range(2):
-            third = qkv[half].shape[1] // 3
-            bias = jnp.concatenate(
-                [qv[half][:third], jnp.zeros((third,), jnp.float32), qv[half][third:]]
-            )
-            projected = (dot_low(normed, qkv[half]) + bias).astype(jnp.bfloat16)
-            halo = lax.ppermute(projected[rows - BAND :, third:], "dp", to_second)
-            attended, totals = attention_forward(projected, halo, segq, segk)
-            branch = branch + dot_low(attended, out_w[half])
-            saved_attention.append((projected, halo, attended, totals))
-        middle = residual + branch + out_bias[l, 0]
-        normed_two, _, _ = layer_norm(middle, ln_gain[l, 1], ln_bias[l, 1])
-        normed_two = normed_two.astype(jnp.bfloat16)
-        saved_ffn = []
-        branch = 0.0
-        for half in range(2):
-            before = dot_low(normed_two, up[half]) + upb[half]
-            activated = gelu_tanh(before).astype(jnp.bfloat16)
-            slope = gelu_slope(before).astype(jnp.bfloat16)
-            branch = branch + dot_low(activated, down[half])
-            saved_ffn.append((activated, slope))
-        kept.append((residual, normed, saved_attention, middle, normed_two, saved_ffn))
-        residual = middle + branch + out_bias[l, 1]
-    out_act = swap_windows(residual.astype(jnp.bfloat16))
-
-    def stacked(pick):
-        return jnp.stack([pick(kept[l]) for l in range(layers)])
-
-    def stacked_halves(group, member):
-        return jnp.stack(
-            [jnp.stack([kept[l][group][half][member] for half in range(2)]) for l in range(layers)]
-        )
-
-    saved = (
-        stacked_halves(5, 0),
-        stacked_halves(5, 1),
-        stacked(lambda state: state[4]),
-        stacked(lambda state: state[3]),
-        stacked_halves(2, 2),
-        stacked_halves(2, 0),
-        stacked_halves(2, 1),
-        stacked_halves(2, 3),
-        stacked(lambda state: state[1]),
-        stacked(lambda state: state[0]),
-    )
-    both = []
-    for member in range(4):
-        for half in range(2):
-            both.append(jnp.stack([weights[l][member][half] for l in range(layers)]))
-    grad_in, *reduced, summed = run_backward(
-        grad_residual, ln_gain.reshape(-1, width), segq, segk, saved, both, width // 2
-    )
-    grad_in = swap_windows(grad_in)
+    weights = (w_qkv.transpose(0, 2, 1, 3), w_out, w_up, w_down)
+    gain = ln_gain.reshape(-1, width)
+    out_act, cot, segk, *rest = run_forward(
+        tokens_in,
+        cotangent,
+        segments,
+        weights,
+        (qv_bias.reshape(-1, block), up_bias),
+        out_bias.reshape(-1, width),
+        gain,
+        ln_bias.reshape(-1, width),
+        block,
+    )
+    others, saved = rest[: len(weights)], rest[len(weights) :]
+    both = [member for pair in zip(weights, others) for member in pair]
+    out_act, grad_in, *reduced, summed = run_backward(
+        cot, gain, segk, out_act, saved, both, block
+    )
     summed = summed.reshape(layers, -1)
     hidden = 2 * up_bias.shape[1]
     ends = [2 * width, 2 * width + hidden, 4 * width + hidden, 6 * width + hidden]
@@ -1481,7 +1953,7 @@
     return (
         out_act,
         grad_in,
-        grad_qkv.reshape(w_qkv.shape),
+        grad_qkv.transpose(0, 2, 1, 3),
         grad_qv_bias,
         grad_out,
         grad_up,

time: 893 us -> 570 us (0.64); the launches traced: 883 us -> 569 us
  Pallas kernels: 359 us -> 525 us
  waiting for transfers between devices: 150 us -> 0 us
  other arithmetic: 167 us -> 32.7 us
  local copies, waits for them, and re-layouts: 93.3 us -> 10.5 us
  starting transfers between devices: 56.8 us -> 0 us
  matrix products: 55.2 us -> 0 us
    pallas_call x4 -> x1, Pallas kernels: 32.6 us -> 184 us  [run_forward(): pl.pallas_call(functools.partial(forward_kernel, layers, block, hidden_ha...]
    ppermute x37 -> x0, waiting for transfers between devices: 150 us -> none  [the longest x12 93.2 us: swap_y(): return lax.ppermute(array, 'tensor', [(0, 1), (1, 0)])]
    another operation x34 -> x0, other arithmetic: 89.2 us -> none  [the longest x16 35.3 us: stacked_halves(): jnp.stack([jnp.stack([kept[l][group][half][member] for half in range(2)])...]
    ppermute x37 -> x0, starting transfers between devices: 56.8 us -> none  [the longest x4 22.7 us: swap_windows(): return lax.ppermute(array, ('dp', 'tensor'), pairs)]
    dot_general x16 -> x0, matrix products: 55.2 us -> none  [dot_low(): return jnp.dot(left, right, preferred_element_type=jnp.float32)]
    select_n x18 -> x0, other arithmetic: 49.2 us -> none  [the longest x16 49.2 us: join_halves(): jnp.where(bit == 0, jnp.concatenate([mine, other], axis=0), jnp.concatena...]
    unnamed x158 -> x14, local copies, waits for them, and re-layouts: 31.5 us -> 1.96 us
    slice x15 -> x0, local copies, waits for them, and re-layouts: 24.5 us -> none  [the longest x3 14.4 us: local_split(): own = (qkv_rows[l], w_out[l], w_up[l], w_down[l])]
  transfers between devices with their start and end apart: 37 -> 0, of which waited for: 10 -> 0; matrix products, arithmetic and copies ran while one was open for 33% -> 0% of each run, Pallas kernels for 41% -> 0%
where the time goes in v4:
time: 570 us; the launch traced here: 569 us
  Pallas kernels  525 us (92%)
  other arithmetic  32.7 us (6%)
  local copies, waits for them, and re-layouts  10.5 us (2%)
    pallas_call x1, Pallas kernels, run_backward(): pl.pallas_call(functools.partial(backward_kernel, layers, block, hidden_h...  342 us
    pallas_call x1, Pallas kernels, run_forward(): pl.pallas_call(functools.partial(forward_kernel, layers, block, hidden_ha...  184 us
    convert_element_type x3, other arithmetic, local_split(): member.astype(jnp.float32)  26.2 us

profile of v4, /device:TPU:0, one launch (start us, length us, event | category | flops | bytes accessed | tf_op | source)
XLA Modules:
  0.0 569.1 jit_solution(4019606323168620003)
XLA Ops:
  0.6 1.3 reshape.51.refs_10_.refs_1_
  2.0 1.3 reshape.50.refs_9_
  3.3 1.3 reshape.52.refs_11_
  4.7 1.3 reshape.49.refs_7_
  6.0 183.6 %forward.1 = (bf16[512,1024]{1,0:T(8,128)(2,1)}, bf16[512,1024]{1,0:T(8,128)(2,1)}, s32[1,768]{1,0:T(1,128)}, bf16[2,3,1024,512]{3,2,1,0:T(8,128)(2,1)}, bf16[2,...) custom-call(bf16[512,1024]{1,0:T(8,128)(2,1)} %refs_0_.1, ...), custom_call_target="tpu_custom_call" | custom-call | tf_op jit(solution)/shard_map/forward/pallas_call | solution.py:961
  189.6 341.6 %backward.1 = (bf16[512,1024]{1,0:T(8,128)(2,1)}, bf16[512,1024]{1,0:T(8,128)(2,1)}, bf16[2,2048,1024]{2,1,0:T(8,128)(2,1)}, bf16[2,1024,2048]{2,1,0:T(8,128)(2,...) custom-call(bf16[512,1024]{1,0:T(8,128)(2,1)} %get-tuple-element.35.refs_0_, ...), custom_call_target="tpu_custom_call" | custom-call | tf_op jit(solution)/shard_map/backward/pallas_call | solution.py:1841
  531.2 0.0 slice-start
  531.2 11.8 %convert_element_type.11 = f32[2,1024,2048]{2,1,0:T(8,128)} convert(bf16[2,1024,2048]{2,1,0:T(8,128)(2,1)} %get-tuple-element.57) | non-fusion elementwise | flops 4194304 | bytes 25165824 | tf_op jit(solution)/shard_map/convert_element_type | solution.py:1952
  543.0 0.0 slice-start.1
  543.0 11.8 %convert_element_type.12 = f32[2,2048,1024]{2,1,0:T(8,128)} convert(bf16[2,2048,1024]{2,1,0:T(8,128)(2,1)} %get-tuple-element.58) | non-fusion elementwise | flops 4194304 | bytes 25165824 | tf_op jit(solution)/shard_map/convert_element_type | solution.py:1952
  554.9 0.0 slice-done
  554.9 0.0 slice-done.1
  554.9 0.0 copy-start
  554.9 6.5 %convert_bitcast_fusion = f32[2,1024,3,512]{3,1,2,0:T(8,128)} fusion(bf16[2,3,1024,512]{3,2,1,0:T(8,128)(2,1)S(1)} %bitcast.6), kind=kLoop, calls=%fused_computation | loop fusion | flops 3145728 | bytes 18874368 | tf_op jit(solution)/shard_map/transpose | solution.py:1956
  561.4 0.0 copy-start.3
  561.4 0.0 copy-start.2
  561.4 0.0 copy-start.1
  561.4 0.0 copy-done
  561.4 2.5 convert_element_type.10
  563.9 0.0 copy-done.3
  563.9 0.1 reshape.53
  564.0 0.6 constant_dynamic-slice_fusion.1
  564.6 0.6 reshape.55
  565.3 0.6 reshape.56
  565.9 0.6 reshape.57
  566.5 0.6 constant_dynamic-slice_fusion
  567.1 0.0 copy-done.2
  567.2 1.0 copy.25
  568.1 0.0 copy-done.1
  568.1 1.0 copy.26
  (4 shorter events, 0.0 us)
Async XLA Ops:
  531.2 23.7 %slice-start = ((s8[6291456]{0:T(1024)(128)(4,1)}), s8[4194304]{0:T(1024)(128)(4,1)S(1)}, s32[]{:S(2)}) async-start(s8[6291456]{0:T(1024)(128)(4,1)} %bitcast.5), calls=%async_computation | async-start | bytes 8388608
  543.0 11.9 %slice-start.1 = ((s8[6291456]{0:T(1024)(128)(4,1)}), s8[2097152]{0:T(1024)(128)(4,1)S(1)}, s32[]{:S(2)}) async-start(s8[6291456]{0:T(1024)(128)(4,1)} %bitcast.5), calls=%async_computation.1 | async-start | bytes 4194304
  554.9 6.6 %copy-start = (bf16[2,512,1024]{2,1,0:T(8,128)(2,1)S(1)}, bf16[2,512,1024]{2,1,0:T(8,128)(2,1)}, u32[]{:S(2)}) copy-start(bf16[2,512,1024]{2,1,0:T(8,128)(2,1)} %get-tuple-element.56) | copy-start | bytes 6291460
  561.4 2.5 copy-start.3
  561.4 5.7 %copy-start.2 = (bf16[512,1024]{1,0:T(8,128)(2,1)S(1)}, bf16[512,1024]{1,0:T(8,128)(2,1)}, u32[]{:S(2)}) copy-start(bf16[512,1024]{1,0:T(8,128)(2,1)} %get-tuple-element.74) | copy-start | bytes 3145732
  561.4 6.7 %copy-start.1 = (bf16[512,1024]{1,0:T(8,128)(2,1)S(1)}, bf16[512,1024]{1,0:T(8,128)(2,1)}, u32[]{:S(2)}) copy-start(bf16[512,1024]{1,0:T(8,128)(2,1)} %get-tuple-element.75) | copy-start | bytes 3145732

commit v5 on v4

--- a/solution.py
+++ b/solution.py
@@ -1012,7 +1012,9 @@
 RESULT_SLOTS = 11
 STAGED = 2
 FIRST = 2
-LAGS = dict(core=1, y=3, x=5, outer=7, inner=9, back=11, gather=13, whole=14, stored=15)
+LAGS = dict(
+    core=1, first=3, second=5, third=7, fourth=9, fifth=11, sixth=13, whole=14, stored=15
+)
 VECTOR_STEP = 3
 VECTOR_ROWS = 12
 MESH = pl.DeviceIdType.MESH
@@ -1078,15 +1080,12 @@
         one_buf,
         part_buf,
         core_in,
-        own_kept,
-        other_kept,
-        y_in,
-        x_kept,
-        x_out,
-        x_in,
-        z_kept,
-        outer_in,
-        inner_in,
+        sent,
+        held,
+        kept,
+        first_in,
+        second_in,
+        third_in,
         result,
         vec_in,
         load_sem,
@@ -1215,6 +1214,9 @@
             device_id_type=MESH,
         )
 
+    def x_first(chunk):
+        return ((3 * chunk) % 8 < 3) | (chunk >= chunks - 1)
+
     def core_copy(chunk):
         return remote(
             0,
@@ -1224,35 +1226,46 @@
             core_partner,
         )
 
+    low_middle = z - 1
+    far_middle = 2 - z
+
+    def first_copy(chunk, partner):
+        slot = chunk % SLOTS
+        return remote(1, chunk, sent.at[slot], first_in.at[slot], partner)
+
     def y_copy(chunk):
         slot = chunk % SLOTS
-        return remote(1, chunk, other_kept.at[slot], y_in.at[slot], y_partner)
-
-    def x_copy(chunk):
+        return remote(2, chunk, kept.at[slot, 1], second_in.at[slot, 0], y_partner)
+
+    def pair_copy(chunk):
         slot = chunk % SLOTS
-        return remote(2, chunk, x_out.at[slot], x_in.at[slot], x_partner)
-
-    def outer_copy(chunk):
+        return remote(2, chunk, kept.at[slot], second_in.at[slot], z_partner)
+
+    def single_copy(chunk):
         slot = chunk % SLOTS
-        return remote(3, chunk, z_kept.at[slot], outer_in.at[slot], z_partner)
-
-    def inner_copy(chunk):
+        return remote(3, chunk, kept.at[slot, 0], third_in.at[slot, 0], z_partner)
+
+    def split_copy(chunk):
         slot = chunk % SLOTS
-        return remote(4, chunk, z_kept.at[slot], inner_in.at[slot], middle_partner)
-
-    own_rows = aligned(2 * core + x, quarter)
-
-    def back_copy(chunk):
-        piece = result.at[chunk % RESULT_SLOTS, own_rows]
-        return remote(5, chunk, piece, piece, z_partner)
-
-    def gather_copy(chunk):
-        piece = result.at[chunk % RESULT_SLOTS, own_rows]
-        return remote(6, chunk, piece, piece, x_partner)
-
-    def whole_copy(chunk):
-        piece = result.at[chunk % RESULT_SLOTS, aligned(core, half)]
-        return remote(7, chunk, piece, piece, core_partner)
+        return remote(3, chunk, kept.at[slot, far_middle], third_in.at[slot, 0], middle_partner)
+
+    def middle_copy(chunk):
+        slot = chunk % SLOTS
+        return remote(4, chunk, kept.at[slot, 0], third_in.at[slot, 1], middle_partner)
+
+    def across_copy(chunk):
+        slot = chunk % SLOTS
+        return remote(4, chunk, kept.at[slot, low_middle], third_in.at[slot, 1], x_partner)
+
+    def result_copy(step, chunk, rows, partner):
+        piece = result.at[chunk % RESULT_SLOTS, rows]
+        return remote(step, chunk, piece, piece, partner)
+
+    x_rows = aligned(2 * core + x, quarter)
+    core_rows = aligned(core, half)
+
+    def middle_rows():
+        return aligned(2 * core + low_middle, quarter)
 
     def store_copy(chunk, target):
         slot = chunk % RESULT_SLOTS
@@ -1279,70 +1292,140 @@
 
         core_copy(chunk).start()
 
+    def branch(chunk, by_x, by_y):
+        is_x = x_first(chunk)
+
+        @pl.when(is_x)
+        def _():
+            by_x()
+
+        @pl.when(jnp.logical_not(is_x))
+        def _():
+            by_y()
+
+    def on_middle(action):
+        @pl.when(inner == 1)
+        def _():
+            action()
+
+    def by_place(at_end, at_middle):
+        @pl.when(inner == 0)
+        def _():
+            at_end()
+
+        on_middle(at_middle)
+
     def after_core(chunk):
+        slot, core_slot, part_slot = chunk % SLOTS, chunk % CORE_SLOTS, chunk % STAGED
+        core_copy(chunk).wait()
+        is_x = x_first(chunk).astype(jnp.int32)
+
+        def summed(which, row):
+            near = part_buf[part_slot, which, aligned(2 * core + row, quarter), :]
+            return added(near, core_in[core_slot, which, aligned(row, quarter), :])
+
+        for index in range(2):
+            sent[slot, index] = summed(
+                is_x * index + (1 - is_x), is_x * (1 - x) + (1 - is_x) * index
+            )
+        branch(
+            chunk,
+            lambda: first_copy(chunk, x_partner).start(),
+            lambda: first_copy(chunk, y_partner).start(),
+        )
+        for index in range(2):
+            held[slot, index] = summed(is_x * index, is_x * x + (1 - is_x) * index)
+
+    def after_first(chunk):
         slot = chunk % SLOTS
-        core_copy(chunk).wait()
-        mine = aligned(core, half)
-        other_kept[slot] = added(part_buf[chunk % STAGED, 1, mine, :], core_in[chunk % CORE_SLOTS, 1])
-        y_copy(chunk).start()
-        own_kept[slot] = added(part_buf[chunk % STAGED, 0, mine, :], core_in[chunk % CORE_SLOTS, 0])
-
-    def after_y(chunk):
+        first_copy(chunk, y_partner).wait()
+        for index in (1, 0):
+            kept[slot, index] = added(held[slot, index], first_in[slot, index])
+
+        def by_y():
+            @pl.when(inner == 0)
+            def _():
+                pair_copy(chunk).start()
+
+        branch(chunk, lambda: y_copy(chunk).start(), by_y)
+
+    def after_second(chunk):
         slot = chunk % SLOTS
-        y_copy(chunk).wait()
-        away, here = aligned(1 - x, quarter), aligned(x, quarter)
-        x_out[slot] = added(own_kept[slot, away, :], y_in[slot, away, :])
-        x_copy(chunk).start()
-        x_kept[slot] = added(own_kept[slot, here, :], y_in[slot, here, :])
-
-    def after_x(chunk):
+
+        def by_x():
+            y_copy(chunk).wait()
+            kept[slot, 0] = added(kept[slot, 0], second_in[slot, 0])
+
+            @pl.when(inner == 0)
+            def _():
+                single_copy(chunk).start()
+
+        def at_middle():
+            pair_copy(chunk).wait_recv()
+            kept[slot, far_middle] = added(kept[slot, far_middle], second_in[slot, far_middle])
+            split_copy(chunk).start()
+            kept[slot, low_middle] = added(kept[slot, low_middle], second_in[slot, low_middle])
+
+        branch(chunk, by_x, lambda: by_place(lambda: pair_copy(chunk).wait_send(), at_middle))
+
+    def after_third(chunk):
         slot = chunk % SLOTS
-        x_copy(chunk).wait()
-        z_kept[slot] = added(x_kept[slot], x_in[slot])
-
-        @pl.when(inner == 0)
-        def _():
-            outer_copy(chunk).start()
-
-    def after_outer(chunk):
-        slot = chunk % SLOTS
-
-        @pl.when(inner == 0)
-        def _():
-            outer_copy(chunk).wait_send()
-
-        @pl.when(inner == 1)
-        def _():
-            outer_copy(chunk).wait_recv()
-            z_kept[slot] = added(z_kept[slot], outer_in[slot])
-            inner_copy(chunk).start()
-
-    def after_inner(chunk):
-        slot = chunk % SLOTS
-
-        @pl.when(inner == 1)
-        def _():
-            inner_copy(chunk).wait()
-            result[chunk % RESULT_SLOTS, own_rows, :] = added(z_kept[slot], inner_in[slot])
-            back_copy(chunk).start()
-
-    def after_back(chunk):
-        @pl.when(inner == 0)
-        def _():
-            back_copy(chunk).wait_recv()
-
-        @pl.when(inner == 1)
-        def _():
-            back_copy(chunk).wait_send()
-
-        gather_copy(chunk).start()
-
-    def after_gather(chunk):
-        gather_copy(chunk).wait()
-        whole_copy(chunk).start()
+
+        def one_at_middle():
+            single_copy(chunk).wait_recv()
+            kept[slot, 0] = added(kept[slot, 0], third_in[slot, 0])
+            middle_copy(chunk).start()
+
+        def by_y():
+            split_copy(chunk).wait()
+            kept[slot, low_middle] = added(kept[slot, low_middle], third_in[slot, 0])
+            across_copy(chunk).start()
+
+        branch(
+            chunk,
+            lambda: by_place(lambda: single_copy(chunk).wait_send(), one_at_middle),
+            lambda: on_middle(by_y),
+        )
+
+    def after_fourth(chunk):
+        slot, result_slot = chunk % SLOTS, chunk % RESULT_SLOTS
+
+        def by_x():
+            middle_copy(chunk).wait()
+            result[result_slot, x_rows, :] = added(kept[slot, 0], third_in[slot, 1])
+            result_copy(5, chunk, x_rows, z_partner).start()
+
+        def by_y():
+            across_copy(chunk).wait()
+            result[result_slot, middle_rows(), :] = added(
+                kept[slot, low_middle], third_in[slot, 1]
+            )
+            result_copy(5, chunk, middle_rows(), middle_partner).start()
+
+        branch(chunk, lambda: on_middle(by_x), lambda: on_middle(by_y))
+
+    def after_fifth(chunk):
+        def by_x():
+            back = result_copy(5, chunk, x_rows, z_partner)
+            by_place(back.wait_recv, back.wait_send)
+            result_copy(6, chunk, x_rows, x_partner).start()
+
+        def by_y():
+            result_copy(5, chunk, middle_rows(), middle_partner).wait()
+            result_copy(6, chunk, core_rows, z_partner).start()
+
+        branch(chunk, by_x, lambda: on_middle(by_y))
+
+    def after_sixth(chunk):
+        def by_y():
+            back = result_copy(6, chunk, core_rows, z_partner)
+            by_place(back.wait_recv, back.wait_send)
+
+        branch(chunk, lambda: result_copy(6, chunk, x_rows, x_partner).wait(), by_y)
+        result_copy(7, chunk, core_rows, core_partner).start()
 
     def after_whole(chunk):
-        whole_copy(chunk).wait()
+        result_copy(7, chunk, core_rows, core_partner).wait()
 
         def action(member, layer, i, j):
             if member == 3:
@@ -1359,7 +1442,7 @@
     vector_partners = (core_partner, y_partner, x_partner, z_partner, middle_partner, z_partner)
 
     def vector_copy(step):
-        target = vector_out if step == 5 else vec_in.at[step]
+        target = vec_in.at[min(step, 4)]
         return pltpu.make_async_remote_copy(
             src_ref=vector_out,
             dst_ref=target,
@@ -1415,6 +1498,7 @@
             @pl.when(inner == 0)
             def _():
                 vector_copy(5).wait_recv()
+                vector_out[...] = vec_in[4]
 
     norm_two_step = FFN_STEPS
     out_step = norm_two_step + 1
@@ -1735,12 +1819,12 @@
         (LAGS["core"], after_core),
         (0, multiply),
         (None, job),
-        (LAGS["y"], after_y),
-        (LAGS["x"], after_x),
-        (LAGS["outer"], after_outer),
-        (LAGS["inner"], after_inner),
-        (LAGS["back"], after_back),
-        (LAGS["gather"], after_gather),
+        (LAGS["first"], after_first),
+        (LAGS["second"], after_second),
+        (LAGS["third"], after_third),
+        (LAGS["fourth"], after_fourth),
+        (LAGS["fifth"], after_fifth),
+        (LAGS["sixth"], after_sixth),
         (LAGS["stored"], after_store),
         (LAGS["whole"], after_whole),
     )
@@ -1875,15 +1959,12 @@
             vmem((STAGED, rows, block), low),
             vmem((STAGED, 2, block, block), low),
             vmem((CORE_SLOTS, 2, half, block), low),
-            vmem((SLOTS, half, block), low),
-            vmem((SLOTS, half, block), low),
-            vmem((SLOTS, half, block), low),
-            vmem((SLOTS, quarter, block), low),
-            vmem((SLOTS, quarter, block), low),
-            vmem((SLOTS, quarter, block), low),
-            vmem((SLOTS, quarter, block), low),
-            vmem((SLOTS, quarter, block), low),
-            vmem((SLOTS, quarter, block), low),
+            vmem((SLOTS, 2, quarter, block), low),
+            vmem((SLOTS, 2, quarter, block), low),
+            vmem((SLOTS, 2, quarter, block), low),
+            vmem((SLOTS, 2, quarter, block), low),
+            vmem((SLOTS, 2, quarter, block), low),
+            vmem((SLOTS, 2, quarter, block), low),
             vmem((RESULT_SLOTS, block, block), low),
             vmem((5,) + vector, wide),
             pltpu.SemaphoreType.DMA((2, 6)),

time: 570 us -> 543 us (0.953)
  Pallas kernels: 525 us -> 498 us
    pallas_call x1, Pallas kernels: 342 us -> 315 us  [run_backward(): pl.pallas_call(functools.partial(backward_kernel, layers, block, hidden_h...]
where the time goes in v5:
time: 543 us; the launch traced here: 542 us
  Pallas kernels  498 us (92%)
  other arithmetic  32.7 us (6%)
  local copies, waits for them, and re-layouts  10.5 us (2%)
    pallas_call x1, Pallas kernels, run_backward(): pl.pallas_call(functools.partial(backward_kernel, layers, block, hidden_h...  315 us
    pallas_call x1, Pallas kernels, run_forward(): pl.pallas_call(functools.partial(forward_kernel, layers, block, hidden_ha...  184 us
    convert_element_type x3, other arithmetic, local_split(): member.astype(jnp.float32)  26.2 us

profile of v5, /device:TPU:0, one launch (start us, length us, event | category | flops | bytes accessed | tf_op | source)
XLA Modules:
  0.0 542.1 jit_solution(10137351213786288319)
XLA Ops:
  0.6 1.3 reshape.51.refs_10_.refs_1_
  2.0 1.3 reshape.50.refs_9_
  3.3 1.3 reshape.52.refs_11_
  4.7 1.3 reshape.49.refs_7_
  6.0 183.6 %forward.1 = (bf16[512,1024]{1,0:T(8,128)(2,1)}, bf16[512,1024]{1,0:T(8,128)(2,1)}, s32[1,768]{1,0:T(1,128)}, bf16[2,3,1024,512]{3,2,1,0:T(8,128)(2,1)}, bf16[2,...) custom-call(bf16[512,1024]{1,0:T(8,128)(2,1)} %refs_0_.1, ...), custom_call_target="tpu_custom_call" | custom-call | tf_op jit(solution)/shard_map/forward/pallas_call | solution.py:961
  189.6 314.6 %backward.1 = (bf16[512,1024]{1,0:T(8,128)(2,1)}, bf16[512,1024]{1,0:T(8,128)(2,1)}, bf16[2,2048,1024]{2,1,0:T(8,128)(2,1)}, bf16[2,1024,2048]{2,1,0:T(8,128)(2,...) custom-call(bf16[512,1024]{1,0:T(8,128)(2,1)} %get-tuple-element.35.refs_0_, ...), custom_call_target="tpu_custom_call" | custom-call | tf_op jit(solution)/shard_map/backward/pallas_call | solution.py:1925
  504.2 0.0 slice-start
  504.2 11.8 %convert_element_type.11 = f32[2,1024,2048]{2,1,0:T(8,128)} convert(bf16[2,1024,2048]{2,1,0:T(8,128)(2,1)} %get-tuple-element.57) | non-fusion elementwise | flops 4194304 | bytes 25165824 | tf_op jit(solution)/shard_map/convert_element_type | solution.py:2033
  516.1 0.0 slice-start.1
  516.1 11.8 %convert_element_type.12 = f32[2,2048,1024]{2,1,0:T(8,128)} convert(bf16[2,2048,1024]{2,1,0:T(8,128)(2,1)} %get-tuple-element.58) | non-fusion elementwise | flops 4194304 | bytes 25165824 | tf_op jit(solution)/shard_map/convert_element_type | solution.py:2033
  527.9 0.0 slice-done
  527.9 0.0 slice-done.1
  527.9 0.0 copy-start
  527.9 6.5 %convert_bitcast_fusion = f32[2,1024,3,512]{3,1,2,0:T(8,128)} fusion(bf16[2,3,1024,512]{3,2,1,0:T(8,128)(2,1)S(1)} %bitcast.6), kind=kLoop, calls=%fused_computation | loop fusion | flops 3145728 | bytes 18874368 | tf_op jit(solution)/shard_map/transpose | solution.py:2037
  534.5 0.0 copy-start.3
  534.5 0.0 copy-start.2
  534.5 0.0 copy-start.1
  534.5 0.0 copy-done
  534.5 2.5 convert_element_type.10
  537.0 0.0 copy-done.3
  537.0 0.1 reshape.53
  537.1 0.6 constant_dynamic-slice_fusion.1
  537.7 0.6 reshape.55
  538.3 0.6 reshape.56
  539.0 0.6 reshape.57
  539.6 0.6 constant_dynamic-slice_fusion
  540.2 0.0 copy-done.2
  540.2 1.0 copy.25
  541.2 0.0 copy-done.1
  541.2 1.0 copy.26
  (4 shorter events, 0.0 us)
Async XLA Ops:
  504.2 23.7 %slice-start = ((s8[6291456]{0:T(1024)(128)(4,1)}), s8[4194304]{0:T(1024)(128)(4,1)S(1)}, s32[]{:S(2)}) async-start(s8[6291456]{0:T(1024)(128)(4,1)} %bitcast.5), calls=%async_computation | async-start | bytes 8388608
  516.1 11.9 %slice-start.1 = ((s8[6291456]{0:T(1024)(128)(4,1)}), s8[2097152]{0:T(1024)(128)(4,1)S(1)}, s32[]{:S(2)}) async-start(s8[6291456]{0:T(1024)(128)(4,1)} %bitcast.5), calls=%async_computation.1 | async-start | bytes 4194304
  527.9 6.6 %copy-start = (bf16[2,512,1024]{2,1,0:T(8,128)(2,1)S(1)}, bf16[2,512,1024]{2,1,0:T(8,128)(2,1)}, u32[]{:S(2)}) copy-start(bf16[2,512,1024]{2,1,0:T(8,128)(2,1)} %get-tuple-element.56) | copy-start | bytes 6291460
  534.5 2.5 copy-start.3
  534.5 5.7 %copy-start.2 = (bf16[512,1024]{1,0:T(8,128)(2,1)S(1)}, bf16[512,1024]{1,0:T(8,128)(2,1)}, u32[]{:S(2)}) copy-start(bf16[512,1024]{1,0:T(8,128)(2,1)} %get-tuple-element.74) | copy-start | bytes 3145732
  534.5 6.7 %copy-start.1 = (bf16[512,1024]{1,0:T(8,128)(2,1)S(1)}, bf16[512,1024]{1,0:T(8,128)(2,1)}, u32[]{:S(2)}) copy-start(bf16[512,1024]{1,0:T(8,128)(2,1)} %get-tuple-element.75) | copy-start | bytes 3145732

commit v6 on v5

--- a/solution.py
+++ b/solution.py
@@ -678,8 +678,8 @@
     fine_tiles = [slice(r, r + LANES) for r in range(0, rows_all, LANES)]
 
     def normalize(layer, index, target):
-        gain = gain_ref[pl.ds(2 * layer + index, 1), :]
-        shift = shift_ref[pl.ds(2 * layer + index, 1), :]
+        gain = gain_ref[layer, pl.ds(index, 1), :]
+        shift = shift_ref[layer, pl.ds(index, 1), :]
         for tile in fine_tiles:
             values, _, _ = layer_norm(resid[tile, :], gain, shift)
             target[tile, :] = values.astype(low)
@@ -745,7 +745,7 @@
             for tile in tiles:
                 product = dot_low(normed[tile, :], qkv_weight[third])
                 if third != 1:
-                    product = product + bias[pl.ds(2 * layer + third // 2, 1), :]
+                    product = product + bias[layer, pl.ds(third // 2, 1), :]
                 proj[which, third, tile, :] = product.astype(low)
 
         @pl.when(core == 0)
@@ -799,7 +799,7 @@
         for which in range(2):
             wait_all(proj_stores(layer, which))
             halo_store(layer, which).wait()
-        bias = out_bias_ref[pl.ds(2 * layer, 1), :]
+        bias = out_bias_ref[layer, pl.ds(0, 1), :]
         for tile in tiles:
             branch = dot_low(attended[0, tile, :], out_weight[0])
             branch = branch + dot_low(attended[1, tile, :], out_weight[1])
@@ -854,7 +854,7 @@
         wait_all(second_stores(layer))
         for which in range(2):
             wait_all(attended_stores(layer, which))
-        bias = out_bias_ref[pl.ds(2 * layer + 1, 1), :]
+        bias = out_bias_ref[layer, pl.ds(1, 1), :]
         for tile in tiles:
             resid[tile, :] = resid[tile, :] + collected[tile, :] + bias
 
@@ -1011,7 +1011,7 @@
 CORE_SLOTS = 4
 RESULT_SLOTS = 11
 STAGED = 2
-FIRST = 2
+FIRST = 0
 LAGS = dict(
     core=1, first=3, second=5, third=7, fourth=9, fifth=11, sixth=13, whole=14, stored=15
 )
@@ -1215,7 +1215,7 @@
         )
 
     def x_first(chunk):
-        return ((3 * chunk) % 8 < 3) | (chunk >= chunks - 1)
+        return ((5 * chunk) % 8 < 3) | (chunk >= chunks - 1)
 
     def core_copy(chunk):
         return remote(
@@ -1633,7 +1633,7 @@
 
     def norm_job(layer, index, slot):
         wait_loads("wide", slot)
-        gain = gain_ref[pl.ds(2 * layer + index, 1), :]
+        gain = gain_ref[layer, pl.ds(index, 1), :]
         gain_sum, shift_sum, attn_sum, branch_sum = 0.0, 0.0, 0.0, 0.0
         for tile in fine_tiles:
             incoming = collected[tile, :]
@@ -1866,6 +1866,7 @@
     first_load.wait()
     for tile in tiles:
         grad_res[tile, :] = grad_branch[tile, :].astype(jnp.float32)
+    stage_operands(0)
     swap_start(0, out_act_ref, out_act_out)
     vector_ticks = [jobs + VECTOR_STEP * step for step in range(7)]
 
@@ -1876,7 +1877,7 @@
 
         ahead = t + 1 - FIRST
 
-        @pl.when((ahead >= 0) & (ahead < chunks))
+        @pl.when((ahead > 0) & (ahead < chunks))
         def _():
             stage_operands(ahead)
 
@@ -1894,7 +1895,7 @@
             def _(chunk=chunk, action=action):
                 action(chunk)
 
-        @pl.when(t == jobs)
+        @pl.when(t == chunks + FIRST + LAGS["second"] - 1)
         def _():
             swap_start(1, grad_branch, grad_in_ref)
 
@@ -1987,6 +1988,120 @@
     )(cotangent, gain, segk, out_act, *saved, *weights)
 
 
+FINISH_DEPTH = 4
+
+
+def finish_kernel(layers, copies, steps, *refs):
+    count = len(steps)
+    ins, refs = refs[:count], refs[count:]
+    vector_ref, refs = refs[0], refs[1:]
+    copy_ins, refs = refs[:copies], refs[copies:]
+    outs, refs = refs[:count], refs[count:]
+    qv_out, up_out, bias_out, gain_out, shift_out = refs[:5]
+    copy_outs, refs = refs[5 : 5 + copies], refs[5 + copies :]
+    in_bufs, refs = refs[:count], refs[count:]
+    out_bufs, (in_sem, out_sem, copy_sem) = refs[:count], refs[count:]
+    moved = [
+        pltpu.make_async_copy(source, target, copy_sem.at[index])
+        for index, (source, target) in enumerate(zip(copy_ins, copy_outs))
+    ]
+    for copy in moved:
+        copy.start()
+    plan = []
+    for member, (rows, parts) in enumerate(steps):
+        for layer in range(layers):
+            for part in range(parts):
+                plan.append((member, layer, part * rows, rows, (layer * parts + part) % FINISH_DEPTH))
+
+    def view(ref, layer, begin, rows):
+        if len(ref.shape) == 4:
+            return ref.at[layer, begin // rows]
+        return ref.at[layer, pl.ds(begin, rows)]
+
+    def load(entry):
+        member, layer, begin, rows, slot = entry
+        return pltpu.make_async_copy(
+            view(ins[member], layer, begin, rows), in_bufs[member].at[slot], in_sem.at[member, slot]
+        )
+
+    def save(entry):
+        member, layer, begin, rows, slot = entry
+        return pltpu.make_async_copy(
+            out_bufs[member].at[slot], view(outs[member], layer, begin, rows), out_sem.at[member, slot]
+        )
+
+    for entry in plan[:FINISH_DEPTH]:
+        load(entry).start()
+    y = lax.axis_index("tensor")
+    half = qv_out.shape[2]
+    for layer in range(layers):
+        base = layer * VECTOR_ROWS
+        for index in range(2):
+            mine = pl.ds(pl.multiple_of(y * half, half), half)
+            qv_out[layer, pl.ds(index, 1), :] = vector_ref[pl.ds(base + index, 1), mine]
+            width = vector_ref.shape[1]
+            up_out[pl.ds(layer, 1), index * width : (index + 1) * width] = vector_ref[
+                pl.ds(base + 2 + 2 * y + index, 1), :
+            ]
+            for row, target in ((6, bias_out), (8, gain_out), (10, shift_out)):
+                target[layer, pl.ds(index, 1), :] = vector_ref[pl.ds(base + row + index, 1), :]
+    busy = {}
+    for place, entry in enumerate(plan):
+        member, slot = entry[0], entry[4]
+        load(entry).wait()
+        if (member, slot) in busy:
+            save(busy.pop((member, slot))).wait()
+        out_bufs[member][slot] = in_bufs[member][slot].astype(jnp.float32)
+        save(entry).start()
+        busy[(member, slot)] = entry
+        if place + FINISH_DEPTH < len(plan):
+            load(plan[place + FINISH_DEPTH]).start()
+    for entry in busy.values():
+        save(entry).wait()
+    for copy in moved:
+        copy.wait()
+
+
+def run_finish(reduced, vector, whole, block):
+    layers, width = reduced[0].shape[0], vector.shape[1]
+    hidden_half = reduced[0].shape[1]
+    wide, low = jnp.float32, jnp.bfloat16
+    shape = jax.ShapeDtypeStruct
+    anywhere = pl.BlockSpec(memory_space=pl.ANY)
+    in_vmem = pl.BlockSpec(memory_space=pltpu.VMEM)
+    steps = (
+        (block, hidden_half // block),
+        (block // 2, width * 2 // block),
+        (block, 1),
+        (width, 3),
+    )
+    blocks = ((block, width), (block // 2, hidden_half), (block, width), (width, block))
+    deep = lambda kind: [pltpu.VMEM((FINISH_DEPTH,) + size, kind) for size in blocks]
+    return pl.pallas_call(
+        functools.partial(finish_kernel, layers, len(whole), steps),
+        in_specs=[anywhere] * len(reduced) + [in_vmem] + [anywhere] * len(whole),
+        out_specs=[anywhere] * len(reduced) + [in_vmem] * 5 + [anywhere] * len(whole),
+        out_shape=[shape(member.shape, wide) for member in reduced]
+        + [
+            shape((layers, 2, block), wide),
+            shape((layers, hidden_half), wide),
+            shape((layers, 2, width), wide),
+            shape((layers, 2, width), wide),
+            shape((layers, 2, width), wide),
+        ]
+        + [shape(member.shape, member.dtype) for member in whole],
+        scratch_shapes=deep(low)
+        + deep(wide)
+        + [
+            pltpu.SemaphoreType.DMA((4, FINISH_DEPTH)),
+            pltpu.SemaphoreType.DMA((4, FINISH_DEPTH)),
+            pltpu.SemaphoreType.DMA((len(whole),)),
+        ],
+        compiler_params=pltpu.CompilerParams(vmem_limit_bytes=VMEM_ASKED),
+        name="finish",
+    )(*reduced, vector, *whole)
+
+
 def local_split(
     tokens_in,
     segments,
@@ -2001,48 +2116,40 @@
     ln_bias,
     cotangent,
 ):
-    layers, width = w_qkv.shape[0], w_qkv.shape[1]
     block = w_qkv.shape[3]
-    y = lax.axis_index("tensor")
     weights = (w_qkv.transpose(0, 2, 1, 3), w_out, w_up, w_down)
-    gain = ln_gain.reshape(-1, width)
     out_act, cot, segk, *rest = run_forward(
         tokens_in,
         cotangent,
         segments,
         weights,
-        (qv_bias.reshape(-1, block), up_bias),
-        out_bias.reshape(-1, width),
-        gain,
-        ln_bias.reshape(-1, width),
+        (qv_bias, up_bias),
+        out_bias,
+        ln_gain,
+        ln_bias,
         block,
     )
     others, saved = rest[: len(weights)], rest[len(weights) :]
     both = [member for pair in zip(weights, others) for member in pair]
     out_act, grad_in, *reduced, summed = run_backward(
-        cot, gain, segk, out_act, saved, both, block
-    )
-    summed = summed.reshape(layers, -1)
-    hidden = 2 * up_bias.shape[1]
-    ends = [2 * width, 2 * width + hidden, 4 * width + hidden, 6 * width + hidden]
-    qv_sum = summed[:, : ends[0]].reshape(layers, 2, width)
-    grad_qv_bias = lax.dynamic_slice_in_dim(qv_sum, y * (width // 2), width // 2, axis=2)
-    grad_up_bias = lax.dynamic_slice_in_dim(
-        summed[:, ends[0] : ends[1]], y * (hidden // 2), hidden // 2, axis=1
-    )
-    grad_down, grad_up, grad_out, grad_qkv = [member.astype(jnp.float32) for member in reduced]
+        cot, ln_gain, segk, out_act, saved, both, block
+    )
+    *grads, grad_qv, grad_up_bias, grad_bias, grad_gain, grad_shift, out_act, grad_in = run_finish(
+        reduced, summed, (out_act, grad_in), block
+    )
+    grad_down, grad_up, grad_out, grad_qkv = grads
     return (
         out_act,
         grad_in,
         grad_qkv.transpose(0, 2, 1, 3),
-        grad_qv_bias,
+        grad_qv,
         grad_out,
         grad_up,
         grad_up_bias,
         grad_down,
-        summed[:, ends[1] : ends[2]].reshape(layers, 2, width),
-        summed[:, ends[2] : ends[3]].reshape(layers, 2, width),
-        summed[:, ends[3] :].reshape(layers, 2, width),
+        grad_bias,
+        grad_gain,
+        grad_shift,
     )
 
 

time: 543 us -> 552 us (1.017)
  Pallas kernels: 498 us -> 551 us
  other arithmetic: 32.7 us -> 0 us
  local copies, waits for them, and re-layouts: 10.5 us -> 0 us
    pallas_call x0 -> x1, Pallas kernels: none -> 66.5 us  [run_finish(): pl.pallas_call(functools.partial(finish_kernel, layers, len(whole), steps...]
    convert_element_type x3 -> x0, other arithmetic: 26.2 us -> none  [local_split(): member.astype(jnp.float32)]
    pallas_call x1, Pallas kernels: 315 us -> 301 us  [run_backward(): pl.pallas_call(functools.partial(backward_kernel, layers, block, hidden_h...]
    reshape x9 -> x0, local copies, waits for them, and re-layouts: 7.34 us -> none  [the longest x1 1.34 us: local_split(): gain = ln_gain.reshape(-1, width)]
    transpose x1 -> x0, other arithmetic: 6.54 us -> none  [local_split(): grad_qkv.transpose(0, 2, 1, 3)]
where the time goes in v6:
time: 552 us
  Pallas kernels  551 us (100%)
    pallas_call x1, Pallas kernels, run_backward(): pl.pallas_call(functools.partial(backward_kernel, layers, block, hidden_h...  301 us
    pallas_call x1, Pallas kernels, run_forward(): pl.pallas_call(functools.partial(forward_kernel, layers, block, hidden_ha...  184 us
    pallas_call x1, Pallas kernels, run_finish(): pl.pallas_call(functools.partial(finish_kernel, layers, len(whole), steps...  66.5 us

profile of v6, /device:TPU:0, one launch (start us, length us, event | category | flops | bytes accessed | tf_op | source)
XLA Modules:
  0.0 551.6 jit_solution(7671013641187385405)
XLA Ops:
  0.6 183.6 %forward.1 = (bf16[512,1024]{1,0:T(8,128)(2,1)}, bf16[512,1024]{1,0:T(8,128)(2,1)}, s32[1,768]{1,0:T(1,128)}, bf16[2,3,1024,512]{3,2,1,0:T(8,128)(2,1)}, bf16[2,...) custom-call(bf16[512,1024]{1,0:T(8,128)(2,1)} %refs_0_.1, ...), custom_call_target="tpu_custom_call" | custom-call | tf_op jit(solution)/shard_map/forward/pallas_call | solution.py:961
  184.3 300.7 %backward.1 = (bf16[512,1024]{1,0:T(8,128)(2,1)}, bf16[512,1024]{1,0:T(8,128)(2,1)}, bf16[2,2048,1024]{2,1,0:T(8,128)(2,1)}, bf16[2,1024,2048]{2,1,0:T(8,128)(2,...) custom-call(bf16[512,1024]{1,0:T(8,128)(2,1)} %get-tuple-element.46.refs_0_, ...), custom_call_target="tpu_custom_call" | custom-call | tf_op jit(solution)/shard_map/backward/pallas_call | solution.py:1926
  485.0 66.5 %finish.1 = (f32[2,2048,1024]{2,1,0:T(8,128)}, f32[2,1024,2048]{2,1,0:T(8,128)}, f32[2,512,1024]{2,1,0:T(8,128)}, f32[2,3,1024,512]{3,2,1,0:T(8,128)}, f32[2,2,5...) custom-call(bf16[2,2048,1024]{2,1,0:T(8,128)(2,1)} %get-tuple-elemen, ...), custom_call_target="tpu_custom_call" | custom-call | tf_op jit(solution)/shard_map/finish/pallas_call | solution.py:2080

commit v7 on v6

--- a/solution.py
+++ b/solution.py
@@ -515,7 +515,7 @@
 
         @pl.when(swaps == 0)
         def _():
-            pltpu.make_async_copy(source, target, swap_sem.at[index]).start()
+            pltpu.make_async_copy(source, tokens_buf, swap_sem.at[index]).start()
 
     def swap_wait(index, source, target):
         @pl.when(swaps == 1)
@@ -524,7 +524,7 @@
 
         @pl.when(swaps == 0)
         def _():
-            pltpu.make_async_copy(source, target, swap_sem.at[index]).wait()
+            pltpu.make_async_copy(source, tokens_buf, swap_sem.at[index]).wait()
 
     segments_copy = remote(
         segments_ref, segments_in, start_send.at[2], start_recv.at[2], core_partner
@@ -919,6 +919,11 @@
         @pl.when(t == cot_tick)
         def _():
             swap_start(1, cot_ref, cot_out)
+
+        @pl.when((t == cot_tick + 4) & (swaps == 0))
+        def _():
+            pltpu.make_async_copy(cot_ref, tokens_buf, swap_sem.at[1]).wait()
+            pltpu.make_async_copy(tokens_buf, cot_out, swap_sem.at[1]).start()
 
         @pl.when(t + 1 < jobs)
         def _():
@@ -1846,18 +1851,22 @@
         def _():
             swap_copy(index, source, target).start()
 
-        @pl.when(swaps == 0)
-        def _():
-            pltpu.make_async_copy(source, target, io_sem.at[1 + index]).start()
+        if index:
+
+            @pl.when(swaps == 0)
+            def _():
+                pltpu.make_async_copy(source, target, io_sem.at[1]).start()
 
     def swap_wait(index, source, target):
         @pl.when(swaps == 1)
         def _():
             swap_copy(index, source, target).wait()
 
-        @pl.when(swaps == 0)
-        def _():
-            pltpu.make_async_copy(source, target, io_sem.at[1 + index]).wait()
+        if index:
+
+            @pl.when(swaps == 0)
+            def _():
+                pltpu.make_async_copy(source, target, io_sem.at[1]).wait()
 
     first_load = pltpu.make_async_copy(cot_ref, grad_branch, io_sem.at[0])
     first_load.start()
@@ -1969,7 +1978,7 @@
             vmem((RESULT_SLOTS, block, block), low),
             vmem((5,) + vector, wide),
             pltpu.SemaphoreType.DMA((2, 6)),
-            pltpu.SemaphoreType.DMA((3,)),
+            pltpu.SemaphoreType.DMA((2,)),
             pltpu.SemaphoreType.DMA((pairs,)),
             pltpu.SemaphoreType.DMA((pairs,)),
             pltpu.SemaphoreType.DMA((STAGED, 3)),
@@ -1991,22 +2000,34 @@
 FINISH_DEPTH = 4
 
 
-def finish_kernel(layers, copies, steps, *refs):
+def finish_kernel(layers, steps, *refs):
     count = len(steps)
     ins, refs = refs[:count], refs[count:]
     vector_ref, refs = refs[0], refs[1:]
-    copy_ins, refs = refs[:copies], refs[copies:]
+    (act_own, act_swapped, grad_in_ref), refs = refs[:3], refs[3:]
     outs, refs = refs[:count], refs[count:]
     qv_out, up_out, bias_out, gain_out, shift_out = refs[:5]
-    copy_outs, refs = refs[5 : 5 + copies], refs[5 + copies :]
+    (act_out, grad_in_out), refs = refs[5:7], refs[7:]
     in_bufs, refs = refs[:count], refs[count:]
-    out_bufs, (in_sem, out_sem, copy_sem) = refs[:count], refs[count:]
-    moved = [
-        pltpu.make_async_copy(source, target, copy_sem.at[index])
-        for index, (source, target) in enumerate(zip(copy_ins, copy_outs))
-    ]
-    for copy in moved:
-        copy.start()
+    out_bufs, (moved_buf, in_sem, out_sem, copy_sem) = refs[:count], refs[count:]
+    y = lax.axis_index("tensor")
+    core = lax.axis_index("dp") % 2
+
+    def fetch(index, source):
+        return pltpu.make_async_copy(source, moved_buf.at[index], copy_sem.at[index])
+
+    def put(index, target):
+        return pltpu.make_async_copy(moved_buf.at[index], target, copy_sem.at[index])
+
+    @pl.when(core == y)
+    def _():
+        fetch(0, act_own).start()
+
+    @pl.when(core != y)
+    def _():
+        fetch(0, act_swapped).start()
+
+    fetch(1, grad_in_ref).start()
     plan = []
     for member, (rows, parts) in enumerate(steps):
         for layer in range(layers):
@@ -2032,7 +2053,6 @@
 
     for entry in plan[:FINISH_DEPTH]:
         load(entry).start()
-    y = lax.axis_index("tensor")
     half = qv_out.shape[2]
     for layer in range(layers):
         base = layer * VECTOR_ROWS
@@ -2045,6 +2065,9 @@
             ]
             for row, target in ((6, bias_out), (8, gain_out), (10, shift_out)):
                 target[layer, pl.ds(index, 1), :] = vector_ref[pl.ds(base + row + index, 1), :]
+    for index, target in enumerate((act_out, grad_in_out)):
+        fetch(index, target).wait()
+        put(index, target).start()
     busy = {}
     for place, entry in enumerate(plan):
         member, slot = entry[0], entry[4]
@@ -2058,11 +2081,11 @@
             load(plan[place + FINISH_DEPTH]).start()
     for entry in busy.values():
         save(entry).wait()
-    for copy in moved:
-        copy.wait()
-
-
-def run_finish(reduced, vector, whole, block):
+    for index, target in enumerate((act_out, grad_in_out)):
+        put(index, target).wait()
+
+
+def run_finish(reduced, vector, acts, grad_in, block):
     layers, width = reduced[0].shape[0], vector.shape[1]
     hidden_half = reduced[0].shape[1]
     wide, low = jnp.float32, jnp.bfloat16
@@ -2078,9 +2101,9 @@
     blocks = ((block, width), (block // 2, hidden_half), (block, width), (width, block))
     deep = lambda kind: [pltpu.VMEM((FINISH_DEPTH,) + size, kind) for size in blocks]
     return pl.pallas_call(
-        functools.partial(finish_kernel, layers, len(whole), steps),
-        in_specs=[anywhere] * len(reduced) + [in_vmem] + [anywhere] * len(whole),
-        out_specs=[anywhere] * len(reduced) + [in_vmem] * 5 + [anywhere] * len(whole),
+        functools.partial(finish_kernel, layers, steps),
+        in_specs=[anywhere] * len(reduced) + [in_vmem] + [anywhere] * 3,
+        out_specs=[anywhere] * len(reduced) + [in_vmem] * 5 + [anywhere] * 2,
         out_shape=[shape(member.shape, wide) for member in reduced]
         + [
             shape((layers, 2, block), wide),
@@ -2089,17 +2112,18 @@
             shape((layers, 2, width), wide),
             shape((layers, 2, width), wide),
         ]
-        + [shape(member.shape, member.dtype) for member in whole],
+        + [shape(grad_in.shape, low)] * 2,
         scratch_shapes=deep(low)
         + deep(wide)
         + [
+            pltpu.VMEM((2,) + grad_in.shape, low),
             pltpu.SemaphoreType.DMA((4, FINISH_DEPTH)),
             pltpu.SemaphoreType.DMA((4, FINISH_DEPTH)),
-            pltpu.SemaphoreType.DMA((len(whole),)),
+            pltpu.SemaphoreType.DMA((2,)),
         ],
         compiler_params=pltpu.CompilerParams(vmem_limit_bytes=VMEM_ASKED),
         name="finish",
-    )(*reduced, vector, *whole)
+    )(*reduced, vector, *acts, grad_in)
 
 
 def local_split(
@@ -2118,7 +2142,7 @@
 ):
     block = w_qkv.shape[3]
     weights = (w_qkv.transpose(0, 2, 1, 3), w_out, w_up, w_down)
-    out_act, cot, segk, *rest = run_forward(
+    act_own, cot, segk, *rest = run_forward(
         tokens_in,
         cotangent,
         segments,
@@ -2131,11 +2155,11 @@
     )
     others, saved = rest[: len(weights)], rest[len(weights) :]
     both = [member for pair in zip(weights, others) for member in pair]
-    out_act, grad_in, *reduced, summed = run_backward(
-        cot, ln_gain, segk, out_act, saved, both, block
+    act_swapped, grad_in, *reduced, summed = run_backward(
+        cot, ln_gain, segk, act_own, saved, both, block
     )
     *grads, grad_qv, grad_up_bias, grad_bias, grad_gain, grad_shift, out_act, grad_in = run_finish(
-        reduced, summed, (out_act, grad_in), block
+        reduced, summed, (act_own, act_swapped), grad_in, block
     )
     grad_down, grad_up, grad_out, grad_qkv = grads
     return (

time: 552 us -> 514 us (0.931)
  Pallas kernels: 551 us -> 513 us
    pallas_call x1, Pallas kernels: 66.5 us -> 28.3 us  [run_finish(): pl.pallas_call(functools.partial(finish_kernel, layers, steps), in_specs=...]
where the time goes in v7:
time: 514 us
  Pallas kernels  513 us (100%)
    pallas_call x1, Pallas kernels, run_backward(): pl.pallas_call(functools.partial(backward_kernel, layers, block, hidden_h...  300 us
    pallas_call x1, Pallas kernels, run_forward(): pl.pallas_call(functools.partial(forward_kernel, layers, block, hidden_ha...  184 us
    pallas_call x1, Pallas kernels, run_finish(): pl.pallas_call(functools.partial(finish_kernel, layers, steps), in_specs=...  28.3 us

profile of v7, /device:TPU:0, one launch (start us, length us, event | category | flops | bytes accessed | tf_op | source)
XLA Modules:
  0.0 513.6 jit_solution(16694182710170453587)
XLA Ops:
  0.6 184.0 %forward.1 = (bf16[512,1024]{1,0:T(8,128)(2,1)}, bf16[512,1024]{1,0:T(8,128)(2,1)}, s32[1,768]{1,0:T(1,128)}, bf16[2,3,1024,512]{3,2,1,0:T(8,128)(2,1)}, bf16[2,...) custom-call(bf16[512,1024]{1,0:T(8,128)(2,1)} %refs_0_.1, ...), custom_call_target="tpu_custom_call" | custom-call | tf_op jit(solution)/shard_map/forward/pallas_call | solution.py:966
  184.7 300.5 %backward.1 = (bf16[512,1024]{1,0:T(8,128)(2,1)}, bf16[512,1024]{1,0:T(8,128)(2,1)}, bf16[2,2048,1024]{2,1,0:T(8,128)(2,1)}, bf16[2,1024,2048]{2,1,0:T(8,128)(2,...) custom-call(bf16[512,1024]{1,0:T(8,128)(2,1)} %get-tuple-element.46.refs_0_, ...), custom_call_target="tpu_custom_call" | custom-call | tf_op jit(solution)/shard_map/backward/pallas_call | solution.py:1935
  485.2 28.3 %finish.1 = (f32[2,2048,1024]{2,1,0:T(8,128)}, f32[2,1024,2048]{2,1,0:T(8,128)}, f32[2,512,1024]{2,1,0:T(8,128)}, f32[2,3,1024,512]{3,2,1,0:T(8,128)}, f32[2,2,5...) custom-call(bf16[2,2048,1024]{2,1,0:T(8,128)(2,1)} %get-tuple-elemen, ...), custom_call_target="tpu_custom_call" | custom-call | tf_op jit(solution)/shard_map/finish/pallas_call | solution.py:2103

commit v8 on v7

--- a/solution.py
+++ b/solution.py
@@ -384,8 +384,10 @@
 
 
 UNITS_LAYER = 12
-BEATS_EVERY_TICK = 18
-Y_AHEAD = 2
+Y_AHEAD = 6
+HOP_BEATS = (1, 3, 5, 6)
+IDLE_STEPS = 3
+LOADS_AHEAD = 2
 
 
 def fill_band_bias(segk_ref, bias_ref):
@@ -460,6 +462,10 @@
         out_weight,
         up_weight,
         down_weight,
+        qkv_arrived,
+        out_arrived,
+        up_arrived,
+        down_arrived,
         bias_buf,
         start_send,
         start_recv,
@@ -471,6 +477,7 @@
         load_sem,
         store_sem,
         pair_store_sem,
+        unit_store_sem,
     ) = refs
     width = 2 * block
     rows_all = tokens_buf.shape[0]
@@ -539,21 +546,21 @@
 
         @pl.when(inside < 3)
         def _():
-            action(qkv_own.at[layer, inside], qkv_other.at[layer, inside])
+            action(*[ref.at[layer, inside] for ref in (qkv_own, qkv_arrived, qkv_other)])
 
         @pl.when(inside == 3)
         def _():
-            action(out_own.at[layer], out_other.at[layer])
+            action(*[ref.at[layer] for ref in (out_own, out_arrived, out_other)])
+
+        cut = aligned((inside - 4) // 2, block)
 
         @pl.when((inside >= 4) & (inside % 2 == 0))
         def _():
-            cut = aligned((inside - 4) // 2, block)
-            action(up_own.at[layer, :, cut], up_other.at[layer, :, cut])
+            action(*[ref.at[layer, :, cut] for ref in (up_own, up_arrived, up_other)])
 
         @pl.when((inside >= 4) & (inside % 2 == 1))
         def _():
-            cut = aligned((inside - 4) // 2, block)
-            action(down_own.at[layer, cut, :], down_other.at[layer, cut, :])
+            action(*[ref.at[layer, cut, :] for ref in (down_own, down_arrived, down_other)])
 
     def hop_copy(hop, unit, source, target):
         partner = (y_partner, x_partner, z_partner, core_partner)[hop]
@@ -585,10 +592,10 @@
                 action(False)
 
     def hop_start(hop, unit):
-        def go(own, other):
+        def go(own, arrived, _):
             def one(short):
-                source = piece_of(own if hop == 0 else other, hop, short)
-                hop_copy(hop, unit, source, piece_of(other, hop, short)).start()
+                source = piece_of(own if hop == 0 else arrived, hop, short)
+                hop_copy(hop, unit, source, piece_of(arrived, hop, short)).start()
 
             by_length(unit, hop, one)
 
@@ -596,7 +603,7 @@
 
     def hop_wait(hop, unit):
         def one(short):
-            piece = piece_of(down_other.at[0, pl.ds(0, block), :], hop, short)
+            piece = piece_of(down_arrived.at[0, pl.ds(0, block), :], hop, short)
             hop_copy(hop, unit, piece, piece).wait()
 
         by_length(unit, hop, one)
@@ -619,13 +626,19 @@
             hop_wait(2, unit)
             hop_start(3, unit)
 
+        def after_all(unit):
+            hop_wait(3, unit)
+
+            def keep(_, arrived, other):
+                pltpu.make_async_copy(arrived, other, unit_store_sem.at[unit]).start()
+
+            for_unit(unit, keep)
+
         when_unit(b + Y_AHEAD, lambda unit: hop_start(0, unit))
-        when_unit(b - 1, after_y)
-        when_unit(b - 2, after_x)
-        when_unit(b - 3, after_z)
-        when_unit(b - 4, lambda unit: hop_wait(3, unit))
-
-    other_step = 3 + pairs_half
+        for lag, action in zip(HOP_BEATS, (after_y, after_x, after_z, after_all)):
+            when_unit(b - lag, action)
+
+    other_step = 2 + pairs_half + IDLE_STEPS
     out_step = other_step + 1 + pairs_half
     norm_two_step = out_step + 1
     ffn_step = norm_two_step + 1
@@ -634,14 +647,14 @@
     jobs = layers * period
 
     def loads(kind, slot, *sources):
-        targets = {
-            "qkv": (qkv_weight,),
-            "out": (out_weight.at[0], out_weight.at[1]),
-            "ffn": (up_weight.at[slot], down_weight.at[slot]),
+        place, targets = {
+            "qkv": (blocks_hidden, (qkv_weight,)),
+            "out": (blocks_hidden + 1, (out_weight,)),
+            "ffn": (slot, (up_weight.at[slot], down_weight.at[slot])),
         }[kind]
         sources = sources or targets
         return [
-            pltpu.make_async_copy(source, target, load_sem.at[slot, index])
+            pltpu.make_async_copy(source, target, load_sem.at[place, index])
             for index, (source, target) in enumerate(zip(sources, targets))
         ]
 
@@ -654,25 +667,23 @@
             copy.wait()
 
     def prefetch(t):
-        slot = t % 2
         layer, step = t // period, t % period
-        for at, source in ((1, qkv_own), (other_step, qkv_other)):
-
-            @pl.when(step == at)
-            def _(source=source):
-                start_all(loads("qkv", slot, source.at[layer]))
+
+        @pl.when(step == 1)
+        def _():
+            start_all(loads("qkv", 0, qkv_own.at[layer]))
 
         @pl.when(step == out_step)
         def _():
-            start_all(loads("out", slot, out_own.at[layer], out_other.at[layer]))
-
-        for which, (up_ref, down_ref) in enumerate(((up_own, down_own), (up_other, down_other))):
-            begin = ffn_step + which * blocks_hidden
-
-            @pl.when((step >= begin) & (step < begin + blocks_hidden))
-            def _(begin=begin, up_ref=up_ref, down_ref=down_ref):
-                cut = aligned(step - begin, block)
-                start_all(loads("ffn", slot, up_ref.at[layer, :, cut], down_ref.at[layer, cut, :]))
+            start_all(loads("out", 0, out_own.at[layer]))
+
+        @pl.when((step >= ffn_step) & (step < ffn_step + blocks_hidden))
+        def _():
+            inside = step - ffn_step
+            cut = aligned(inside, block)
+            start_all(
+                loads("ffn", inside, up_own.at[layer, :, cut], down_own.at[layer, cut, :])
+            )
 
     tiles = [slice(r, r + BAND) for r in range(0, rows_all, BAND)]
     fine_tiles = [slice(r, r + LANES) for r in range(0, rows_all, LANES)]
@@ -738,12 +749,14 @@
         normalize(layer, 0, normed)
         start_all(first_stores(layer))
 
-    def qkv_job(layer, which, slot):
-        wait_all(loads("qkv", slot))
+    def qkv_job(layer, which):
+        if not which:
+            wait_all(loads("qkv", 0))
         bias = qv_bias_in if which else qv_bias_ref
         for third in range(3):
             for tile in tiles:
-                product = dot_low(normed[tile, :], qkv_weight[third])
+                weight = qkv_arrived[layer, third] if which else qkv_weight[third]
+                product = dot_low(normed[tile, :], weight)
                 if third != 1:
                     product = product + bias[layer, pl.ds(third // 2, 1), :]
                 proj[which, third, tile, :] = product.astype(low)
@@ -793,16 +806,16 @@
         def _():
             start_all(attended_stores(layer, which))
 
-    def out_job(layer, slot):
-        wait_all(loads("out", slot))
+    def out_job(layer):
+        wait_all(loads("out", 0))
         wait_all(first_stores(layer))
         for which in range(2):
             wait_all(proj_stores(layer, which))
             halo_store(layer, which).wait()
         bias = out_bias_ref[layer, pl.ds(0, 1), :]
         for tile in tiles:
-            branch = dot_low(attended[0, tile, :], out_weight[0])
-            branch = branch + dot_low(attended[1, tile, :], out_weight[1])
+            branch = dot_low(attended[0, tile, :], out_weight[...])
+            branch = branch + dot_low(attended[1, tile, :], out_arrived[layer])
             resid[tile, :] = resid[tile, :] + branch + bias
 
     def second_job(layer):
@@ -811,15 +824,18 @@
 
     def ffn_job(layer, which, inside, slot):
         index = which * blocks_hidden + inside
-        wait_all(loads("ffn", slot))
+        if not which:
+            wait_all(loads("ffn", inside))
 
         @pl.when(index >= 2)
         def _():
             wait_all(ffn_stores(layer, index - 2, slot))
 
         bias = (up_bias_in if which else up_bias_ref)[pl.ds(layer, 1), aligned(inside, block)]
+        cut = aligned(inside, block)
         for tile in tiles:
-            before = dot_low(normed_two[tile, :], up_weight[slot]) + bias
+            up_block = up_arrived[layer, :, cut] if which else up_weight[inside]
+            before = dot_low(normed_two[tile, :], up_block) + bias
             square = before * before
             tangent = jnp.tanh(gelu_coeff * before * (1.0 + cubic_coeff * square))
             raised = 0.5 * (1.0 + tangent)
@@ -833,7 +849,8 @@
                 * gelu_coeff
                 * (1.0 + 3.0 * cubic_coeff * square)
             ).astype(low)
-            product = dot_low(activated, down_weight[slot])
+            down_block = down_arrived[layer, cut, :] if which else down_weight[inside]
+            product = dot_low(activated, down_block)
             if which:
                 collected[tile, :] = collected[tile, :] + product
                 continue
@@ -868,11 +885,11 @@
                 action(step - first)
 
         at(0, 1, lambda _: first_job(layer))
-        at(1, 1, lambda _: qkv_job(layer, 0, slot))
+        at(1, 1, lambda _: qkv_job(layer, 0))
         at(2, pairs_half, lambda pair: attention_job(layer, 0, pair))
-        at(other_step, 1, lambda _: qkv_job(layer, 1, slot))
+        at(other_step, 1, lambda _: qkv_job(layer, 1))
         at(other_step + 1, pairs_half, lambda pair: attention_job(layer, 1, pair))
-        at(out_step, 1, lambda _: out_job(layer, slot))
+        at(out_step, 1, lambda _: out_job(layer))
         at(norm_two_step, 1, lambda _: second_job(layer))
         at(ffn_step, blocks_hidden, lambda inside: ffn_job(layer, 0, inside, slot))
         at(ffn_step + blocks_hidden, blocks_hidden, lambda inside: ffn_job(layer, 1, inside, slot))
@@ -903,18 +920,21 @@
     swap_wait(0, tokens_ref, tokens_buf)
     for tile in tiles:
         resid[tile, :] = tokens_buf[tile, :].astype(jnp.float32)
-    cot_tick = BEATS_EVERY_TICK + 6
+    cot_tick = period + other_step + 4
+
+    def past(t, begin):
+        return (t - begin) * (t > begin).astype(jnp.int32)
+
+    def beat_at(t):
+        return (10 * t - 4 * past(t, 10) - past(t, 22)) // 10
+
+    for ahead in range(LOADS_AHEAD):
+        prefetch(jnp.int32(ahead))
 
     def tick(t, carry):
-        @pl.when(t <= BEATS_EVERY_TICK)
-        def _():
-            beat(t)
-
-        late = t - BEATS_EVERY_TICK
-
-        @pl.when((late > 0) & (late % 2 == 0))
-        def _():
-            beat(BEATS_EVERY_TICK + late // 2)
+        @pl.when((t == 0) | (beat_at(t) != beat_at(t - 1)))
+        def _():
+            beat(beat_at(t))
 
         @pl.when(t == cot_tick)
         def _():
@@ -925,9 +945,9 @@
             pltpu.make_async_copy(cot_ref, tokens_buf, swap_sem.at[1]).wait()
             pltpu.make_async_copy(tokens_buf, cot_out, swap_sem.at[1]).start()
 
-        @pl.when(t + 1 < jobs)
-        def _():
-            prefetch(t + 1)
+        @pl.when(t + LOADS_AHEAD < jobs)
+        def _():
+            prefetch(t + LOADS_AHEAD)
 
         job(t)
         return carry
@@ -939,6 +959,9 @@
     last_store.start()
     last_store.wait()
     swap_wait(1, cot_ref, cot_out)
+    for unit in range(units):
+        block_ref = down_arrived.at[0, pl.ds(0, block), :]
+        pltpu.make_async_copy(block_ref, block_ref, unit_store_sem.at[unit]).wait()
 
 
 def run_forward(tokens, cotangent, segments, weights, biases, out_bias, gain, shift, block):
@@ -990,9 +1013,12 @@
             vmem((2, rows, block), low),
             vmem((2, rows, block), low),
             vmem((3, width, block), low),
-            vmem((2, block, width), low),
-            vmem((2, width, block), low),
-            vmem((2, block, width), low),
+            vmem((block, width), low),
+            vmem((hidden_half // block, width, block), low),
+            vmem((hidden_half // block, block, width), low),
+        ]
+        + [vmem(member.shape, low) for member in weights]
+        + [
             vmem((rows // BAND, BAND, 2 * BAND), wide),
             pltpu.SemaphoreType.DMA((5,)),
             pltpu.SemaphoreType.DMA((5,)),
@@ -1001,9 +1027,10 @@
             pltpu.SemaphoreType.DMA((4, units)),
             pltpu.SemaphoreType.DMA((layers, 2)),
             pltpu.SemaphoreType.DMA((layers, 2)),
-            pltpu.SemaphoreType.DMA((2, 2)),
+            pltpu.SemaphoreType.DMA((hidden_half // block + 2, 2)),
             pltpu.SemaphoreType.DMA((16,)),
             pltpu.SemaphoreType.DMA((2, 2)),
+            pltpu.SemaphoreType.DMA((units,)),
         ],
         compiler_params=pltpu.CompilerParams(
             collective_id=1, has_side_effects=True, vmem_limit_bytes=VMEM_ASKED

time: 514 us -> 484 us (0.942)
  Pallas kernels: 513 us -> 483 us
    pallas_call x1, Pallas kernels: 184 us -> 155 us  [run_forward(): pl.pallas_call(functools.partial(forward_kernel, layers, block, hidden_ha...]
where the time goes in v8:
time: 484 us
  Pallas kernels  483 us (100%)
    pallas_call x1, Pallas kernels, run_backward(): pl.pallas_call(functools.partial(backward_kernel, layers, block, hidden_h...  300 us
    pallas_call x1, Pallas kernels, run_forward(): pl.pallas_call(functools.partial(forward_kernel, layers, block, hidden_ha...  155 us
    pallas_call x1, Pallas kernels, run_finish(): pl.pallas_call(functools.partial(finish_kernel, layers, steps), in_specs=...  28.3 us

profile of v8, /device:TPU:0, one launch (start us, length us, event | category | flops | bytes accessed | tf_op | source)
XLA Modules:
  0.0 484.1 jit_solution(15393807037855711078)
XLA Ops:
  0.6 155.4 %forward.1 = (bf16[512,1024]{1,0:T(8,128)(2,1)}, bf16[512,1024]{1,0:T(8,128)(2,1)}, s32[1,768]{1,0:T(1,128)}, bf16[2,3,1024,512]{3,2,1,0:T(8,128)(2,1)}, bf16[2,...) custom-call(bf16[512,1024]{1,0:T(8,128)(2,1)} %refs_0_.1, ...), custom_call_target="tpu_custom_call" | custom-call | tf_op jit(solution)/shard_map/forward/pallas_call | solution.py:989
  156.1 299.5 %backward.1 = (bf16[512,1024]{1,0:T(8,128)(2,1)}, bf16[512,1024]{1,0:T(8,128)(2,1)}, bf16[2,2048,1024]{2,1,0:T(8,128)(2,1)}, bf16[2,1024,2048]{2,1,0:T(8,128)(2,...) custom-call(bf16[512,1024]{1,0:T(8,128)(2,1)} %get-tuple-element.46.refs_0_, ...), custom_call_target="tpu_custom_call" | custom-call | tf_op jit(solution)/shard_map/backward/pallas_call | solution.py:1962
  455.6 28.3 %finish.1 = (f32[2,2048,1024]{2,1,0:T(8,128)}, f32[2,1024,2048]{2,1,0:T(8,128)}, f32[2,512,1024]{2,1,0:T(8,128)}, f32[2,3,1024,512]{3,2,1,0:T(8,128)}, f32[2,2,5...) custom-call(bf16[2,2048,1024]{2,1,0:T(8,128)(2,1)} %get-tuple-elemen, ...), custom_call_target="tpu_custom_call" | custom-call | tf_op jit(solution)/shard_map/finish/pallas_call | solution.py:2130

commit v9 on v8

--- a/solution.py
+++ b/solution.py
@@ -384,9 +384,9 @@
 
 
 UNITS_LAYER = 12
-Y_AHEAD = 6
+Y_AHEAD = 4
 HOP_BEATS = (1, 3, 5, 6)
-IDLE_STEPS = 3
+IDLE_STEPS = 2
 LOADS_AHEAD = 2
 
 
@@ -581,13 +581,15 @@
             action(False)
             return
 
-        @pl.when(unit % 3 != 0)
+        whole = (unit % 3 == 0) & (unit > 0)
+
+        @pl.when(jnp.logical_not(whole))
         def _():
             action(True)
 
         if hop < 2:
 
-            @pl.when(unit % 3 == 0)
+            @pl.when(whole)
             def _():
                 action(False)
 
@@ -753,40 +755,47 @@
         if not which:
             wait_all(loads("qkv", 0))
         bias = qv_bias_in if which else qv_bias_ref
-        for third in range(3):
+        for third in (1, 2, 0):
             for tile in tiles:
                 weight = qkv_arrived[layer, third] if which else qkv_weight[third]
                 product = dot_low(normed[tile, :], weight)
                 if third != 1:
                     product = product + bias[layer, pl.ds(third // 2, 1), :]
                 proj[which, third, tile, :] = product.astype(low)
-
-        @pl.when(core == 0)
-        def _():
-            halo_copy(layer, which).start()
+            if third == 2:
+
+                @pl.when(core == 0)
+                def _():
+                    halo_copy(layer, which).start()
 
         start_all(proj_stores(layer, which))
 
     def attention_job(layer, which, pair):
         @pl.when(pair == 0)
         def _():
-            @pl.when(core == 0)
-            def _():
-                halo_copy(layer, which).wait_send()
-
-            @pl.when(core == 1)
-            def _():
-                halo_copy(layer, which).wait_recv()
-
-            halo_store(layer, which).start()
             totals[which] = jnp.zeros_like(totals[which])
 
         lane = lax.broadcasted_iota(jnp.int32, (BAND, LANES), 1)
         here = aligned(pair, LANES)
-        for index, tile in enumerate(tiles):
+        for index, tile in reversed(list(enumerate(tiles))):
+            if index == 0:
+
+                @pl.when(pair == 0)
+                def _():
+                    @pl.when(core == 0)
+                    def _():
+                        halo_copy(layer, which).wait_send()
+
+                    @pl.when(core == 1)
+                    def _():
+                        halo_copy(layer, which).wait_recv()
+
+                    halo_store(layer, which).start()
+
             query = proj[which, 0, tile, here]
-            keys = band_rows(halo[layer, which, 0, :, here], proj[which, 1, :, here], index)
-            values = band_rows(halo[layer, which, 1, :, here], proj[which, 2, :, here], index)
+            first = [halo[layer, which, part, :, here] if index == 0 else None for part in range(2)]
+            keys = band_rows(first[0], proj[which, 1, :, here], index)
+            values = band_rows(first[1], proj[which, 2, :, here], index)
             parts = []
             kept = totals[which, tile, :]
             for head in range(2):
@@ -885,10 +894,13 @@
                 action(step - first)
 
         at(0, 1, lambda _: first_job(layer))
+        later = (layer > 0).astype(jnp.int32)
+        other_at = other_step + later * (2 - other_step)
+        other_first = other_step + 1 + later * (2 + pairs_half - other_step)
         at(1, 1, lambda _: qkv_job(layer, 0))
-        at(2, pairs_half, lambda pair: attention_job(layer, 0, pair))
-        at(other_step, 1, lambda _: qkv_job(layer, 1))
-        at(other_step + 1, pairs_half, lambda pair: attention_job(layer, 1, pair))
+        at(2 + later, pairs_half, lambda pair: attention_job(layer, 0, pair))
+        at(other_at, 1, lambda _: qkv_job(layer, 1))
+        at(other_first, pairs_half, lambda pair: attention_job(layer, 1, pair))
         at(out_step, 1, lambda _: out_job(layer))
         at(norm_two_step, 1, lambda _: second_job(layer))
         at(ffn_step, blocks_hidden, lambda inside: ffn_job(layer, 0, inside, slot))
@@ -926,7 +938,7 @@
         return (t - begin) * (t > begin).astype(jnp.int32)
 
     def beat_at(t):
-        return (10 * t - 4 * past(t, 10) - past(t, 22)) // 10
+        return (10 * t - 4 * past(t, 12) - past(t, 22)) // 10
 
     for ahead in range(LOADS_AHEAD):
         prefetch(jnp.int32(ahead))

time: 484 us -> 477 us (0.986)
  Pallas kernels: 483 us -> 476 us
    pallas_call x1, Pallas kernels: 155 us -> 149 us  [run_forward(): pl.pallas_call(functools.partial(forward_kernel, layers, block, hidden_ha...]
where the time goes in v9:
time: 477 us
  Pallas kernels  476 us (100%)
    pallas_call x1, Pallas kernels, run_backward(): pl.pallas_call(functools.partial(backward_kernel, layers, block, hidden_h...  298 us
    pallas_call x1, Pallas kernels, run_forward(): pl.pallas_call(functools.partial(forward_kernel, layers, block, hidden_ha...  149 us
    pallas_call x1, Pallas kernels, run_finish(): pl.pallas_call(functools.partial(finish_kernel, layers, steps), in_specs=...  28.3 us

profile of v9, /device:TPU:0, one launch (start us, length us, event | category | flops | bytes accessed | tf_op | source)
XLA Modules:
  0.0 476.7 jit_solution(9641308720095243777)
XLA Ops:
  0.6 149.3 %forward.1 = (bf16[512,1024]{1,0:T(8,128)(2,1)}, bf16[512,1024]{1,0:T(8,128)(2,1)}, s32[1,768]{1,0:T(1,128)}, bf16[2,3,1024,512]{3,2,1,0:T(8,128)(2,1)}, bf16[2,...) custom-call(bf16[512,1024]{1,0:T(8,128)(2,1)} %refs_0_.1, ...), custom_call_target="tpu_custom_call" | custom-call | tf_op jit(solution)/shard_map/forward/pallas_call | solution.py:1001
  150.0 298.3 %backward.1 = (bf16[512,1024]{1,0:T(8,128)(2,1)}, bf16[512,1024]{1,0:T(8,128)(2,1)}, bf16[2,2048,1024]{2,1,0:T(8,128)(2,1)}, bf16[2,1024,2048]{2,1,0:T(8,128)(2,...) custom-call(bf16[512,1024]{1,0:T(8,128)(2,1)} %get-tuple-element.46.refs_0_, ...), custom_call_target="tpu_custom_call" | custom-call | tf_op jit(solution)/shard_map/backward/pallas_call | solution.py:1974
  448.3 28.3 %finish.1 = (f32[2,2048,1024]{2,1,0:T(8,128)}, f32[2,1024,2048]{2,1,0:T(8,128)}, f32[2,512,1024]{2,1,0:T(8,128)}, f32[2,3,1024,512]{3,2,1,0:T(8,128)}, f32[2,2,5...) custom-call(bf16[2,2048,1024]{2,1,0:T(8,128)(2,1)} %get-tuple-elemen, ...), custom_call_target="tpu_custom_call" | custom-call | tf_op jit(solution)/shard_map/finish/pallas_call | solution.py:2142

commit v10 on v9

--- a/solution.py
+++ b/solution.py
@@ -1259,7 +1259,12 @@
         )
 
     def x_first(chunk):
-        return ((5 * chunk) % 8 < 3) | (chunk >= chunks - 1)
+        left = chunks - 1 - chunk
+        near = (chunk <= 10) & (chunk % 2 == 0) | (left <= 10) & (left % 2 == 0)
+        far = (chunk > 10) & (left > 10)
+        third = far & (chunk % 3 == 1) & ((chunk < 18) | (left < 19))
+        fourth = far & (chunk % 4 == 0) & (chunk >= 18) & (left >= 19)
+        return near | third | fourth
 
     def core_copy(chunk):
         return remote(
@@ -1910,15 +1915,17 @@
     first_load = pltpu.make_async_copy(cot_ref, grad_branch, io_sem.at[0])
     first_load.start()
     prefetch(0)
-    fill_band_bias(segk_ref, bias_buf)
     first_load.wait()
-    for tile in tiles:
-        grad_res[tile, :] = grad_branch[tile, :].astype(jnp.float32)
     stage_operands(0)
-    swap_start(0, out_act_ref, out_act_out)
     vector_ticks = [jobs + VECTOR_STEP * step for step in range(7)]
 
     def tick(t, carry):
+        @pl.when(t == 1)
+        def _():
+            fill_band_bias(segk_ref, bias_buf)
+            for tile in tiles:
+                grad_res[tile, :] = grad_branch[tile, :].astype(jnp.float32)
+
         @pl.when(t + 1 < jobs)
         def _():
             prefetch(t + 1)
@@ -1945,6 +1952,7 @@
 
         @pl.when(t == chunks + FIRST + LAGS["second"] - 1)
         def _():
+            swap_start(0, out_act_ref, out_act_out)
             swap_start(1, grad_branch, grad_in_ref)
 
         for step, when in enumerate(vector_ticks):

time: 477 us -> 471 us (0.987)
  Pallas kernels: 476 us -> 470 us
    pallas_call x1, Pallas kernels: 298 us -> 292 us  [run_backward(): pl.pallas_call(functools.partial(backward_kernel, layers, block, hidden_h...]
where the time goes in v10:
time: 471 us
  Pallas kernels  470 us (100%)
    pallas_call x1, Pallas kernels, run_backward(): pl.pallas_call(functools.partial(backward_kernel, layers, block, hidden_h...  292 us
    pallas_call x1, Pallas kernels, run_forward(): pl.pallas_call(functools.partial(forward_kernel, layers, block, hidden_ha...  149 us
    pallas_call x1, Pallas kernels, run_finish(): pl.pallas_call(functools.partial(finish_kernel, layers, steps), in_specs=...  28.3 us

profile of v10, /device:TPU:0, one launch (start us, length us, event | category | flops | bytes accessed | tf_op | source)
XLA Modules:
  0.0 470.8 jit_solution(1652824325087724196)
XLA Ops:
  0.6 149.3 %forward.1 = (bf16[512,1024]{1,0:T(8,128)(2,1)}, bf16[512,1024]{1,0:T(8,128)(2,1)}, s32[1,768]{1,0:T(1,128)}, bf16[2,3,1024,512]{3,2,1,0:T(8,128)(2,1)}, bf16[2,...) custom-call(bf16[512,1024]{1,0:T(8,128)(2,1)} %refs_0_.1, ...), custom_call_target="tpu_custom_call" | custom-call | tf_op jit(solution)/shard_map/forward/pallas_call | solution.py:1001
  150.0 292.4 %backward.1 = (bf16[512,1024]{1,0:T(8,128)(2,1)}, bf16[512,1024]{1,0:T(8,128)(2,1)}, bf16[2,2048,1024]{2,1,0:T(8,128)(2,1)}, bf16[2,1024,2048]{2,1,0:T(8,128)(2,...) custom-call(bf16[512,1024]{1,0:T(8,128)(2,1)} %get-tuple-element.46.refs_0_, ...), custom_call_target="tpu_custom_call" | custom-call | tf_op jit(solution)/shard_map/backward/pallas_call | solution.py:1982
  442.4 28.3 %finish.1 = (f32[2,2048,1024]{2,1,0:T(8,128)}, f32[2,1024,2048]{2,1,0:T(8,128)}, f32[2,512,1024]{2,1,0:T(8,128)}, f32[2,3,1024,512]{3,2,1,0:T(8,128)}, f32[2,2,5...) custom-call(bf16[2,2048,1024]{2,1,0:T(8,128)(2,1)} %get-tuple-elemen, ...), custom_call_target="tpu_custom_call" | custom-call | tf_op jit(solution)/shard_map/finish/pallas_call | solution.py:2150

commit v11 on v10

--- a/solution.py
+++ b/solution.py
@@ -384,7 +384,7 @@
 
 
 UNITS_LAYER = 12
-Y_AHEAD = 4
+Y_AHEAD = 1
 HOP_BEATS = (1, 3, 5, 6)
 IDLE_STEPS = 2
 LOADS_AHEAD = 2
@@ -500,8 +500,6 @@
     barrier = pltpu.get_barrier_semaphore()
     for partner in (core_partner, x_partner, y_partner, z_partner, swap_partner):
         pl.semaphore_signal(barrier, inc=1, device_id=partner, device_id_type=MESH)
-    pl.semaphore_wait(barrier, 5)
-
     def remote(source, target, send, recv, partner):
         return pltpu.make_async_remote_copy(
             src_ref=source,
@@ -907,8 +905,9 @@
         at(ffn_step + blocks_hidden, blocks_hidden, lambda inside: ffn_job(layer, 1, inside, slot))
         at(end_step, 1, lambda _: end_job(layer, slot))
 
+    halo[...] = jnp.zeros_like(halo)
+    pl.semaphore_wait(barrier, 5)
     swap_start(0, tokens_ref, tokens_buf)
-    halo[...] = jnp.zeros_like(halo)
     segments_copy.start()
     qv_copy.start()
     up_copy.start()
@@ -1172,11 +1171,6 @@
     @pl.when(inner == 1)
     def _():
         pl.semaphore_signal(barrier, inc=1, device_id=middle_partner, device_id_type=MESH)
-        pl.semaphore_wait(barrier, 6)
-
-    @pl.when(inner == 0)
-    def _():
-        pl.semaphore_wait(barrier, 5)
 
     blocks_hidden = hidden_half // block
     plan = (
@@ -1917,6 +1911,14 @@
     prefetch(0)
     first_load.wait()
     stage_operands(0)
+
+    @pl.when(inner == 1)
+    def _():
+        pl.semaphore_wait(barrier, 6)
+
+    @pl.when(inner == 0)
+    def _():
+        pl.semaphore_wait(barrier, 5)
     vector_ticks = [jobs + VECTOR_STEP * step for step in range(7)]
 
     def tick(t, carry):

time: 471 us -> 465 us (0.987)
  Pallas kernels: 470 us -> 463 us
    pallas_call x1, Pallas kernels: 149 us -> 144 us  [run_forward(): pl.pallas_call(functools.partial(forward_kernel, layers, block, hidden_ha...]
where the time goes in v11:
time: 465 us; the launch traced here: 464 us
  Pallas kernels  463 us (100%)
    pallas_call x1, Pallas kernels, run_backward(): pl.pallas_call(functools.partial(backward_kernel, layers, block, hidden_h...  291 us
    pallas_call x1, Pallas kernels, run_forward(): pl.pallas_call(functools.partial(forward_kernel, layers, block, hidden_ha...  144 us
    pallas_call x1, Pallas kernels, run_finish(): pl.pallas_call(functools.partial(finish_kernel, layers, steps), in_specs=...  28.3 us

profile of v11, /device:TPU:0, one launch (start us, length us, event | category | flops | bytes accessed | tf_op | source)
XLA Modules:
  0.0 464.2 jit_solution(12691910332654384583)
XLA Ops:
  0.6 144.2 %forward.1 = (bf16[512,1024]{1,0:T(8,128)(2,1)}, bf16[512,1024]{1,0:T(8,128)(2,1)}, s32[1,768]{1,0:T(1,128)}, bf16[2,3,1024,512]{3,2,1,0:T(8,128)(2,1)}, bf16[2,...) custom-call(bf16[512,1024]{1,0:T(8,128)(2,1)} %refs_0_.1, ...), custom_call_target="tpu_custom_call" | custom-call | tf_op jit(solution)/shard_map/forward/pallas_call | solution.py:1000
  144.9 290.8 %backward.1 = (bf16[512,1024]{1,0:T(8,128)(2,1)}, bf16[512,1024]{1,0:T(8,128)(2,1)}, bf16[2,2048,1024]{2,1,0:T(8,128)(2,1)}, bf16[2,1024,2048]{2,1,0:T(8,128)(2,...) custom-call(bf16[512,1024]{1,0:T(8,128)(2,1)} %get-tuple-element.46.refs_0_, ...), custom_call_target="tpu_custom_call" | custom-call | tf_op jit(solution)/shard_map/backward/pallas_call | solution.py:1984
  435.7 28.3 %finish.1 = (f32[2,2048,1024]{2,1,0:T(8,128)}, f32[2,1024,2048]{2,1,0:T(8,128)}, f32[2,512,1024]{2,1,0:T(8,128)}, f32[2,3,1024,512]{3,2,1,0:T(8,128)}, f32[2,2,5...) custom-call(bf16[2,2048,1024]{2,1,0:T(8,128)(2,1)} %get-tuple-elemen, ...), custom_call_target="tpu_custom_call" | custom-call | tf_op jit(solution)/shard_map/finish/pallas_call | solution.py:2152

commit v12 on v11

--- a/solution.py
+++ b/solution.py
@@ -905,6 +905,8 @@
         at(ffn_step + blocks_hidden, blocks_hidden, lambda inside: ffn_job(layer, 1, inside, slot))
         at(end_step, 1, lambda _: end_job(layer, slot))
 
+    for ahead in range(LOADS_AHEAD):
+        prefetch(jnp.int32(ahead))
     halo[...] = jnp.zeros_like(halo)
     pl.semaphore_wait(barrier, 5)
     swap_start(0, tokens_ref, tokens_buf)
@@ -938,9 +940,6 @@
 
     def beat_at(t):
         return (10 * t - 4 * past(t, 12) - past(t, 22)) // 10
-
-    for ahead in range(LOADS_AHEAD):
-        prefetch(jnp.int32(ahead))
 
     def tick(t, carry):
         @pl.when((t == 0) | (beat_at(t) != beat_at(t - 1)))
@@ -1908,9 +1907,9 @@
 
     first_load = pltpu.make_async_copy(cot_ref, grad_branch, io_sem.at[0])
     first_load.start()
-    prefetch(0)
     first_load.wait()
     stage_operands(0)
+    prefetch(0)
 
     @pl.when(inner == 1)
     def _():

time: 465 us -> 464 us (level)
  no operation moved by 1% of the time
where the time goes in v12:
time: 464 us
  Pallas kernels  463 us (100%)
    pallas_call x1, Pallas kernels, run_backward(): pl.pallas_call(functools.partial(backward_kernel, layers, block, hidden_h...  291 us
    pallas_call x1, Pallas kernels, run_forward(): pl.pallas_call(functools.partial(forward_kernel, layers, block, hidden_ha...  144 us
    pallas_call x1, Pallas kernels, run_finish(): pl.pallas_call(functools.partial(finish_kernel, layers, steps), in_specs=...  28.3 us

profile of v12, /device:TPU:0, one launch (start us, length us, event | category | flops | bytes accessed | tf_op | source)
XLA Modules:
  0.0 463.5 jit_solution(2669955809528233924)
XLA Ops:
  0.6 143.8 %forward.1 = (bf16[512,1024]{1,0:T(8,128)(2,1)}, bf16[512,1024]{1,0:T(8,128)(2,1)}, s32[1,768]{1,0:T(1,128)}, bf16[2,3,1024,512]{3,2,1,0:T(8,128)(2,1)}, bf16[2,...) custom-call(bf16[512,1024]{1,0:T(8,128)(2,1)} %refs_0_.1, ...), custom_call_target="tpu_custom_call" | custom-call | tf_op jit(solution)/shard_map/forward/pallas_call | solution.py:999
  144.5 290.6 %backward.1 = (bf16[512,1024]{1,0:T(8,128)(2,1)}, bf16[512,1024]{1,0:T(8,128)(2,1)}, bf16[2,2048,1024]{2,1,0:T(8,128)(2,1)}, bf16[2,1024,2048]{2,1,0:T(8,128)(2,...) custom-call(bf16[512,1024]{1,0:T(8,128)(2,1)} %get-tuple-element.46.refs_0_, ...), custom_call_target="tpu_custom_call" | custom-call | tf_op jit(solution)/shard_map/backward/pallas_call | solution.py:1983
  435.1 28.3 %finish.1 = (f32[2,2048,1024]{2,1,0:T(8,128)}, f32[2,1024,2048]{2,1,0:T(8,128)}, f32[2,512,1024]{2,1,0:T(8,128)}, f32[2,3,1024,512]{3,2,1,0:T(8,128)}, f32[2,2,5...) custom-call(bf16[2,2048,1024]{2,1,0:T(8,128)(2,1)} %get-tuple-elemen, ...), custom_call_target="tpu_custom_call" | custom-call | tf_op jit(solution)/shard_map/finish/pallas_call | solution.py:2151
